TPU v7x, 32 devices: a whole 2x2x4 slice. The times are simulated.
32 devices in a mesh: wide: 16 (over z, y, core), narrow: 2 (over x).
Axes of the slice: x: 2, y: 2, z: 4, core: 2. Of those that a mesh axis runs over, the one named last changes fastest.
Arguments:
- hidden_in: bfloat16 [8192, 768], P('wide'), may hold values from -6 to 6
- gainfirst: float32 [768], replicated, may hold values from 0.5 to 1.5
- shiftfirst: float32 [768], replicated, may hold values from -2 to 2
- valueright: bfloat16 [192, 768], replicated, may hold values from -0.4375 to 0.4375
- valueleft: bfloat16 [192, 768], replicated, may hold values from -0.4375 to 0.4375
- shaperight: bfloat16 [192, 768], replicated, may hold values from -0.4375 to 0.4375
- shapeleft: bfloat16 [192, 768], replicated, may hold values from -0.4375 to 0.4375
- convtaps: float32 [3, 768], replicated, may hold values from -3 to 3
- posweight: float32 [5, 128], replicated, may hold values from -14 to 14
- posbias: float32 [128], replicated, may hold values from -3 to 3
- sinefreq: float32 [128], replicated, may hold values from 1.5 to 2
- midweight: float32 [128, 128], replicated, may hold values from -2.2 to 2.2
- midbias: float32 [128], replicated, may hold values from -3 to 3
- filterout: float32 [128, 768], replicated, may hold values from -0.5 to 0.5
- outright: bfloat16 [192, 768], replicated, may hold values from -0.4375 to 0.4375
- outleft: bfloat16 [192, 768], replicated, may hold values from -0.4375 to 0.4375
- gainsecond: float32 [768], replicated, may hold values from 0.5 to 1.5
- shiftsecond: float32 [768], replicated, may hold values from -2 to 2
- gateright: bfloat16 [192, 768], P(None, 'narrow'), may hold values from -0.4375 to 0.4375
- gateleft: bfloat16 [192, 3072], P(None, 'narrow'), may hold values from -0.4375 to 0.4375
- liftright: bfloat16 [192, 768], P(None, 'narrow'), may hold values from -0.4375 to 0.4375
- liftleft: bfloat16 [192, 3072], P(None, 'narrow'), may hold values from -0.4375 to 0.4375
- lowerright: bfloat16 [768, 768], P(None, 'narrow'), may hold values from -0.21875 to 0.21875
- lowerleft: bfloat16 [192, 768], P('narrow'), may hold values from -0.4375 to 0.4375
- grad_out: bfloat16 [8192, 768], P('wide', 'narrow'), may hold values from -6 to 6
Outputs:
- hidden_out: bfloat16 [8192, 768], P('wide', 'narrow')
- hidden_grad: bfloat16 [8192, 768], P('wide', 'narrow')
- grad_gainfirst: float32 [768], replicated
- grad_shiftfirst: float32 [768], replicated
- grad_valueright: float32 [192, 768], replicated
- grad_valueleft: float32 [192, 768], replicated
- grad_shaperight: float32 [192, 768], replicated
- grad_shapeleft: float32 [192, 768], replicated
- grad_convtaps: float32 [3, 768], replicated
- grad_posweight: float32 [5, 128], replicated
- grad_posbias: float32 [128], replicated
- grad_sinefreq: float32 [128], replicated
- grad_midweight: float32 [128, 128], replicated
- grad_midbias: float32 [128], replicated
- grad_filterout: float32 [128, 768], P(None, ('wide', 'narrow'))
- grad_outright: float32 [192, 768], replicated
- grad_outleft: float32 [192, 768], replicated
- grad_gainsecond: float32 [768], replicated
- grad_shiftsecond: float32 [768], replicated
- grad_gateright: float32 [192, 768], P(None, 'narrow')
- grad_gateleft: float32 [192, 3072], P(None, 'narrow')
- grad_liftright: float32 [192, 768], P(None, 'narrow')
- grad_liftleft: float32 [192, 3072], P(None, 'narrow')
- grad_lowerright: float32 [768, 768], P(None, 'narrow')
- grad_lowerleft: float32 [192, 768], P('narrow')
All inputs are finite; a program needn't handle non-finite values.
Results may differ from a plain program's by a relative error of at most 0.02.
Values may be sent and summed in bfloat16 or wider, within the bound.
A program may use at most 192 MiB of HBM per device.

v0:
```python
import math

import jax
import jax.numpy as jnp
import numpy as np
from jax import lax
from jax.experimental import pallas as pl
from jax.experimental.pallas import tpu as pltpu
from jax.sharding import PartitionSpec as P

D = 768
BLOCKS = 4
SEQS = 8


EPSILON = 1e-05
HIGHEST = lax.Precision.HIGHEST


def from_behind(x, axis, by):
    length = lax.axis_size(axis)
    pairs = [(i, i + by) for i in range(length) if 0 <= i + by < length]
    return lax.ppermute(x, axis, pairs)


def norm_forward(values, gain, shift):
    center = values - jnp.mean(values, axis=-1, keepdims=True)
    inverse = lax.rsqrt(jnp.mean(center * center, axis=-1, keepdims=True) + EPSILON)
    normed = center * inverse
    return (normed * gain + shift, normed, inverse)


def norm_backward(upstream, normed, inverse, gain):
    scaled = upstream * gain
    result = inverse * (
        scaled
        - jnp.mean(scaled, axis=-1, keepdims=True)
        - normed * jnp.mean(scaled * normed, axis=-1, keepdims=True)
    )
    return (result, jnp.sum(upstream * normed, axis=0), jnp.sum(upstream, axis=0))


def right_view(right, nblocks, groups, group_first):
    width_in = right.shape[0]
    piece = right.shape[1] // (nblocks * groups)
    if group_first:
        return (right.reshape(width_in, groups, nblocks, piece), "ikbc")
    return (right.reshape(width_in, nblocks, groups, piece), "ibkc")


def section_one(inputs, right, groups, group_first):
    rowcount = inputs.shape[0]
    width_in = right.shape[0]
    nblocks = inputs.shape[1] // width_in
    factor, letters = right_view(right, nblocks, groups, group_first)
    first = jnp.einsum(
        "tbi," + letters + "->tkbc",
        inputs.reshape(rowcount, nblocks, width_in),
        factor,
        preferred_element_type=jnp.float32,
    )
    return first.reshape(rowcount, groups, -1).astype(jnp.bfloat16)


def section_two(middle_part, left):
    groups = middle_part.shape[1]
    result = jnp.einsum(
        "tkj,jke->tke",
        middle_part,
        left.reshape(left.shape[0], groups, -1),
        preferred_element_type=jnp.float32,
    )
    return result.reshape(result.shape[0], -1)


def back_two(middle_part, left, upstream):
    groups = middle_part.shape[1]
    left_view = left.reshape(left.shape[0], groups, -1)
    grad_left = jnp.einsum(
        "tkj,tke->jke", middle_part, upstream, preferred_element_type=jnp.float32
    )
    grad_middle = jnp.einsum(
        "tke,jke->tkj", upstream, left_view, preferred_element_type=jnp.float32
    )
    return (grad_left.reshape(left.shape[0], -1), grad_middle.astype(jnp.bfloat16))


def back_one(inputs, right, grad_middle, group_first):
    rowcount = inputs.shape[0]
    width_in = right.shape[0]
    nblocks = inputs.shape[1] // width_in
    groups = grad_middle.shape[1]
    factor, letters = right_view(right, nblocks, groups, group_first)
    spread_back = grad_middle.reshape(rowcount, groups, nblocks, -1)
    blocked = inputs.reshape(rowcount, nblocks, width_in)
    grad_right = jnp.einsum(
        "tbi,tkbc->" + letters, blocked, spread_back, preferred_element_type=jnp.float32
    )
    grad_inputs = jnp.einsum(
        "tkbc," + letters + "->tbi", spread_back, factor, preferred_element_type=jnp.float32
    )
    return (grad_right.reshape(width_in, -1), grad_inputs.reshape(rowcount, -1))


def fourier_tables(length):
    span = length // 128
    slow_index = jnp.arange(span, dtype=jnp.int32)
    fast_index = jnp.arange(128, dtype=jnp.int32)
    small = (slow_index[:, None] * slow_index[None, :] % span).astype(jnp.float32) * (
        2.0 * math.pi / span
    )
    twist = (slow_index[:, None] * fast_index[None, :] % length).astype(jnp.float32) * (
        2.0 * math.pi / length
    )
    large = (fast_index[:, None] * fast_index[None, :] % 128).astype(jnp.float32) * (
        2.0 * math.pi / 128
    )
    return (
        jnp.cos(small),
        jnp.sin(small),
        jnp.cos(twist),
        jnp.sin(twist),
        jnp.cos(large),
        jnp.sin(large),
    )


def to_spectrum(signal, tables):
    cos_small, sin_small, cos_twist, sin_twist, cos_large, sin_large = tables
    span = cos_small.shape[0]
    padded = jnp.concatenate([signal, jnp.zeros_like(signal)], axis=-1)
    padded = padded.reshape(signal.shape[:-1] + (span, 128))
    first_re = jnp.einsum("...qp,qk->...kp", padded, cos_small, precision=HIGHEST)
    first_im = -jnp.einsum("...qp,qk->...kp", padded, sin_small, precision=HIGHEST)
    turned_re = first_re * cos_twist + first_im * sin_twist
    turned_im = first_im * cos_twist - first_re * sin_twist
    out_re = jnp.einsum("...kp,pj->...kj", turned_re, cos_large, precision=HIGHEST) + jnp.einsum(
        "...kp,pj->...kj", turned_im, sin_large, precision=HIGHEST
    )
    out_im = jnp.einsum("...kp,pj->...kj", turned_im, cos_large, precision=HIGHEST) - jnp.einsum(
        "...kp,pj->...kj", turned_re, sin_large, precision=HIGHEST
    )
    return (out_re, out_im)


def from_spectrum(real_part, imag_part, tables):
    cos_small, sin_small, cos_twist, sin_twist, cos_large, sin_large = tables
    span = cos_small.shape[0]
    back_re = jnp.einsum("...kj,pj->...kp", real_part, cos_large, precision=HIGHEST) - jnp.einsum(
        "...kj,pj->...kp", imag_part, sin_large, precision=HIGHEST
    )
    back_im = jnp.einsum("...kj,pj->...kp", imag_part, cos_large, precision=HIGHEST) + jnp.einsum(
        "...kj,pj->...kp", real_part, sin_large, precision=HIGHEST
    )
    turned_re = back_re * cos_twist - back_im * sin_twist
    turned_im = back_im * cos_twist + back_re * sin_twist
    signal = (
        jnp.einsum("...kp,qk->...qp", turned_re, cos_small, precision=HIGHEST)
        - jnp.einsum("...kp,qk->...qp", turned_im, sin_small, precision=HIGHEST)
    ) / (span * 128)
    signal = signal.reshape(signal.shape[:-2] + (span * 128,))
    return signal[..., : span * 64]


def position_features(length):
    places = jnp.arange(length, dtype=jnp.float32)
    angle = places * (2.0 * math.pi / length)
    return jnp.stack(
        [
            places / length,
            jnp.cos(angle),
            jnp.sin(angle),
            jnp.cos(2.0 * angle),
            jnp.sin(2.0 * angle),
        ],
        axis=1,
    )


def decay_factors(channel_ids, length):
    rank = (channel_ids * 5 % D).astype(jnp.float32) / D
    lowest = math.log(0.25 / length)
    highest = math.log(1.0 / 30.0)
    rate = jnp.exp(lowest + rank * (highest - lowest))
    places = jnp.arange(length, dtype=jnp.float32)
    return jnp.exp(-rate[:, None] * places[None, :]) * jnp.sqrt(2.0 * rate)[:, None]


def channel_order(data, nwide, nnarrow, rows_half):
    count = data.shape[0]
    return data.reshape(count, nnarrow, nwide, rows_half).transpose(0, 2, 1, 3).reshape(count, -1)


def row_order(data, nwide, nnarrow):
    total = data.shape[0]
    rows_half = data.shape[1]
    count = total // (nwide * nnarrow)
    return (
        data.reshape(nnarrow, nwide, count, rows_half)
        .transpose(1, 0, 2, 3)
        .reshape(total, rows_half)
        .T
    )


def body(
    hidden_in,
    gainfirst,
    shiftfirst,
    valueright,
    valueleft,
    shaperight,
    shapeleft,
    convtaps,
    posweight,
    posbias,
    sinefreq,
    midweight,
    midbias,
    filterout,
    outright,
    outleft,
    gainsecond,
    shiftsecond,
    gateright,
    gateleft,
    liftright,
    liftleft,
    lowerright,
    lowerleft,
    grad_out,
):
    rowcount = hidden_in.shape[0]
    local_groups = gateright.shape[1] // gateleft.shape[0]
    nwide = lax.axis_size("wide")
    nnarrow = lax.axis_size("narrow")
    narrow_index = lax.axis_index("narrow")
    rows_half = rowcount // nnarrow
    row_start = narrow_index * rows_half
    combined = lax.axis_index("wide") * nnarrow + narrow_index
    resid = lax.dynamic_slice_in_dim(hidden_in, row_start, rows_half, 0).astype(jnp.float32)
    normone, hat_one, inv_one = norm_forward(resid, gainfirst, shiftfirst)
    normone = normone.astype(jnp.bfloat16)
    mid_value = section_one(normone, valueright, BLOCKS, False)
    signal = section_two(mid_value, valueleft).astype(jnp.bfloat16)
    mid_shape = section_one(normone, shaperight, BLOCKS, False)
    shaping = section_two(mid_shape, shapeleft)
    group = nwide // SEQS * nnarrow
    place = combined % group
    before = from_behind(signal[-2:], ("wide", "narrow"), 1)
    before = jnp.where(place == 0, jnp.zeros_like(before), before)
    extended = jnp.concatenate([before, signal], axis=0).astype(jnp.float32)
    shortconv = (
        convtaps[0] * extended[2:] + convtaps[1] * extended[1:-1] + convtaps[2] * extended[:-2]
    ).astype(jnp.bfloat16)
    channels = lax.all_to_all(
        lax.all_to_all(shortconv.T, "wide", split_axis=0, concat_axis=1, tiled=True),
        "narrow",
        split_axis=0,
        concat_axis=1,
        tiled=True,
    )
    channels = channel_order(channels, nwide, nnarrow, rows_half)
    count = channels.shape[0]
    length = channels.shape[1] // SEQS
    feats = position_features(length)
    lin_one = jnp.dot(feats, posweight, precision=HIGHEST) + posbias
    act_one = jnp.sin(sinefreq * lin_one)
    lin_two = jnp.dot(act_one, midweight, precision=HIGHEST) + midbias
    act_two = jnp.sin(sinefreq * lin_two)
    own_cols = lax.dynamic_slice_in_dim(filterout, combined * count, count, 1)
    channel_ids = combined * count + jnp.arange(count, dtype=jnp.int32)
    modulation = decay_factors(channel_ids, length)
    taps = jnp.dot(act_two, own_cols, precision=HIGHEST).T * modulation
    tables = fourier_tables(2 * length)
    sig_re, sig_im = to_spectrum(channels.astype(jnp.float32).reshape(count, SEQS, length), tables)
    fil_re, fil_im = to_spectrum(taps.reshape(count, 1, length), tables)
    conv_chan = from_spectrum(
        sig_re * fil_re - sig_im * fil_im, sig_re * fil_im + sig_im * fil_re, tables
    )
    conv_chan = conv_chan.reshape(count, SEQS * length).astype(jnp.bfloat16)
    longconv = lax.all_to_all(
        lax.all_to_all(conv_chan, "wide", split_axis=1, concat_axis=0, tiled=True),
        "narrow",
        split_axis=1,
        concat_axis=0,
        tiled=True,
    )
    longconv = row_order(longconv, nwide, nnarrow)
    mixed = (shaping * longconv.astype(jnp.float32)).astype(jnp.bfloat16)
    mid_out = section_one(mixed, outright, BLOCKS, False)
    middle = resid + section_two(mid_out, outleft)
    normtwo, hat_two, inv_two = norm_forward(middle, gainsecond, shiftsecond)
    normtwo = normtwo.astype(jnp.bfloat16)
    norm_all = lax.all_gather(normtwo, "narrow", axis=0, tiled=True)
    mid_gate = section_one(norm_all, gateright, local_groups, True)
    pregate = section_two(mid_gate, gateleft)
    mid_lift = section_one(norm_all, liftright, local_groups, True)
    prelift = section_two(mid_lift, liftleft)
    cumulative = 0.5 * (1.0 + lax.erf(pregate * (1.0 / math.sqrt(2.0))))
    activated = pregate * cumulative
    hidden = (activated * prelift).astype(jnp.bfloat16)
    mid_lower = section_one(hidden, lowerright, BLOCKS, False)
    partial_sum = section_two(mid_lower, lowerleft)
    partial_sum = partial_sum + lax.dynamic_update_slice_in_dim(
        jnp.zeros_like(partial_sum), middle, row_start, 0
    )
    hidden_out = lax.psum_scatter(
        partial_sum.astype(jnp.bfloat16), "narrow", scatter_dimension=1, tiled=True
    )
    upstream = lax.all_gather(grad_out, "narrow", axis=1, tiled=True)
    grad_lowerleft, grad_mid_lower = back_two(
        mid_lower, lowerleft, upstream.reshape(rowcount, BLOCKS, -1)
    )
    grad_lowerright, grad_hidden = back_one(hidden, lowerright, grad_mid_lower, False)
    density = jnp.exp(-0.5 * pregate * pregate) * (1.0 / math.sqrt(2.0 * math.pi))
    grad_pregate = (grad_hidden * prelift * (cumulative + pregate * density)).astype(jnp.bfloat16)
    grad_prelift = (grad_hidden * activated).astype(jnp.bfloat16)
    grad_gateleft, grad_mid_gate = back_two(
        mid_gate, gateleft, grad_pregate.reshape(rowcount, local_groups, -1)
    )
    grad_gateright, into_gate = back_one(norm_all, gateright, grad_mid_gate, True)
    grad_liftleft, grad_mid_lift = back_two(
        mid_lift, liftleft, grad_prelift.reshape(rowcount, local_groups, -1)
    )
    grad_liftright, into_lift = back_one(norm_all, liftright, grad_mid_lift, True)
    ffn_local = (
        grad_gateright,
        grad_gateleft,
        grad_liftright,
        grad_liftleft,
        grad_lowerright,
        grad_lowerleft,
    )
    dnormtwo = lax.psum_scatter(
        (into_gate + into_lift).astype(jnp.bfloat16), "narrow", scatter_dimension=0, tiled=True
    ).astype(jnp.float32)
    back_two_norm, grad_gainsecond, grad_shiftsecond = norm_backward(
        dnormtwo, hat_two, inv_two, gainsecond
    )
    up_rows = lax.dynamic_slice_in_dim(upstream, row_start, rows_half, 0)
    dmiddle = up_rows.astype(jnp.float32) + back_two_norm
    dbranch = dmiddle.astype(jnp.bfloat16)
    grad_outleft, grad_mid_out = back_two(mid_out, outleft, dbranch.reshape(rows_half, BLOCKS, -1))
    grad_outright, dmixed = back_one(mixed, outright, grad_mid_out, False)
    dshaping = (dmixed * longconv.astype(jnp.float32)).astype(jnp.bfloat16)
    dlong = (dmixed * shaping).astype(jnp.bfloat16)
    grad_chan = lax.all_to_all(
        lax.all_to_all(dlong.T, "wide", split_axis=0, concat_axis=1, tiled=True),
        "narrow",
        split_axis=0,
        concat_axis=1,
        tiled=True,
    )
    grad_chan = channel_order(grad_chan, nwide, nnarrow, rows_half)
    dlong_re, dlong_im = to_spectrum(
        grad_chan.astype(jnp.float32).reshape(count, SEQS, length), tables
    )
    dshort_chan = from_spectrum(
        dlong_re * fil_re + dlong_im * fil_im, dlong_im * fil_re - dlong_re * fil_im, tables
    )
    dshort_chan = dshort_chan.reshape(count, SEQS * length).astype(jnp.bfloat16)
    filt_re = jnp.sum(dlong_re * sig_re + dlong_im * sig_im, axis=1, keepdims=True)
    filt_im = jnp.sum(dlong_im * sig_re - dlong_re * sig_im, axis=1, keepdims=True)
    grad_taps = from_spectrum(filt_re, filt_im, tables).reshape(count, length)
    dshort = lax.all_to_all(
        lax.all_to_all(dshort_chan, "wide", split_axis=1, concat_axis=0, tiled=True),
        "narrow",
        split_axis=1,
        concat_axis=0,
        tiled=True,
    )
    dshort = row_order(dshort, nwide, nnarrow)
    grad_modded = grad_taps * modulation
    grad_filterout = jnp.dot(act_two.T, grad_modded.T, precision=HIGHEST)
    dact_two = jnp.dot(grad_modded.T, own_cols.T, precision=HIGHEST)
    dlin_two = dact_two * jnp.cos(sinefreq * lin_two)
    scaled_two = dlin_two * sinefreq
    grad_midweight = jnp.dot(act_one.T, scaled_two, precision=HIGHEST)
    grad_midbias = jnp.sum(scaled_two, axis=0)
    dact_one = jnp.dot(scaled_two, midweight.T, precision=HIGHEST)
    dlin_one = dact_one * jnp.cos(sinefreq * lin_one)
    scaled_one = dlin_one * sinefreq
    grad_posweight = jnp.dot(feats.T, scaled_one, precision=HIGHEST)
    grad_posbias = jnp.sum(scaled_one, axis=0)
    grad_sinefreq = jnp.sum(dlin_one * lin_one, axis=0) + jnp.sum(dlin_two * lin_two, axis=0)
    after = from_behind(dshort[:2], ("wide", "narrow"), -1)
    after = jnp.where(place == group - 1, jnp.zeros_like(after), after)
    ext_grad = jnp.concatenate([dshort, after], axis=0).astype(jnp.float32)
    dsignal = (
        convtaps[0] * ext_grad[:-2] + convtaps[1] * ext_grad[1:-1] + convtaps[2] * ext_grad[2:]
    ).astype(jnp.bfloat16)
    short_grad = dshort.astype(jnp.float32)
    grad_convtaps = jnp.stack(
        [
            jnp.sum(extended[2:] * short_grad, axis=0),
            jnp.sum(extended[1:-1] * short_grad, axis=0),
            jnp.sum(extended[:-2] * short_grad, axis=0),
        ]
    )
    grad_valueleft, grad_mid_value = back_two(
        mid_value, valueleft, dsignal.reshape(rows_half, BLOCKS, -1)
    )
    grad_valueright, into_value = back_one(normone, valueright, grad_mid_value, False)
    grad_shapeleft, grad_mid_shape = back_two(
        mid_shape, shapeleft, dshaping.reshape(rows_half, BLOCKS, -1)
    )
    grad_shaperight, into_shape = back_one(normone, shaperight, grad_mid_shape, False)
    back_one_norm, grad_gainfirst, grad_shiftfirst = norm_backward(
        into_value + into_shape, hat_one, inv_one, gainfirst
    )
    full_grad = (dmiddle + back_one_norm).astype(jnp.bfloat16)
    hidden_grad = lax.all_to_all(full_grad, "narrow", split_axis=1, concat_axis=0, tiled=True)
    mixer_grads = lax.psum(
        (
            grad_gainfirst,
            grad_shiftfirst,
            grad_valueright,
            grad_valueleft,
            grad_shaperight,
            grad_shapeleft,
            grad_convtaps,
            grad_posweight,
            grad_posbias,
            grad_sinefreq,
            grad_midweight,
            grad_midbias,
            grad_outright,
            grad_outleft,
            grad_gainsecond,
            grad_shiftsecond,
        ),
        ("wide", "narrow"),
    )
    ffn_grads = lax.psum(
        (ffn_local[0], ffn_local[1], ffn_local[2], ffn_local[3], ffn_local[4], ffn_local[5]), "wide"
    )
    return (
        hidden_out,
        hidden_grad,
        mixer_grads[0],
        mixer_grads[1],
        mixer_grads[2],
        mixer_grads[3],
        mixer_grads[4],
        mixer_grads[5],
        mixer_grads[6],
        mixer_grads[7],
        mixer_grads[8],
        mixer_grads[9],
        mixer_grads[10],
        mixer_grads[11],
        grad_filterout,
        mixer_grads[12],
        mixer_grads[13],
        mixer_grads[14],
        mixer_grads[15],
        ffn_grads[0],
        ffn_grads[1],
        ffn_grads[2],
        ffn_grads[3],
        ffn_grads[4],
        ffn_grads[5],
    )


F32 = jnp.float32
BF16 = jnp.bfloat16
MESH = pl.DeviceIdType.MESH
TILE = 256
PAD = 256


def mm(a, b, precision=None):
    return lax.dot_general(
        a, b, (((1,), (0,)), ((), ())), precision=precision, preferred_element_type=F32
    )


def mm_nt(a, b, precision=None):
    return lax.dot_general(
        a, b, (((1,), (1,)), ((), ())), precision=precision, preferred_element_type=F32
    )


def mm_tn(a, b, precision=None):
    return lax.dot_general(
        a, b, (((0,), (0,)), ((), ())), precision=precision, preferred_element_type=F32
    )


def lanes(width):
    return lax.broadcasted_iota(jnp.int32, (1, width), 1)


def mask(condition, dtype=BF16):
    return jnp.where(condition, 1.0, 0.0).astype(dtype)


def between(width, low, high, dtype=BF16):
    lane = lanes(width)
    return mask((lane >= low) & (lane < high), dtype)


def join(first, second):
    return jnp.concatenate(
        [first[:, :128], first[:, 128:] + second[:, :128], second[:, 128:]], axis=1
    )


def sine_cosine(angle):
    turns = jnp.floor(angle * (1.0 / math.pi) + 0.5)
    rest = angle - turns * 3.140625
    rest = rest - turns * 9.67502593994140625e-4
    rest = rest - turns * 1.509957990978376e-7
    flip = 1.0 - 2.0 * (turns - 2.0 * jnp.floor(turns * 0.5))
    square = rest * rest
    sine = 1.0
    for divisor in (110.0, 72.0, 42.0, 20.0, 6.0):
        sine = 1.0 - square * (1.0 / divisor) * sine
    cosine = 1.0
    for divisor in (132.0, 90.0, 56.0, 30.0, 12.0, 2.0):
        cosine = 1.0 - square * (1.0 / divisor) * cosine
    return (sine * rest * flip, cosine * flip)


def fold(whole, side):
    return [
        whole[192 * b + 96 * side : 192 * b + 96 * side + 48, :] * between(384, 0, 192, F32)
        + whole[192 * b + 96 * side + 48 : 192 * b + 96 * side + 96, :] * between(384, 192, 384, F32)
        for b in range(2)
    ]


def tile_rows(index, size=TILE):
    return pl.ds(pl.multiple_of(index * size, size), size)


def whole_kernel(
    inputs,
    upstream,
    table_cos,
    table_sin,
    place,
    vectors,
    filter_vectors,
    midweight,
    filterout,
    valueright,
    valueleft,
    shaperight,
    shapeleft,
    outright,
    outleft,
    gateright,
    gateleft,
    liftright,
    liftleft,
    lowerright,
    lowerleft,
    hidden_out,
    hidden_grad,
    grad_valueright,
    grad_valueleft,
    grad_shaperight,
    grad_shapeleft,
    grad_outright,
    grad_outleft,
    grad_gateright,
    grad_gateleft,
    grad_liftright,
    grad_liftleft,
    grad_lowerright,
    grad_lowerleft,
    grad_filterout,
    grad_vectors,
    grad_filter,
    w_first,
    w_value,
    w_shape,
    w_out_first,
    w_out_second,
    w_glu,
    w_gate,
    w_lift,
    w_lower,
    w_lower_second,
    up_halves,
    stats,
    norm_one,
    inner_one,
    sig_halves,
    sig_rows,
    shaping,
    sig_pad,
    short,
    lin_one,
    act_one,
    cos_one,
    lin_two,
    act_two,
    cos_two,
    fil_spec,
    sig_spec,
    prod_spec,
    long_rows,
    long_halves,
    inner_out,
    hat_two,
    norm_two,
    inner_glu,
    factor_gate,
    factor_lift,
    hid,
    inner_lower,
    out_own,
    part_send,
    part_recv,
    d_inner_lower,
    d_gate,
    d_lift,
    d_inner_glu,
    dn_own,
    dn_send,
    dn_recv,
    d_inner_out,
    d_shaping,
    dl_rows,
    ds_pad,
    ds_halves,
    d_inner_one,
    tail_own,
    do_send,
    do_recv,
    d_lin,
    own_out,
    send_sem,
    recv_sem,
    load_sem,
):
    rows = inputs.shape[0]
    half = rows // 2
    tiles = rows // TILE
    length = 2 * rows
    spans = length // TILE
    wide = lax.axis_index("wide")
    narrow = lax.axis_index("narrow")
    core = lax.rem(wide, 2)
    sibling = (wide + 1 - 2 * core, narrow)
    partner = (wide, 1 - narrow)
    quarter = 2 * narrow + core
    own_half = pl.ds(pl.multiple_of(narrow * 384, 384), 384)
    other_half = pl.ds(pl.multiple_of((1 - narrow) * 384, 384), 384)

    barrier = pltpu.get_barrier_semaphore()
    for device in (sibling, partner):
        pl.semaphore_signal(barrier, inc=1, device_id=device, device_id_type=MESH)
    pl.semaphore_wait(barrier, 2)

    def send(source, target, device, index):
        return pltpu.make_async_remote_copy(
            src_ref=source,
            dst_ref=target,
            send_sem=send_sem.at[index],
            recv_sem=recv_sem.at[index],
            device_id=device,
            device_id_type=MESH,
        )

    load_copies = []
    for source, target in ((gateleft, w_gate), (liftleft, w_lift)):
        for k in range(2):
            copy = pltpu.make_async_copy(
                source.at[:, pl.ds(D * k, D)],
                target.at[k, pl.ds(64 * k, 192)],
                load_sem.at[len(load_copies)],
            )
            copy.start()
            load_copies.append(copy)

    up_copy = send(upstream, up_halves.at[narrow], partner, 0)
    up_copy.start()
    up_halves[narrow] = upstream[...]

    row = lax.broadcasted_iota(jnp.int32, (D, 384), 0)
    lane = lax.broadcasted_iota(jnp.int32, (D, 384), 1)
    step = jnp.where(lane >= 96, 96, 0) + jnp.where(lane >= 192, 96, 0) + jnp.where(lane >= 288, 96, 0)
    select = mask(row == lane + step + narrow * 96)
    right_half = mm(valueright[...], select).astype(BF16)
    shape_half = mm(shaperight[...], select).astype(BF16)
    for b in range(4):
        kept = between(384, 96 * b, 96 * b + 96)
        w_first[192 * b : 192 * b + 192, 0:384] = right_half * kept
        w_first[192 * b : 192 * b + 192, 384:768] = shape_half * kept
    row = lax.broadcasted_iota(jnp.int32, (D, 2 * PAD), 0)
    lane = lax.broadcasted_iota(jnp.int32, (D, 2 * PAD), 1)
    group = jnp.where(lane >= PAD, 1, 0)
    entry = lane - PAD * group
    spread = mask((row == (2 * narrow + group) * 192 + entry) & (entry < 192))
    for source, target in ((valueleft, w_value), (shapeleft, w_shape)):
        wider = mm(source[...], spread).astype(BF16)
        for b in range(4):
            for k in range(2):
                target[96 * b + 48 * k : 96 * b + 48 * k + 48, :] = wider[
                    48 * b : 48 * b + 48, :
                ] * between(2 * PAD, PAD * k, PAD * k + PAD)
    first = vectors[0:1, :]
    shift_first = vectors[1:2, :]

    @pl.loop(0, tiles)
    def _(index):
        at = tile_rows(index)
        values = inputs[at, :].astype(F32)
        average = jnp.mean(values, axis=-1, keepdims=True)
        center = values - average
        inverse = lax.rsqrt(jnp.mean(center * center, axis=-1, keepdims=True) + EPSILON)
        hat = center * inverse
        stats[at, 0:1] = average
        stats[at, 1:2] = inverse
        normed = (hat * first + shift_first).astype(BF16)
        norm_one[at, :] = normed
        inner = mm(normed, w_first[...]).astype(BF16)
        inner_one[at, :] = inner
        signal = mm(inner[:, :384], w_value[...]).astype(BF16)
        sig_halves[0, at, :] = signal[:, :PAD]
        sig_halves[1, at, :] = signal[:, PAD:]
        shaped = mm(inner[:, 384:], w_shape[...])
        shaping[0, at, :] = shaped[:, :PAD]
        shaping[1, at, :] = shaped[:, PAD:]

    sig_copy = send(sig_halves.at[1 - core], sig_rows.at[core], sibling, 1)
    sig_copy.start()
    sig_rows[core] = sig_halves[core]

    row = lax.broadcasted_iota(jnp.int32, (D, PAD), 0)
    lane = lax.broadcasted_iota(jnp.int32, (D, PAD), 1)
    pick = mask((row == quarter * 192 + lane) & (lane < 192), F32)
    conv = mm(vectors[...], pick, HIGHEST)
    own_out[...] = mm(filterout[...], pick, HIGHEST)
    pos_bias = filter_vectors[8:9, :]
    mid_bias = filter_vectors[9:10, :]
    frequency = filter_vectors[10:11, :]
    ranks = 5 * (quarter * 192 + lanes(PAD))
    for bound in range(5):
        ranks = jnp.where(ranks >= D, ranks - D, ranks)
    lowest = math.log(0.25 / length)
    highest = math.log(1.0 / 30.0)
    rate = jnp.exp(lowest + ranks.astype(F32) * (1.0 / D) * (highest - lowest))
    loud = jnp.sqrt(2.0 * rate)

    def decay(index):
        places = (lax.broadcasted_iota(jnp.int32, (TILE, PAD), 0) + index * TILE).astype(F32)
        return jnp.exp(-rate * places) * loud

    @pl.loop(0, spans)
    def _(index):
        at = tile_rows(index)
        one = mm(place[at, :], filter_vectors[0:8, :], HIGHEST) + pos_bias
        sine, cosine = sine_cosine(frequency * one)
        lin_one[at, :] = one
        act_one[at, :] = sine
        cos_one[at, :] = cosine
        two = mm(sine, midweight[...], HIGHEST) + mid_bias
        sine, cosine = sine_cosine(frequency * two)
        lin_two[at, :] = two
        act_two[at, :] = sine
        cos_two[at, :] = cosine
        short[at, :] = (mm(sine, own_out[...], HIGHEST) * decay(index)).astype(BF16)

    @pl.loop(0, spans)
    def _(index):
        at = tile_rows(index)
        real = mm(table_cos[at, :], short[...])
        imag = mm(table_sin[at, :], short[...])
        turn_cos = place[at, 5:6] * (1.0 / length)
        turn_sin = place[at, 6:7] * (1.0 / length)
        fil_spec[0, at, :] = real * turn_cos + imag * turn_sin
        fil_spec[1, at, :] = imag * turn_cos - real * turn_sin

    out_half = outright[:, own_half]
    w_out_first[0:192, :] = out_half * between(384, 0, 192)
    w_out_first[192:256, :] = jnp.zeros((64, 384), BF16)
    w_out_first[256:448, :] = out_half * between(384, 192, 384)
    w_out_first[448:512, :] = jnp.zeros((64, 384), BF16)
    for b in range(4):
        for k in range(4):
            w_out_second[b // 2, 192 * (b % 2) + 48 * k : 192 * (b % 2) + 48 * k + 48, :] = outleft[
                48 * b : 48 * b + 48, :
            ] * between(D, 192 * k, 192 * k + 192)
    lane = lanes(384)
    inside = lane - jnp.where(lane >= 192, 192, 0)
    for b in range(4):
        kept = mask((inside >= 48 * b) & (inside < 48 * b + 48))
        w_glu[192 * b : 192 * b + 192, 0:384] = gateright[...] * kept
        w_glu[192 * b : 192 * b + 192, 384:768] = liftright[...] * kept
    for target in (w_gate, w_lift):
        target[0, 192:256, :] = jnp.zeros((64, D), BF16)
        target[1, 0:64, :] = jnp.zeros((64, D), BF16)
    w_lower[0] = lowerright[:, 0:256] * between(256, 0, 192)
    w_lower[1] = lowerright[:, 128:384] * between(256, 64, 256)
    for b in range(2):
        for k in range(4):
            w_lower_second[192 * b + 48 * k : 192 * b + 48 * k + 48, :] = lowerleft[
                48 * b : 48 * b + 48, :
            ] * between(D, 192 * k, 192 * k + 192)

    sig_copy.wait_recv()
    sig_pad[0:8, :] = jnp.zeros((8, PAD), F32)
    for part in range(2):
        sig_pad[8 + part * rows : 8 + part * rows + rows, :] = sig_rows[part].astype(F32)
    for index in range(spans):
        start = 8 + index * TILE
        total = conv[4:5, :] * sig_pad[start : start + TILE, :]
        total += conv[5:6, :] * sig_pad[start - 1 : start - 1 + TILE, :]
        total += conv[6:7, :] * sig_pad[start - 2 : start - 2 + TILE, :]
        short[index * TILE : index * TILE + TILE, :] = total.astype(BF16)

    @pl.loop(0, spans)
    def _(index):
        at = tile_rows(index)
        real = mm(table_cos[at, :], short[...])
        imag = mm(table_sin[at, :], short[...])
        sig_spec[0, at, :] = real
        sig_spec[1, at, :] = imag
        fil_re = fil_spec[0, at, :]
        fil_im = fil_spec[1, at, :]
        prod_spec[0, at, :] = (real * fil_re - imag * fil_im).astype(BF16)
        prod_spec[1, at, :] = (real * fil_im + imag * fil_re).astype(BF16)

    per_half = rows // TILE

    @pl.loop(0, spans)
    def _(index):
        at = tile_rows(index)
        result = mm(table_cos[at, :], prod_spec[0]) + mm(table_sin[at, :], prod_spec[1])
        long_rows[index // per_half, tile_rows(lax.rem(index, per_half)), :] = result.astype(BF16)

    long_copy = send(long_rows.at[1 - core], long_halves.at[core], sibling, 2)
    long_copy.start()
    long_halves[core] = long_rows[core]
    long_copy.wait_recv()
    sig_copy.wait_send()
    long_copy.wait_send()

    def inner_copy(index):
        at = tile_rows(index)
        return send(inner_out.at[narrow, at], inner_out.at[narrow, at], partner, 3 + index)

    def dn_copy(index):
        at = tile_rows(index)
        return send(dn_send.at[at], dn_recv.at[at], partner, 5 + index)

    def part_copy(index):
        at = tile_rows(index)
        return send(part_send.at[at], part_recv.at[at], partner, 7 + index)

    def do_copy(index):
        at = tile_rows(index)
        return send(do_send.at[at], do_recv.at[at], partner, 11 + index)

    @pl.loop(0, tiles)
    def _(index):
        at = tile_rows(index)
        inner = None
        for k in range(2):
            product = (shaping[k, at, :] * long_halves[k, at, :].astype(F32)).astype(BF16)
            term = mm(product, w_out_first[k * PAD : k * PAD + PAD, :])
            inner = term if inner is None else inner + term
        inner_out[narrow, at, :] = inner.astype(BF16)
        inner_copy(index).start()

    up_copy.wait_recv()
    for copy in load_copies:
        copy.wait()

    gain_second = vectors[2:3, :]
    shift_second = vectors[3:4, :]

    @pl.loop(0, tiles)
    def _(index):
        at = tile_rows(index)
        inner_copy(index).wait_recv()
        mid = inputs[at, :].astype(F32)
        mid += mm(inner_out[0, at, :], w_out_second[0])
        mid += mm(inner_out[1, at, :], w_out_second[1])
        dn_own[at, :] = mid
        center = mid - jnp.mean(mid, axis=-1, keepdims=True)
        inverse = lax.rsqrt(jnp.mean(center * center, axis=-1, keepdims=True) + EPSILON)
        hat = center * inverse
        hat_two[at, :] = hat
        stats[at, 2:3] = inverse
        normed = (hat * gain_second + shift_second).astype(BF16)
        norm_two[at, :] = normed
        inner = mm(normed, w_glu[...]).astype(BF16)
        inner_glu[at, :] = inner
        lower = [None, None]
        for k in range(2):
            for columns in (slice(0, 256), slice(256, 512), slice(512, 768)):
                gate = mm(inner[:, 128 * k : 128 * k + 256], w_gate[k, :, columns])
                lift = mm(inner[:, 384 + 128 * k : 384 + 128 * k + 256], w_lift[k, :, columns])
                cumulative = 0.5 * (1.0 + lax.erf(gate * (1.0 / math.sqrt(2.0))))
                density = jnp.exp(-0.5 * gate * gate) * (1.0 / math.sqrt(2.0 * math.pi))
                activated = gate * cumulative
                unit = (activated * lift).astype(BF16)
                hid[k, at, columns] = unit
                factor_lift[k, :, columns] = activated
                factor_gate[k, :, columns] = lift * (cumulative + gate * density)
                term = mm(unit, w_lower[k, columns, :])
                lower[k] = term if lower[k] is None else lower[k] + term
        inner_low = join(*lower).astype(BF16)
        inner_lower[at, :] = inner_low
        out_own[at, :] = dn_own[at, own_half] + mm(inner_low, w_lower_second[:, own_half])
        part_send[at, :] = mm(inner_low, w_lower_second[:, other_half]).astype(BF16)

        above = jnp.concatenate([up_halves[0, at, :], up_halves[1, at, :]], axis=1)
        d_low = mm_nt(above, w_lower_second[...]).astype(BF16)
        d_inner_lower[at, :] = d_low
        gates = [None, None]
        lifts = [None, None]
        for k in range(2):
            for columns in (slice(0, 256), slice(256, 512), slice(512, 768)):
                d_hidden = mm_nt(d_low[:, 128 * k : 128 * k + 256], w_lower[k, columns, :])
                to_gate = (d_hidden * factor_gate[k, :, columns]).astype(BF16)
                to_lift = (d_hidden * factor_lift[k, :, columns]).astype(BF16)
                d_gate[k, at, columns] = to_gate
                d_lift[k, at, columns] = to_lift
                term = mm_nt(to_gate, w_gate[k, :, columns])
                gates[k] = term if gates[k] is None else gates[k] + term
                term = mm_nt(to_lift, w_lift[k, :, columns])
                lifts[k] = term if lifts[k] is None else lifts[k] + term
        d_glu = jnp.concatenate([join(*gates), join(*lifts)], axis=1).astype(BF16)
        d_inner_glu[at, :] = d_glu
        into = mm_nt(d_glu, w_glu[...])
        dn_own[at, :] = into
        dn_send[at, :] = into.astype(BF16)
        dn_copy(index).start()

    @pl.loop(0, tiles)
    def _(index):
        part_copy(index).start()

    for side in range(2):
        columns = slice(384 * side, 384 * side + 384)
        folded = fold(mm_tn(inner_lower[...], up_halves[side]), side)
        for b in range(2):
            grad_lowerleft[48 * b : 48 * b + 48, columns] = folded[b].astype(BF16)
    low_lanes = lanes(128) < 64
    for columns in (slice(0, 384), slice(384, 768)):
        parts = [
            mm_tn(hid[k, :, columns], d_inner_lower[:, 128 * k : 128 * k + 256]) for k in range(2)
        ]
        grad_lowerright[columns, 0:128] = parts[0][:, 0:128].astype(BF16)
        grad_lowerright[columns, 128:256] = jnp.where(
            low_lanes, parts[0][:, 128:256], parts[1][:, 0:128]
        ).astype(BF16)
        grad_lowerright[columns, 256:384] = parts[1][:, 128:256].astype(BF16)
    for offset, upper, target in ((0, d_gate, grad_gateleft), (384, d_lift, grad_liftleft)):
        for k in range(2):
            for start in (0, 384):
                whole = mm_tn(
                    inner_glu[:, offset + 128 * k : offset + 128 * k + 256],
                    upper[k, :, start : start + 384],
                )
                target[:, D * k + start : D * k + start + 384] = whole[
                    64 * k : 64 * k + 192, :
                ].astype(BF16)
    for offset, target in ((0, grad_gateright), (384, grad_liftright)):
        whole = mm_tn(norm_two[...], d_inner_glu[:, offset : offset + 384])
        total = None
        for b in range(4):
            term = whole[192 * b : 192 * b + 192, :] * mask(
                (inside >= 48 * b) & (inside < 48 * b + 48), F32
            )
            total = term if total is None else total + term
        target[...] = total.astype(BF16)

    half_mask = mask((lanes(D) >= narrow * 384) & (lanes(D) < narrow * 384 + 384), F32)
    grad_vectors[...] = jnp.zeros(grad_vectors.shape, F32)

    @pl.loop(0, tiles)
    def _(index):
        at = tile_rows(index)
        dn_copy(index).wait_recv()
        into = dn_own[at, :] + dn_recv[at, :].astype(F32)
        hat = hat_two[at, :]
        grad_vectors[2:3, :] += jnp.sum(into * hat, axis=0, keepdims=True) * half_mask
        grad_vectors[3:4, :] += jnp.sum(into, axis=0, keepdims=True) * half_mask
        scaled = into * gain_second
        above = jnp.concatenate([up_halves[0, at, :], up_halves[1, at, :]], axis=1)
        d_mid = above.astype(F32) + stats[at, 2:3] * (
            scaled
            - jnp.mean(scaled, axis=-1, keepdims=True)
            - hat * jnp.mean(scaled * hat, axis=-1, keepdims=True)
        )
        hat_two[at, :] = d_mid
        branch = d_mid.astype(BF16)
        d_inner = mm_nt(branch, w_out_second[narrow]).astype(BF16)
        d_inner_out[at, :] = d_inner
        for k in range(2):
            d_mixed = mm_nt(d_inner, w_out_first[k * PAD : k * PAD + PAD, :])
            d_shaping[k, at, :] = (d_mixed * long_halves[k, at, :].astype(F32)).astype(BF16)
            sig_halves[k, at, :] = (d_mixed * shaping[k, at, :]).astype(BF16)

    dl_copy = send(sig_halves.at[1 - core], dl_rows.at[core], sibling, 9)
    dl_copy.start()
    dl_rows[core] = sig_halves[core]

    for side in range(2):
        columns = slice(384 * side, 384 * side + 384)
        folded = fold(mm_tn(inner_out[narrow], hat_two[:, columns].astype(BF16)), side)
        for b in range(2):
            at = pl.ds(pl.multiple_of(narrow * 96 + 48 * b, 16), 48)
            grad_outleft[at, columns] = folded[b].astype(BF16)
            at = pl.ds(pl.multiple_of((1 - narrow) * 96 + 48 * b, 16), 48)
            grad_outleft[at, columns] = jnp.zeros((48, 384), BF16)
    parts = []
    for k in range(2):
        product = (shaping[k] * long_halves[k].astype(F32)).astype(BF16)
        parts.append(mm_tn(product, d_inner_out[...]))
    grad_outright[:, own_half] = jnp.where(
        lanes(384) < 192, parts[0][0:192, :], parts[1][0:192, :]
    ).astype(BF16)
    grad_outright[:, other_half] = jnp.zeros((192, 384), BF16)

    dl_copy.wait_recv()

    @pl.loop(0, spans)
    def _(index):
        at = tile_rows(index)
        upper = dl_rows[...].reshape(length, PAD)
        real = mm(table_cos[at, :], upper)
        imag = mm(table_sin[at, :], upper)
        fil_re = fil_spec[0, at, :]
        fil_im = fil_spec[1, at, :]
        prod_spec[0, at, :] = (real * fil_re + imag * fil_im).astype(BF16)
        prod_spec[1, at, :] = (imag * fil_re - real * fil_im).astype(BF16)
        sig_re = sig_spec[0, at, :]
        sig_im = sig_spec[1, at, :]
        sig_spec[0, at, :] = real * sig_re + imag * sig_im
        sig_spec[1, at, :] = imag * sig_re - real * sig_im

    ds_pad[length : length + 8, :] = jnp.zeros((8, PAD), F32)

    @pl.loop(0, spans)
    def _(index):
        at = tile_rows(index)
        result = mm(table_cos[at, :], prod_spec[0]) + mm(table_sin[at, :], prod_spec[1])
        ds_pad[at, :] = result.astype(BF16).astype(F32)

    for index in range(spans):
        start = index * TILE
        total = conv[4:5, :] * ds_pad[start : start + TILE, :]
        total += conv[5:6, :] * ds_pad[start + 1 : start + 1 + TILE, :]
        total += conv[6:7, :] * ds_pad[start + 2 : start + 2 + TILE, :]
        part, inner_start = divmod(start, rows)
        long_rows[part, inner_start : inner_start + TILE, :] = total.astype(BF16)
    ds_copy = send(long_rows.at[1 - core], ds_halves.at[core], sibling, 10)
    ds_copy.start()
    ds_halves[core] = long_rows[core]

    sums = [jnp.zeros((1, PAD), F32) for _ in range(3)]
    for index in range(spans):
        start = index * TILE
        upper = ds_pad[start : start + TILE, :]
        for j in range(3):
            sums[j] += jnp.sum(
                upper * sig_pad[8 + start - j : 8 + start - j + TILE, :], axis=0, keepdims=True
            )
    sums = jnp.concatenate(sums + [jnp.zeros((5, PAD), F32)], axis=0)
    lane = lax.broadcasted_iota(jnp.int32, (PAD, D), 1)
    row = lax.broadcasted_iota(jnp.int32, (PAD, D), 0)
    unpick = mask((lane == quarter * 192 + row) & (row < 192), F32)
    conv_sums = mm(sums, unpick, HIGHEST)
    grad_vectors[4:7, :] = conv_sums[0:3, :]

    @pl.loop(0, spans)
    def _(index):
        at = tile_rows(index)
        turn_cos = place[at, 5:6] * (1.0 / length)
        turn_sin = place[at, 6:7] * (1.0 / length)
        real = sig_spec[0, at, :]
        imag = sig_spec[1, at, :]
        prod_spec[0, at, :] = (real * turn_cos - imag * turn_sin).astype(BF16)
        prod_spec[1, at, :] = (imag * turn_cos + real * turn_sin).astype(BF16)

    d_lin[...] = jnp.zeros(d_lin.shape, F32)
    grad_filter[...] = jnp.zeros(grad_filter.shape, F32)

    @pl.loop(0, spans)
    def _(index):
        at = tile_rows(index)
        d_taps = mm(table_cos[at, :], prod_spec[0]) + mm(table_sin[at, :], prod_spec[1])
        d_mod = d_taps * decay(index)
        d_lin[...] += mm_tn(act_two[at, :], d_mod, HIGHEST)
        two = mm_nt(d_mod, own_out[...], HIGHEST) * cos_two[at, :]
        scaled_two = two * frequency
        grad_filter[0:128, :] += mm_tn(act_one[at, :], scaled_two, HIGHEST)
        one = mm_nt(scaled_two, midweight[...], HIGHEST) * cos_one[at, :]
        scaled_one = one * frequency
        grad_filter[128:136, :] += mm_tn(place[at, :], scaled_one, HIGHEST)
        grad_filter[136:137, :] += jnp.sum(scaled_one, axis=0, keepdims=True)
        grad_filter[137:138, :] += jnp.sum(scaled_two, axis=0, keepdims=True)
        grad_filter[138:139, :] += jnp.sum(one * lin_one[at, :] + two * lin_two[at, :], axis=0, keepdims=True)

    grad_filterout[...] = mm(d_lin[...], unpick, HIGHEST)

    ds_copy.wait_recv()
    first_half = vectors[0:1, own_half]
    tail_lane = lax.broadcasted_iota(jnp.int32, (TILE, 128), 1)

    @pl.loop(0, tiles)
    def _(index):
        at = tile_rows(index)
        to_value = jnp.concatenate([ds_halves[0, at, :], ds_halves[1, at, :]], axis=1)
        to_shape = jnp.concatenate([d_shaping[0, at, :], d_shaping[1, at, :]], axis=1)
        d_inner = jnp.concatenate(
            [mm_nt(to_value, w_value[...]), mm_nt(to_shape, w_shape[...])], axis=1
        ).astype(BF16)
        d_inner_one[at, :] = d_inner
        into = mm_nt(d_inner, w_first[...])
        dn_own[at, :] = into
        scaled = into * first
        plain = jnp.sum(scaled, axis=-1, keepdims=True)
        hat = (inputs[at, :].astype(F32) - stats[at, 0:1]) * stats[at, 1:2]
        along = jnp.sum(scaled * hat, axis=-1, keepdims=True)
        tail = jnp.where(tail_lane == 0, plain, jnp.where(tail_lane == 1, along, 0.0))
        tail_own[at, :] = tail
        do_send[at, 0:384] = dn_own[at, other_half].astype(BF16)
        do_send[at, 384:512] = tail.astype(BF16)
        do_copy(index).start()

    lane = lax.broadcasted_iota(jnp.int32, (384, D), 1)
    row = lax.broadcasted_iota(jnp.int32, (384, D), 0)
    step = jnp.where(row >= 96, 96, 0) + jnp.where(row >= 192, 96, 0) + jnp.where(row >= 288, 96, 0)
    unselect = mask(lane == row + step + narrow * 96)
    for offset, target in ((0, grad_valueright), (384, grad_shaperight)):
        whole = mm_tn(norm_one[...], d_inner_one[:, offset : offset + 384])
        total = None
        for b in range(4):
            term = whole[192 * b : 192 * b + 192, :] * between(
                384, 96 * b, 96 * b + 96, F32
            )
            total = term if total is None else total + term
        target[...] = mm(total.astype(BF16), unselect).astype(BF16)
    lane = lax.broadcasted_iota(jnp.int32, (2 * PAD, D), 1)
    row = lax.broadcasted_iota(jnp.int32, (2 * PAD, D), 0)
    group = jnp.where(row >= PAD, 1, 0)
    entry = row - PAD * group
    unspread = mask((lane == (2 * narrow + group) * 192 + entry) & (entry < 192))
    for offset, upper, target in ((0, ds_halves, grad_valueleft), (384, d_shaping, grad_shapeleft)):
        above = jnp.concatenate([upper[0], upper[1]], axis=1)
        whole = mm_tn(inner_one[:, offset : offset + 384], above)
        pieces = []
        for b in range(4):
            total = None
            for k in range(2):
                term = whole[96 * b + 48 * k : 96 * b + 48 * k + 48, :] * between(
                    2 * PAD, PAD * k, PAD * k + PAD, F32
                )
                total = term if total is None else total + term
            pieces.append(total)
        total = jnp.concatenate(pieces, axis=0).astype(BF16)
        target[...] = mm(total, unspread).astype(BF16)

    @pl.loop(0, tiles)
    def _(index):
        at = tile_rows(index)
        part_copy(index).wait_recv()
        hidden_out[at, :] = (out_own[at, :] + part_recv[at, :].astype(F32)).astype(BF16)
        do_copy(index).wait_recv()
        came = do_recv[at, :].astype(F32)
        into = dn_own[at, own_half] + came[:, 0:384]
        tail = (tail_own[at, :] + came[:, 384:512]) * (1.0 / D)
        hat = (inputs[at, own_half].astype(F32) - stats[at, 0:1]) * stats[at, 1:2]
        grad_vectors[0:1, own_half] += jnp.sum(into * hat, axis=0, keepdims=True)
        grad_vectors[1:2, own_half] += jnp.sum(into, axis=0, keepdims=True)
        hidden_grad[at, :] = (
            hat_two[at, own_half]
            + stats[at, 1:2] * (into * first_half - tail[:, 0:1] - hat * tail[:, 1:2])
        ).astype(BF16)

    for copy in (up_copy, dl_copy, ds_copy):
        copy.wait_send()

    @pl.loop(0, tiles)
    def _(index):
        for copy in (inner_copy, dn_copy, part_copy, do_copy):
            copy(index).wait_send()


def transform_tables(length):
    index = np.arange(length, dtype=np.float64) + 0.5
    angle = np.outer(index, index) * (math.pi / length)
    return (np.cos(angle).astype(jnp.bfloat16), np.sin(angle).astype(jnp.bfloat16))


def place_table(length):
    places = np.arange(length, dtype=np.float64)
    angle = places * (2.0 * math.pi / length)
    turn = (places + 0.5) * (math.pi / (2.0 * length))
    columns = [
        places / length,
        np.cos(angle),
        np.sin(angle),
        np.cos(2.0 * angle),
        np.sin(2.0 * angle),
        np.cos(turn),
        np.sin(turn),
        np.zeros(length),
    ]
    return np.stack(columns, axis=1).astype(np.float32)


def pair_body(
    hidden_in,
    gainfirst,
    shiftfirst,
    valueright,
    valueleft,
    shaperight,
    shapeleft,
    convtaps,
    posweight,
    posbias,
    sinefreq,
    midweight,
    midbias,
    filterout,
    outright,
    outleft,
    gainsecond,
    shiftsecond,
    gateright,
    gateleft,
    liftright,
    liftleft,
    lowerright,
    lowerleft,
    grad_out,
):
    rows = hidden_in.shape[0]
    length = 2 * rows
    table_cos, table_sin = transform_tables(length)
    vectors = jnp.concatenate(
        [jnp.stack([gainfirst, shiftfirst, gainsecond, shiftsecond]), convtaps, jnp.zeros((1, D), F32)]
    )
    filter_vectors = jnp.concatenate(
        [posweight, jnp.zeros((3, 128), F32), jnp.stack([posbias, midbias, sinefreq]), jnp.zeros((5, 128), F32)]
    )

    def out(extent, dtype=BF16):
        return jax.ShapeDtypeStruct(extent, dtype)

    def buf(*extent, dtype=BF16):
        return pltpu.VMEM(extent, dtype)

    vmem = pl.BlockSpec(memory_space=pltpu.VMEM)
    hbm = pl.BlockSpec(memory_space=pl.ANY)
    results = pl.pallas_call(
        whole_kernel,
        out_shape=(
            out((rows, 384)),
            out((rows, 384)),
            out((192, D)),
            out((192, D)),
            out((192, D)),
            out((192, D)),
            out((192, D)),
            out((192, D)),
            out(gateright.shape),
            out(gateleft.shape),
            out(liftright.shape),
            out(liftleft.shape),
            out(lowerright.shape),
            out(lowerleft.shape),
            out((128, D), F32),
            out((8, D), F32),
            out((144, 128), F32),
        ),
        in_specs=[vmem] * 16 + [hbm, vmem, hbm, vmem, vmem],
        out_specs=[vmem] * 17,
        scratch_shapes=[
            buf(D, D),
            buf(384, 512),
            buf(384, 512),
            buf(512, 384),
            buf(2, 384, D),
            buf(D, D),
            buf(2, 256, D),
            buf(2, 256, D),
            buf(2, D, 256),
            buf(384, D),
            buf(2, rows, 384),
            buf(rows, 128, dtype=F32),
            buf(rows, D),
            buf(rows, D),
            buf(2, rows, PAD),
            buf(2, rows, PAD),
            buf(2, rows, PAD, dtype=F32),
            buf(length + 8, PAD, dtype=F32),
            buf(length, PAD),
            buf(length, 128, dtype=F32),
            buf(length, 128, dtype=F32),
            buf(length, 128, dtype=F32),
            buf(length, 128, dtype=F32),
            buf(length, 128, dtype=F32),
            buf(length, 128, dtype=F32),
            buf(2, length, PAD, dtype=F32),
            buf(2, length, PAD, dtype=F32),
            buf(2, length, PAD),
            buf(2, rows, PAD),
            buf(2, rows, PAD),
            buf(2, rows, 384),
            buf(rows, D, dtype=F32),
            buf(rows, D),
            buf(rows, D),
            buf(2, TILE, D, dtype=F32),
            buf(2, TILE, D, dtype=F32),
            buf(2, rows, D),
            buf(rows, 384),
            buf(rows, 384, dtype=F32),
            buf(rows, 384),
            buf(rows, 384),
            buf(rows, 384),
            buf(2, rows, D),
            buf(2, rows, D),
            buf(rows, D),
            buf(rows, D, dtype=F32),
            buf(rows, D),
            buf(rows, D),
            buf(rows, 384),
            buf(2, rows, PAD),
            buf(2, rows, PAD),
            buf(length + 8, PAD, dtype=F32),
            buf(2, rows, PAD),
            buf(rows, D),
            buf(rows, 128, dtype=F32),
            buf(rows, 512),
            buf(rows, 512),
            buf(128, PAD, dtype=F32),
            buf(128, PAD, dtype=F32),
            pltpu.SemaphoreType.DMA((13,)),
            pltpu.SemaphoreType.DMA((13,)),
            pltpu.SemaphoreType.DMA((4,)),
        ],
        compiler_params=pltpu.CompilerParams(
            collective_id=0, has_side_effects=True, vmem_limit_bytes=63 * 1024 * 1024
        ),
    )(
        hidden_in,
        grad_out,
        table_cos,
        table_sin,
        place_table(length),
        vectors,
        filter_vectors,
        midweight,
        filterout,
        valueright,
        valueleft,
        shaperight,
        shapeleft,
        outright,
        outleft,
        gateright,
        gateleft,
        liftright,
        liftleft,
        lowerright,
        lowerleft,
    )
    hidden_out, hidden_grad = results[:2]
    mixer = lax.psum([grad.astype(F32) for grad in results[2:8]], ("wide", "narrow"))
    channel = lax.psum([grad.astype(F32) for grad in results[8:14]], "wide")
    grad_filterout, grad_vectors, grad_filter = lax.psum(results[14:17], ("wide", "narrow"))
    count = D // (lax.axis_size("wide") * lax.axis_size("narrow"))
    combined = lax.axis_index("wide") * lax.axis_size("narrow") + lax.axis_index("narrow")
    grad_filterout = lax.dynamic_slice_in_dim(grad_filterout, combined * count, count, 1)
    return (
        hidden_out,
        hidden_grad,
        grad_vectors[0],
        grad_vectors[1],
        mixer[0],
        mixer[1],
        mixer[2],
        mixer[3],
        grad_vectors[4:7],
        grad_filter[128:133],
        grad_filter[136],
        grad_filter[138],
        grad_filter[:128],
        grad_filter[137],
        grad_filterout,
        mixer[4],
        mixer[5],
        grad_vectors[2],
        grad_vectors[3],
        *channel,
    )


def solution(mesh):
    pairs = mesh.shape["wide"] == 2 * SEQS and mesh.shape["narrow"] == 2
    return jax.shard_map(
        pair_body if pairs else body,
        mesh=mesh,
        in_specs=(
            P("wide", None),
            P(),
            P(),
            P(),
            P(),
            P(),
            P(),
            P(),
            P(),
            P(),
            P(),
            P(),
            P(),
            P(),
            P(),
            P(),
            P(),
            P(),
            P(None, "narrow"),
            P(None, "narrow"),
            P(None, "narrow"),
            P(None, "narrow"),
            P(None, "narrow"),
            P("narrow", None),
            P("wide", "narrow"),
        ),
        out_specs=(
            P("wide", "narrow"),
            P("wide", "narrow"),
            P(),
            P(),
            P(),
            P(),
            P(),
            P(),
            P(),
            P(),
            P(),
            P(),
            P(),
            P(),
            P(None, ("wide", "narrow")),
            P(),
            P(),
            P(),
            P(),
            P(None, "narrow"),
            P(None, "narrow"),
            P(None, "narrow"),
            P(None, "narrow"),
            P(None, "narrow"),
            P("narrow", None),
        ),
        check_vma=False,
    )
```

profile of v0, /device:TPU:0, one launch (start us, length us, event | category | flops | bytes accessed | tf_op | source)
XLA Modules:
  0.0 310.6 jit_solution(7999417704507240588)
XLA Ops:
  7.2 0.0 all-reduce.7.cloned.1.call-start
  7.2 0.7 stack.21
  7.9 0.7 stack.22
  8.6 0.7 stack.23
  9.3 0.7 stack.24
  10.0 2.6 concatenate.7.filter_vectors
  12.6 1.3 concatenate.6.vectors
  13.9 87.8 %shard_map.459 = (bf16[512,384]{1,0:T(8,128)(2,1)}, bf16[512,384]{1,0:T(8,128)(2,1)}, bf16[192,768]{1,0:T(8,128)(2,1)}, bf16[192,768]{1,0:T(8,128)(2,1)}, bf16[1...) custom-call(bf16[512,768]{1,0:T(8,128)(2,1)} %inputs.1, ...), custom_call_target="tpu_custom_call" | custom-call | tf_op jit(solution)/shard_map/pallas_call | solution.py:1259
  101.8 0.0 copy-start
  101.8 0.0 copy-start.1
  101.8 0.0 copy-start.2
  101.8 0.0 copy-start.5
  101.8 0.0 copy-start.6
  101.8 0.0 copy-start.7
  101.8 0.0 all-reduce.7.cloned.1.call-update
  101.8 89.5 %all-reduce.8 = (f32[8,768]{1,0:T(8,128)S(1)}, f32[192,768]{1,0:T(8,128)}, f32[192,768]{1,0:T(8,128)}, f32[192,768]{1,0:T(8,128)}, f32[192,768]{1,0:T(8,128)}, /*index=5*/f32[192,768]{1,0:T(8,128)}, f32[192,768]{1,0:T(8,128)}) all-reduce(f32[8,768]{1,0:T(8,128)} %get-tuple-element.44, ...), channel_id=1, replica_groups=mesh['wide'=16,'narrow'=2] {'wide','narrow'}, use_global_device_ids=true, to_apply=%region_0.0 | all-reduce | flops 890880 | bytes 5357568 | tf_op jit(solution)/shard_map/psum | solution.py:1375
  191.3 0.6 slice.42
  191.9 0.0 copy-done
  191.9 0.0 copy-done.1
  191.9 0.0 copy-done.2
  191.9 0.0 copy-done.5
  191.9 0.0 copy-done.6
  191.9 0.0 copy-done.7
  192.0 0.0 copy-start.4
  192.0 0.0 copy-start.3
  192.0 103.9 %all-reduce.9 = (f32[192,384]{1,0:T(8,128)}, f32[192,1536]{1,0:T(8,128)}, f32[192,384]{1,0:T(8,128)}, f32[192,1536]{1,0:T(8,128)}, f32[768,384]{1,0:T(8,128)}, /*index=5*/f32[96,768]{1,0:T(8,128)}) all-reduce(bf16[192,384]{1,0:T(8,128)(2,1)S(1)} %copy-done.5, ...), channel_id=1, replica_groups=mesh['wide'=16,'narrow'=2] {'wide'}, use_global_device_ids=true, to_apply=%region_9.0 | all-reduce | flops 1105920 | bytes 6635520 | tf_op jit(solution)/shard_map/psum | solution.py:1374
  295.9 0.6 slice_reduce_fusion
  296.5 0.0 all-reduce.7.cloned.1.call-done
  296.5 1.3 slice_bitcast_fusion
  297.8 1.3 slice.43
  299.1 1.5 slice.46
  300.6 1.0 constant_dynamic-slice_fusion
  301.6 0.7 copy.53
  302.3 0.0 copy-done.4
  302.3 0.7 copy.83
  303.0 0.0 copy-done.3
  303.0 0.7 copy.84
  (3 shorter events, 0.0 us)
Async XLA Ops:
  7.2 289.3 %all-reduce.7.cloned.1.call-start = ((), (), s32[]{:S(2)}) async-start(), calls=%async_computation | async-start | bytes 933888 | tf_op jit(solution)/shard_map/psum | solution.py:1375
  101.8 90.2 %copy-start = (bf16[192,1536]{1,0:T(8,128)(2,1)S(1)}, bf16[192,1536]{1,0:T(8,128)(2,1)}, u32[]{:S(2)}) copy-start(bf16[192,1536]{1,0:T(8,128)(2,1)} %get-tuple-element.54) | copy-start | bytes 1769476
  101.8 90.2 %copy-start.1 = (bf16[192,1536]{1,0:T(8,128)(2,1)S(1)}, bf16[192,1536]{1,0:T(8,128)(2,1)}, u32[]{:S(2)}) copy-start(bf16[192,1536]{1,0:T(8,128)(2,1)} %get-tuple-element.56) | copy-start | bytes 1769476
  101.8 90.2 %copy-start.2 = (bf16[768,384]{1,0:T(8,128)(2,1)S(1)}, bf16[768,384]{1,0:T(8,128)(2,1)}, u32[]{:S(2)}) copy-start(bf16[768,384]{1,0:T(8,128)(2,1)} %get-tuple-element.57) | copy-start | bytes 1769476
  101.8 90.1 %copy-start.5 = (bf16[192,384]{1,0:T(8,128)(2,1)S(1)}, bf16[192,384]{1,0:T(8,128)(2,1)}, u32[]{:S(2)}) copy-start(bf16[192,384]{1,0:T(8,128)(2,1)} %get-tuple-element.53) | copy-start | bytes 442372
  101.8 90.1 %copy-start.6 = (bf16[192,384]{1,0:T(8,128)(2,1)S(1)}, bf16[192,384]{1,0:T(8,128)(2,1)}, u32[]{:S(2)}) copy-start(bf16[192,384]{1,0:T(8,128)(2,1)} %get-tuple-element.55) | copy-start | bytes 442372
  101.8 90.1 %copy-start.7 = (bf16[96,768]{1,0:T(8,128)(2,1)S(1)}, bf16[96,768]{1,0:T(8,128)(2,1)}, u32[]{:S(2)}) copy-start(bf16[96,768]{1,0:T(8,128)(2,1)} %get-tuple-element.58) | copy-start | bytes 442372
  192.0 110.3 %copy-start.4 = (bf16[512,384]{1,0:T(8,128)(2,1)S(1)}, bf16[512,384]{1,0:T(8,128)(2,1)}, u32[]{:S(2)}) copy-start(bf16[512,384]{1,0:T(8,128)(2,1)} %get-tuple-element.131) | copy-start | bytes 1179652
  192.0 111.0 %copy-start.3 = (bf16[512,384]{1,0:T(8,128)(2,1)S(1)}, bf16[512,384]{1,0:T(8,128)(2,1)}, u32[]{:S(2)}) copy-start(bf16[512,384]{1,0:T(8,128)(2,1)} %get-tuple-element.132) | copy-start | bytes 1179652
Sparse Core Ops, SparseCore 0:
  102.0 131.3 all-reduce.6
where the time goes:
time: 312 us; the launch traced here: 311 us
  blocking collectives  193 us (62%)
  Pallas kernels  87.8 us (28%)
  local copies, waits for them, and re-layouts  15.2 us (5%)
  between operations  14.2 us (5%)
    psum x1, blocking collectives, pair_body(): channel = lax.psum([grad.astype(F32) for grad in results[8:14]], 'wide')  104 us
    psum x1, blocking collectives, pair_body(): lax.psum(results[14:17], ('wide', 'narrow'))  89.5 us
    pallas_call x1, Pallas kernels, pair_body(): pl.pallas_call(whole_kernel, out_shape=(out((rows, 384)), out((rows, 384)...  87.8 us
  transfers between devices with their start and end apart: 1, of which 0 were waited for; matrix products, arithmetic and copies ran while one was open for 0% of the time, Pallas kernels for 0%

commit v1 on v0

--- a/solution.py
+++ b/solution.py
@@ -532,6 +532,31 @@
     ]
 
 
+STRIDES = (1, 2, 4, 8)
+ORDERS = ((0, 1, 2, 3), (0, 2, 3, 1))
+LOWER_RIGHT, LOWER_LEFT, GATE_RIGHT, LIFT_RIGHT, GATE_LEFT, LIFT_LEFT, CHANNEL_ROWS = (
+    0,
+    768,
+    960,
+    1152,
+    1344,
+    2112,
+    3072,
+)
+(
+    OUT_RIGHT,
+    OUT_LEFT,
+    SHAPE_RIGHT,
+    SHAPE_LEFT,
+    VALUE_RIGHT,
+    VALUE_LEFT,
+    FILTER_OUT,
+    VECTORS,
+    FILTER,
+    MIXER_ROWS,
+) = (0, 192, 576, 768, 960, 1152, 1344, 1472, 1488, 1536)
+
+
 def tile_rows(index, size=TILE):
     return pl.ds(pl.multiple_of(index * size, size), size)
 
@@ -560,21 +585,8 @@
     lowerleft,
     hidden_out,
     hidden_grad,
-    grad_valueright,
-    grad_valueleft,
-    grad_shaperight,
-    grad_shapeleft,
-    grad_outright,
-    grad_outleft,
-    grad_gateright,
-    grad_gateleft,
-    grad_liftright,
-    grad_liftleft,
-    grad_lowerright,
-    grad_lowerleft,
-    grad_filterout,
-    grad_vectors,
-    grad_filter,
+    sums_channel,
+    sums_mixer,
     w_first,
     w_value,
     w_shape,
@@ -594,10 +606,8 @@
     shaping,
     sig_pad,
     short,
-    lin_one,
     act_one,
     cos_one,
-    lin_two,
     act_two,
     cos_two,
     fil_spec,
@@ -629,14 +639,32 @@
     ds_pad,
     ds_halves,
     d_inner_one,
-    tail_own,
-    do_send,
-    do_recv,
+    cross_send,
+    mid_send,
+    mid_recv,
+    d_middle,
+    branch,
+    shape_send,
+    shape_recv,
+    value_send,
+    value_recv,
+    w_cross,
+    through,
     d_lin,
     own_out,
+    grad_vectors,
+    grad_filter,
+    gain_sums,
     send_sem,
     recv_sem,
     load_sem,
+    got_core,
+    got_one,
+    got_two,
+    got_three,
+    sum_send,
+    sum_recv,
+    sum_free,
 ):
     rows = inputs.shape[0]
     half = rows // 2
@@ -645,7 +673,8 @@
     spans = length // TILE
     wide = lax.axis_index("wide")
     narrow = lax.axis_index("narrow")
-    core = lax.rem(wide, 2)
+    bits = [lax.rem(wide // stride, 2) for stride in STRIDES]
+    core = bits[0]
     sibling = (wide + 1 - 2 * core, narrow)
     partner = (wide, 1 - narrow)
     quarter = 2 * narrow + core
@@ -653,9 +682,10 @@
     other_half = pl.ds(pl.multiple_of((1 - narrow) * 384, 384), 384)
 
     barrier = pltpu.get_barrier_semaphore()
-    for device in (sibling, partner):
+    others = [(wide + stride * (1 - 2 * bit), narrow) for stride, bit in zip(STRIDES, bits)]
+    for device in others + [partner]:
         pl.semaphore_signal(barrier, inc=1, device_id=device, device_id_type=MESH)
-    pl.semaphore_wait(barrier, 2)
+    pl.semaphore_wait(barrier, len(others) + 1)
 
     def send(source, target, device, index):
         return pltpu.make_async_remote_copy(
@@ -666,6 +696,80 @@
             device_id=device,
             device_id_type=MESH,
         )
+
+    received = (got_core, got_one, got_two, got_three)
+
+    def summing(slab, first_sem):
+        part = slab.shape[0] // 2
+        offsets = [[0], [part]]
+        for i in range(2):
+            for step in range(4):
+                move = bits[ORDERS[i][step]] * (part >> (step + 1))
+                offsets[i].append(pl.multiple_of(offsets[i][step] + move, 16))
+
+        def copy(source, target, i, step, back):
+            index = first_sem + 8 * back + 2 * step + i
+            return pltpu.make_async_remote_copy(
+                src_ref=source,
+                dst_ref=target,
+                send_sem=sum_send.at[index],
+                recv_sem=sum_recv.at[index],
+                device_id=others[ORDERS[i][step]],
+                device_id_type=MESH,
+            )
+
+        def scatter(i, step):
+            size = part >> (step + 1)
+            away = (1 - bits[ORDERS[i][step]]) * size
+            away = pl.multiple_of(offsets[i][step] + away, 16)
+            return copy(
+                slab.at[pl.ds(away, size)], received[step].at[pl.ds(i * size, size)], i, step, 0
+            )
+
+        def gather(i, step):
+            at = pl.ds(offsets[i][step + 1], part >> (step + 1))
+            return copy(slab.at[at], slab.at[at], i, step, 1)
+
+        def start(step):
+            for i in range(2):
+                scatter(i, step).start()
+
+        def add(step):
+            size = part >> (step + 1)
+            for i in range(2):
+                scatter(i, step).wait()
+
+                @pl.loop(0, size // 48)
+                def _(index):
+                    own = pl.ds(pl.multiple_of(offsets[i][step + 1] + index * 48, 16), 48)
+                    came = received[step][pl.ds(pl.multiple_of(i * size + index * 48, 16), 48), :]
+                    slab[own, :] = (slab[own, :].astype(F32) + came.astype(F32)).astype(BF16)
+
+            for i in range(2):
+                pl.semaphore_signal(
+                    sum_free.at[first_sem // 2 + 2 * step + i],
+                    inc=1,
+                    device_id=others[ORDERS[i][step]],
+                    device_id_type=MESH,
+                )
+
+        def clear(step):
+            for i in range(2):
+                pl.semaphore_wait(sum_free.at[first_sem // 2 + 2 * step + i], 1)
+
+        def back(step):
+            for i in range(2):
+                gather(i, step).start()
+
+        def take(step):
+            for i in range(2):
+                gather(i, step).wait()
+
+        return (start, add, clear, back, take, offsets)
+
+    mixer_slab = sums_mixer.at[narrow]
+    channel_start, channel_add, channel_clear, channel_back, channel_take, _ = summing(sums_channel, 0)
+    mixer_start, mixer_add, mixer_clear, mixer_back, mixer_take, mixer_offsets = summing(mixer_slab, 16)
 
     load_copies = []
     for source, target in ((gateleft, w_gate), (liftleft, w_lift)):
@@ -704,8 +808,20 @@
                 target[96 * b + 48 * k : 96 * b + 48 * k + 48, :] = wider[
                     48 * b : 48 * b + 48, :
                 ] * between(2 * PAD, PAD * k, PAD * k + PAD)
+    row = lax.broadcasted_iota(jnp.int32, (D, 192), 0)
+    lane = lax.broadcasted_iota(jnp.int32, (D, 192), 1)
+    start = (2 * narrow) * 192 + (1 - narrow) * 96
+    cross = mask(row == start + lane + jnp.where(lane >= 96, 96, 0))
+    for i, source in enumerate((valueright, shaperight)):
+        part = mm(source[...], cross).astype(BF16)
+        for b in range(2):
+            w_cross[i, 192 * b : 192 * b + 192, :] = part * between(192, 96 * b, 96 * b + 96)
     first = vectors[0:1, :]
     shift_first = vectors[1:2, :]
+
+    coarse = vectors[...].astype(BF16)
+    fine = (vectors[...] - coarse.astype(F32)).astype(BF16)
+    through[...] = mm(coarse, w_first[...]) + mm(fine, w_first[...])
 
     @pl.loop(0, tiles)
     def _(index):
@@ -757,12 +873,10 @@
         at = tile_rows(index)
         one = mm(place[at, :], filter_vectors[0:8, :], HIGHEST) + pos_bias
         sine, cosine = sine_cosine(frequency * one)
-        lin_one[at, :] = one
         act_one[at, :] = sine
         cos_one[at, :] = cosine
         two = mm(sine, midweight[...], HIGHEST) + mid_bias
         sine, cosine = sine_cosine(frequency * two)
-        lin_two[at, :] = two
         act_two[at, :] = sine
         cos_two[at, :] = cosine
         short[at, :] = (mm(sine, own_out[...], HIGHEST) * decay(index)).astype(BF16)
@@ -820,8 +934,8 @@
         at = tile_rows(index)
         real = mm(table_cos[at, :], short[...])
         imag = mm(table_sin[at, :], short[...])
-        sig_spec[0, at, :] = real
-        sig_spec[1, at, :] = imag
+        sig_spec[0, at, :] = real.astype(BF16)
+        sig_spec[1, at, :] = imag.astype(BF16)
         fil_re = fil_spec[0, at, :]
         fil_im = fil_spec[1, at, :]
         prod_spec[0, at, :] = (real * fil_re - imag * fil_im).astype(BF16)
@@ -846,20 +960,29 @@
         at = tile_rows(index)
         return send(inner_out.at[narrow, at], inner_out.at[narrow, at], partner, 3 + index)
 
-    def dn_copy(index):
-        at = tile_rows(index)
-        return send(dn_send.at[at], dn_recv.at[at], partner, 5 + index)
+    dn_copy = send(dn_send, dn_recv, partner, 5)
+    own_rows = tile_rows(narrow)
+    cross_copy = send(cross_send, d_inner_out.at[own_rows], partner, 6)
+    middle_copy = send(mid_send, mid_recv, partner, 11)
 
     def part_copy(index):
         at = tile_rows(index)
         return send(part_send.at[at], part_recv.at[at], partner, 7 + index)
 
-    def do_copy(index):
+    def shape_copy(index):
         at = tile_rows(index)
-        return send(do_send.at[at], do_recv.at[at], partner, 11 + index)
+        return send(shape_send.at[at], shape_recv.at[at], partner, 12 + index)
+
+    def value_copy(index):
+        at = tile_rows(index)
+        return send(value_send.at[at], value_recv.at[at], partner, 14 + index)
+
+    def first_other(index):
+        return 1 - narrow + index * (2 * narrow - 1)
 
     @pl.loop(0, tiles)
-    def _(index):
+    def _(order):
+        index = narrow + order * (1 - 2 * narrow)
         at = tile_rows(index)
         inner = None
         for k in range(2):
@@ -877,18 +1000,19 @@
     shift_second = vectors[3:4, :]
 
     @pl.loop(0, tiles)
-    def _(index):
+    def _(order):
+        index = first_other(order)
         at = tile_rows(index)
         inner_copy(index).wait_recv()
         mid = inputs[at, :].astype(F32)
         mid += mm(inner_out[0, at, :], w_out_second[0])
         mid += mm(inner_out[1, at, :], w_out_second[1])
-        dn_own[at, :] = mid
+        dn_own[...] = mid
         center = mid - jnp.mean(mid, axis=-1, keepdims=True)
         inverse = lax.rsqrt(jnp.mean(center * center, axis=-1, keepdims=True) + EPSILON)
         hat = center * inverse
-        hat_two[at, :] = hat
-        stats[at, 2:3] = inverse
+        hat_two[...] = hat
+        stats[0:TILE, 2:3] = inverse
         normed = (hat * gain_second + shift_second).astype(BF16)
         norm_two[at, :] = normed
         inner = mm(normed, w_glu[...]).astype(BF16)
@@ -909,7 +1033,7 @@
                 lower[k] = term if lower[k] is None else lower[k] + term
         inner_low = join(*lower).astype(BF16)
         inner_lower[at, :] = inner_low
-        out_own[at, :] = dn_own[at, own_half] + mm(inner_low, w_lower_second[:, own_half])
+        out_own[at, :] = dn_own[:, own_half] + mm(inner_low, w_lower_second[:, own_half])
         part_send[at, :] = mm(inner_low, w_lower_second[:, other_half]).astype(BF16)
 
         above = jnp.concatenate([up_halves[0, at, :], up_halves[1, at, :]], axis=1)
@@ -931,9 +1055,12 @@
         d_glu = jnp.concatenate([join(*gates), join(*lifts)], axis=1).astype(BF16)
         d_inner_glu[at, :] = d_glu
         into = mm_nt(d_glu, w_glu[...])
-        dn_own[at, :] = into
-        dn_send[at, :] = into.astype(BF16)
-        dn_copy(index).start()
+        dn_own[...] = into
+
+        @pl.when(order == 0)
+        def _():
+            dn_send[...] = dn_own[...].astype(BF16)
+            dn_copy.start()
 
     @pl.loop(0, tiles)
     def _(index):
@@ -943,28 +1070,31 @@
         columns = slice(384 * side, 384 * side + 384)
         folded = fold(mm_tn(inner_lower[...], up_halves[side]), side)
         for b in range(2):
-            grad_lowerleft[48 * b : 48 * b + 48, columns] = folded[b].astype(BF16)
+            first_row = LOWER_LEFT + 96 * side + 48 * b
+            sums_channel[first_row : first_row + 48, :] = folded[b].astype(BF16)
     low_lanes = lanes(128) < 64
     for columns in (slice(0, 384), slice(384, 768)):
+        columns_at = slice(LOWER_RIGHT + columns.start, LOWER_RIGHT + columns.stop)
         parts = [
             mm_tn(hid[k, :, columns], d_inner_lower[:, 128 * k : 128 * k + 256]) for k in range(2)
         ]
-        grad_lowerright[columns, 0:128] = parts[0][:, 0:128].astype(BF16)
-        grad_lowerright[columns, 128:256] = jnp.where(
+        sums_channel[columns_at, 0:128] = parts[0][:, 0:128].astype(BF16)
+        sums_channel[columns_at, 128:256] = jnp.where(
             low_lanes, parts[0][:, 128:256], parts[1][:, 0:128]
         ).astype(BF16)
-        grad_lowerright[columns, 256:384] = parts[1][:, 128:256].astype(BF16)
-    for offset, upper, target in ((0, d_gate, grad_gateleft), (384, d_lift, grad_liftleft)):
+        sums_channel[columns_at, 256:384] = parts[1][:, 128:256].astype(BF16)
+    for offset, upper, target in ((0, d_gate, GATE_LEFT), (384, d_lift, LIFT_LEFT)):
         for k in range(2):
             for start in (0, 384):
                 whole = mm_tn(
                     inner_glu[:, offset + 128 * k : offset + 128 * k + 256],
                     upper[k, :, start : start + 384],
                 )
-                target[:, D * k + start : D * k + start + 384] = whole[
+                first_row = target + 384 * k + start // 2
+                sums_channel[first_row : first_row + 192, :] = whole[
                     64 * k : 64 * k + 192, :
                 ].astype(BF16)
-    for offset, target in ((0, grad_gateright), (384, grad_liftright)):
+    for offset, target in ((0, GATE_RIGHT), (384, LIFT_RIGHT)):
         whole = mm_tn(norm_two[...], d_inner_glu[:, offset : offset + 384])
         total = None
         for b in range(4):
@@ -972,30 +1102,41 @@
                 (inside >= 48 * b) & (inside < 48 * b + 48), F32
             )
             total = term if total is None else total + term
-        target[...] = total.astype(BF16)
-
-    half_mask = mask((lanes(D) >= narrow * 384) & (lanes(D) < narrow * 384 + 384), F32)
-    grad_vectors[...] = jnp.zeros(grad_vectors.shape, F32)
+        sums_channel[target : target + 192, :] = total.astype(BF16)
+
+    sums_channel[2880:3072, :] = jnp.zeros((192, 384), BF16)
+    channel_start(0)
+
+    dn_copy.wait_recv()
+    into = dn_own[...] + dn_recv[...].astype(F32)
+    hat = hat_two[...]
+    gain_sums[0:1, :] = jnp.sum(into * hat, axis=0, keepdims=True)
+    gain_sums[1:2, :] = jnp.sum(into, axis=0, keepdims=True)
+    scaled = into * gain_second
+    above = jnp.concatenate([up_halves[0, own_rows, :], up_halves[1, own_rows, :]], axis=1)
+    d_mid = above.astype(F32) + stats[0:TILE, 2:3] * (
+        scaled
+        - jnp.mean(scaled, axis=-1, keepdims=True)
+        - hat * jnp.mean(scaled * hat, axis=-1, keepdims=True)
+    )
+    hat_two[...] = d_mid
+    branch[...] = d_mid.astype(BF16)
+    cross_send[...] = mm_nt(branch[...], w_out_second[1 - narrow]).astype(BF16)
+    cross_copy.start()
+    mid_send[...] = hat_two[:, other_half].astype(BF16)
+    middle_copy.start()
+    d_inner_out[own_rows, :] = mm_nt(branch[...], w_out_second[narrow]).astype(BF16)
 
     @pl.loop(0, tiles)
-    def _(index):
+    def _(order):
+        index = narrow + order * (1 - 2 * narrow)
         at = tile_rows(index)
-        dn_copy(index).wait_recv()
-        into = dn_own[at, :] + dn_recv[at, :].astype(F32)
-        hat = hat_two[at, :]
-        grad_vectors[2:3, :] += jnp.sum(into * hat, axis=0, keepdims=True) * half_mask
-        grad_vectors[3:4, :] += jnp.sum(into, axis=0, keepdims=True) * half_mask
-        scaled = into * gain_second
-        above = jnp.concatenate([up_halves[0, at, :], up_halves[1, at, :]], axis=1)
-        d_mid = above.astype(F32) + stats[at, 2:3] * (
-            scaled
-            - jnp.mean(scaled, axis=-1, keepdims=True)
-            - hat * jnp.mean(scaled * hat, axis=-1, keepdims=True)
-        )
-        hat_two[at, :] = d_mid
-        branch = d_mid.astype(BF16)
-        d_inner = mm_nt(branch, w_out_second[narrow]).astype(BF16)
-        d_inner_out[at, :] = d_inner
+
+        @pl.when(order == 1)
+        def _():
+            cross_copy.wait_recv()
+
+        d_inner = d_inner_out[at, :]
         for k in range(2):
             d_mixed = mm_nt(d_inner, w_out_first[k * PAD : k * PAD + PAD, :])
             d_shaping[k, at, :] = (d_mixed * long_halves[k, at, :].astype(F32)).astype(BF16)
@@ -1005,22 +1146,33 @@
     dl_copy.start()
     dl_rows[core] = sig_halves[core]
 
-    for side in range(2):
-        columns = slice(384 * side, 384 * side + 384)
-        folded = fold(mm_tn(inner_out[narrow], hat_two[:, columns].astype(BF16)), side)
-        for b in range(2):
-            at = pl.ds(pl.multiple_of(narrow * 96 + 48 * b, 16), 48)
-            grad_outleft[at, columns] = folded[b].astype(BF16)
-            at = pl.ds(pl.multiple_of((1 - narrow) * 96 + 48 * b, 16), 48)
-            grad_outleft[at, columns] = jnp.zeros((48, 384), BF16)
+    @pl.loop(0, tiles)
+    def _(index):
+        at = tile_rows(index)
+        to_shape = jnp.concatenate([d_shaping[0, at, :], d_shaping[1, at, :]], axis=1)
+        d_inner_one[at, 384:768] = mm_nt(to_shape, w_shape[...]).astype(BF16)
+        shape_send[at, :] = mm_nt(
+            to_shape, w_shape[pl.ds(pl.multiple_of((1 - narrow) * 192, 192), 192), :]
+        ).astype(BF16)
+        shape_copy(index).start()
+
+
+    channel_add(0)
+    channel_start(1)
+    for h in range(2):
+        for side in range(2):
+            columns = slice(384 * side, 384 * side + 384)
+            folded = fold(mm_tn(inner_out[h, own_rows, :], branch[:, columns]), side)
+            for b in range(2):
+                first_row = OUT_LEFT + 192 * h + 96 * side + 48 * b
+                mixer_slab[first_row : first_row + 48, :] = folded[b].astype(BF16)
     parts = []
     for k in range(2):
         product = (shaping[k] * long_halves[k].astype(F32)).astype(BF16)
         parts.append(mm_tn(product, d_inner_out[...]))
-    grad_outright[:, own_half] = jnp.where(
+    mixer_slab[OUT_RIGHT : OUT_RIGHT + 192, :] = jnp.where(
         lanes(384) < 192, parts[0][0:192, :], parts[1][0:192, :]
     ).astype(BF16)
-    grad_outright[:, other_half] = jnp.zeros((192, 384), BF16)
 
     dl_copy.wait_recv()
 
@@ -1034,10 +1186,14 @@
         fil_im = fil_spec[1, at, :]
         prod_spec[0, at, :] = (real * fil_re + imag * fil_im).astype(BF16)
         prod_spec[1, at, :] = (imag * fil_re - real * fil_im).astype(BF16)
-        sig_re = sig_spec[0, at, :]
-        sig_im = sig_spec[1, at, :]
-        sig_spec[0, at, :] = real * sig_re + imag * sig_im
-        sig_spec[1, at, :] = imag * sig_re - real * sig_im
+        sig_re = sig_spec[0, at, :].astype(F32)
+        sig_im = sig_spec[1, at, :].astype(F32)
+        turn_cos = place[at, 5:6] * (1.0 / length)
+        turn_sin = place[at, 6:7] * (1.0 / length)
+        both_re = real * sig_re + imag * sig_im
+        both_im = imag * sig_re - real * sig_im
+        sig_spec[0, at, :] = (both_re * turn_cos - both_im * turn_sin).astype(BF16)
+        sig_spec[1, at, :] = (both_im * turn_cos + both_re * turn_sin).astype(BF16)
 
     ds_pad[length : length + 8, :] = jnp.zeros((8, PAD), F32)
 
@@ -1058,6 +1214,9 @@
     ds_copy.start()
     ds_halves[core] = long_rows[core]
 
+    channel_add(1)
+    channel_start(2)
+    grad_vectors[...] = jnp.zeros(grad_vectors.shape, F32)
     sums = [jnp.zeros((1, PAD), F32) for _ in range(3)]
     for index in range(spans):
         start = index * TILE
@@ -1067,29 +1226,19 @@
                 upper * sig_pad[8 + start - j : 8 + start - j + TILE, :], axis=0, keepdims=True
             )
     sums = jnp.concatenate(sums + [jnp.zeros((5, PAD), F32)], axis=0)
-    lane = lax.broadcasted_iota(jnp.int32, (PAD, D), 1)
-    row = lax.broadcasted_iota(jnp.int32, (PAD, D), 0)
-    unpick = mask((lane == quarter * 192 + row) & (row < 192), F32)
-    conv_sums = mm(sums, unpick, HIGHEST)
+    lane = lax.broadcasted_iota(jnp.int32, (PAD, 384), 1)
+    row = lax.broadcasted_iota(jnp.int32, (PAD, 384), 0)
+    place_core = mask((lane == core * 192 + row) & (row < 192))
+    conv_sums = mm(sums.astype(BF16), place_core)
     grad_vectors[4:7, :] = conv_sums[0:3, :]
+
+    d_lin[...] = jnp.zeros(d_lin.shape, F32)
+    grad_filter[...] = jnp.zeros(grad_filter.shape, F32)
 
     @pl.loop(0, spans)
     def _(index):
         at = tile_rows(index)
-        turn_cos = place[at, 5:6] * (1.0 / length)
-        turn_sin = place[at, 6:7] * (1.0 / length)
-        real = sig_spec[0, at, :]
-        imag = sig_spec[1, at, :]
-        prod_spec[0, at, :] = (real * turn_cos - imag * turn_sin).astype(BF16)
-        prod_spec[1, at, :] = (imag * turn_cos + real * turn_sin).astype(BF16)
-
-    d_lin[...] = jnp.zeros(d_lin.shape, F32)
-    grad_filter[...] = jnp.zeros(grad_filter.shape, F32)
-
-    @pl.loop(0, spans)
-    def _(index):
-        at = tile_rows(index)
-        d_taps = mm(table_cos[at, :], prod_spec[0]) + mm(table_sin[at, :], prod_spec[1])
+        d_taps = mm(table_cos[at, :], sig_spec[0]) + mm(table_sin[at, :], sig_spec[1])
         d_mod = d_taps * decay(index)
         d_lin[...] += mm_tn(act_two[at, :], d_mod, HIGHEST)
         two = mm_nt(d_mod, own_out[...], HIGHEST) * cos_two[at, :]
@@ -1100,40 +1249,45 @@
         grad_filter[128:136, :] += mm_tn(place[at, :], scaled_one, HIGHEST)
         grad_filter[136:137, :] += jnp.sum(scaled_one, axis=0, keepdims=True)
         grad_filter[137:138, :] += jnp.sum(scaled_two, axis=0, keepdims=True)
-        grad_filter[138:139, :] += jnp.sum(one * lin_one[at, :] + two * lin_two[at, :], axis=0, keepdims=True)
-
-    grad_filterout[...] = mm(d_lin[...], unpick, HIGHEST)
+        lin_one = mm(place[at, :], filter_vectors[0:8, :], HIGHEST) + pos_bias
+        lin_two = mm(act_one[at, :], midweight[...], HIGHEST) + mid_bias
+        grad_filter[138:139, :] += jnp.sum(one * lin_one + two * lin_two, axis=0, keepdims=True)
+
+    mixer_slab[FILTER_OUT : FILTER_OUT + 128, :] = mm(d_lin[...].astype(BF16), place_core).astype(BF16)
+    for i in range(3):
+        mixer_slab[FILTER : FILTER + 48, 128 * i : 128 * i + 128] = grad_filter[48 * i : 48 * i + 48, :].astype(BF16)
+
+    channel_add(2)
+    channel_start(3)
 
     ds_copy.wait_recv()
-    first_half = vectors[0:1, own_half]
-    tail_lane = lax.broadcasted_iota(jnp.int32, (TILE, 128), 1)
+    other_blocks = pl.ds(pl.multiple_of((1 - narrow) * 192, 192), 192)
 
     @pl.loop(0, tiles)
     def _(index):
         at = tile_rows(index)
         to_value = jnp.concatenate([ds_halves[0, at, :], ds_halves[1, at, :]], axis=1)
-        to_shape = jnp.concatenate([d_shaping[0, at, :], d_shaping[1, at, :]], axis=1)
-        d_inner = jnp.concatenate(
-            [mm_nt(to_value, w_value[...]), mm_nt(to_shape, w_shape[...])], axis=1
-        ).astype(BF16)
-        d_inner_one[at, :] = d_inner
-        into = mm_nt(d_inner, w_first[...])
-        dn_own[at, :] = into
-        scaled = into * first
-        plain = jnp.sum(scaled, axis=-1, keepdims=True)
-        hat = (inputs[at, :].astype(F32) - stats[at, 0:1]) * stats[at, 1:2]
-        along = jnp.sum(scaled * hat, axis=-1, keepdims=True)
-        tail = jnp.where(tail_lane == 0, plain, jnp.where(tail_lane == 1, along, 0.0))
-        tail_own[at, :] = tail
-        do_send[at, 0:384] = dn_own[at, other_half].astype(BF16)
-        do_send[at, 384:512] = tail.astype(BF16)
-        do_copy(index).start()
-
-    lane = lax.broadcasted_iota(jnp.int32, (384, D), 1)
-    row = lax.broadcasted_iota(jnp.int32, (384, D), 0)
-    step = jnp.where(row >= 96, 96, 0) + jnp.where(row >= 192, 96, 0) + jnp.where(row >= 288, 96, 0)
-    unselect = mask(lane == row + step + narrow * 96)
-    for offset, target in ((0, grad_valueright), (384, grad_shaperight)):
+        d_inner = mm_nt(to_value, w_value[...]).astype(BF16)
+        d_inner_one[at, 0:384] = d_inner
+        against = inner_one[at, :].astype(F32) - through[1:2, :]
+        d_inner = d_inner_one[at, :].astype(F32)
+        plain = jnp.sum(d_inner * through[0:1, :], axis=-1, keepdims=True)
+        along = jnp.sum(d_inner * against, axis=-1, keepdims=True)
+        stats[at, 2:3] = plain
+        stats[at, 3:4] = along
+        lane = lanes(128)
+        tail = jnp.where(lane == 64, plain, jnp.where(lane == 65, along, 0.0))
+        away = mm_nt(to_value, w_value[other_blocks, :])
+        value_send[at, 0:128] = away[:, 0:128].astype(BF16)
+        value_send[at, 128:192] = away[:, 128:192].astype(BF16)
+        value_send[at, 192:256] = tail[:, 64:128].astype(BF16)
+        value_copy(index).start()
+
+    channel_add(3)
+    for step in range(4):
+        channel_clear(step)
+    channel_back(3)
+    for offset, target in ((0, VALUE_RIGHT), (384, SHAPE_RIGHT)):
         whole = mm_tn(norm_one[...], d_inner_one[:, offset : offset + 384])
         total = None
         for b in range(4):
@@ -1141,13 +1295,11 @@
                 384, 96 * b, 96 * b + 96, F32
             )
             total = term if total is None else total + term
-        target[...] = mm(total.astype(BF16), unselect).astype(BF16)
-    lane = lax.broadcasted_iota(jnp.int32, (2 * PAD, D), 1)
-    row = lax.broadcasted_iota(jnp.int32, (2 * PAD, D), 0)
-    group = jnp.where(row >= PAD, 1, 0)
-    entry = row - PAD * group
-    unspread = mask((lane == (2 * narrow + group) * 192 + entry) & (entry < 192))
-    for offset, upper, target in ((0, ds_halves, grad_valueleft), (384, d_shaping, grad_shapeleft)):
+        mixer_slab[target : target + 192, :] = total.astype(BF16)
+    lane = lax.broadcasted_iota(jnp.int32, (2 * PAD, 384), 1)
+    row = lax.broadcasted_iota(jnp.int32, (2 * PAD, 384), 0)
+    squeeze = mask(row == lane + jnp.where(lane >= 192, 64, 0))
+    for offset, upper, target in ((0, ds_halves, VALUE_LEFT), (384, d_shaping, SHAPE_LEFT)):
         above = jnp.concatenate([upper[0], upper[1]], axis=1)
         whole = mm_tn(inner_one[:, offset : offset + 384], above)
         pieces = []
@@ -1160,32 +1312,169 @@
                 total = term if total is None else total + term
             pieces.append(total)
         total = jnp.concatenate(pieces, axis=0).astype(BF16)
-        target[...] = mm(total, unspread).astype(BF16)
-
+        mixer_slab[target : target + 192, :] = mm(total, squeeze).astype(BF16)
+
+    channel_take(3)
+    channel_back(2)
+
+    first_half = vectors[0:1, own_half]
+    middle_copy.wait_recv()
+    d_middle[own_rows, :] = hat_two[:, own_half]
+    d_middle[tile_rows(1 - narrow), :] = mid_recv[...].astype(F32)
     @pl.loop(0, tiles)
     def _(index):
         at = tile_rows(index)
         part_copy(index).wait_recv()
         hidden_out[at, :] = (out_own[at, :] + part_recv[at, :].astype(F32)).astype(BF16)
-        do_copy(index).wait_recv()
-        came = do_recv[at, :].astype(F32)
-        into = dn_own[at, own_half] + came[:, 0:384]
-        tail = (tail_own[at, :] + came[:, 384:512]) * (1.0 / D)
+        shape_copy(index).wait_recv()
+        value_copy(index).wait_recv()
+        into = mm_nt(d_inner_one[at, :], w_first[own_half, :])
+        into += mm_nt(value_recv[at, 0:192], w_cross[0])
+        into += mm_nt(shape_recv[at, :], w_cross[1])
+        plain = (stats[at, 2:3] + value_recv[at, 192:193].astype(F32)) * (1.0 / D)
+        along = (stats[at, 3:4] + value_recv[at, 193:194].astype(F32)) * (1.0 / D)
         hat = (inputs[at, own_half].astype(F32) - stats[at, 0:1]) * stats[at, 1:2]
-        grad_vectors[0:1, own_half] += jnp.sum(into * hat, axis=0, keepdims=True)
-        grad_vectors[1:2, own_half] += jnp.sum(into, axis=0, keepdims=True)
+        grad_vectors[0:1, :] += jnp.sum(into * hat, axis=0, keepdims=True)
+        grad_vectors[1:2, :] += jnp.sum(into, axis=0, keepdims=True)
         hidden_grad[at, :] = (
-            hat_two[at, own_half]
-            + stats[at, 1:2] * (into * first_half - tail[:, 0:1] - hat * tail[:, 1:2])
+            d_middle[at, :] + stats[at, 1:2] * (into * first_half - plain - hat * along)
         ).astype(BF16)
 
-    for copy in (up_copy, dl_copy, ds_copy):
+    grad_vectors[2:4, :] = gain_sums[0:2, 0:384]
+    grad_vectors[8:10, :] = gain_sums[0:2, 384:768]
+    mixer_slab[VECTORS : VECTORS + 16, :] = grad_vectors[...].astype(BF16)
+    mixer_start(0)
+    channel_take(2)
+    channel_back(1)
+    mixer_add(0)
+    for step in range(1, 4):
+        mixer_start(step)
+        mixer_add(step)
+    for step in range(4):
+        mixer_clear(step)
+    mixer_back(3)
+    channel_take(1)
+    channel_back(0)
+    for step in (3, 2, 1):
+        mixer_take(step)
+        if step > 1:
+            mixer_back(step - 1)
+    size = MIXER_ROWS // 4
+    across = []
+    for i in range(2):
+        at = pl.ds(mixer_offsets[i][1], size)
+        across.append(
+            pltpu.make_async_remote_copy(
+                src_ref=mixer_slab.at[at],
+                dst_ref=mixer_slab.at[at],
+                send_sem=sum_send.at[32 + i],
+                recv_sem=sum_recv.at[32 + i],
+                device_id=partner,
+                device_id_type=MESH,
+            )
+        )
+        across[i].start()
+    mixer_back(0)
+    for i in range(2):
+        across[i].wait()
+        at = pl.ds(mixer_offsets[i][1], size)
+        across.append(
+            pltpu.make_async_remote_copy(
+                src_ref=sums_mixer.at[1 - narrow, at],
+                dst_ref=sums_mixer.at[1 - narrow, at],
+                send_sem=sum_send.at[34 + i],
+                recv_sem=sum_recv.at[34 + i],
+                device_id=sibling,
+                device_id_type=MESH,
+            )
+        )
+        across[2 + i].start()
+    for i in range(2):
+        across[2 + i].wait()
+    mixer_take(0)
+    channel_take(0)
+
+    for copy in (up_copy, dl_copy, ds_copy, dn_copy, cross_copy, middle_copy):
         copy.wait_send()
 
     @pl.loop(0, tiles)
     def _(index):
-        for copy in (inner_copy, dn_copy, part_copy, do_copy):
+        for copy in (inner_copy, part_copy, shape_copy, value_copy):
             copy(index).wait_send()
+
+
+def finish_kernel(
+    sums_channel,
+    sums_mixer,
+    grad_vectors,
+    grad_valueright,
+    grad_valueleft,
+    grad_shaperight,
+    grad_shapeleft,
+    grad_filter,
+    grad_filterout,
+    grad_outright,
+    grad_outleft,
+    grad_gateright,
+    grad_gateleft,
+    grad_liftright,
+    grad_liftleft,
+    grad_lowerright,
+    grad_lowerleft,
+):
+    grad_lowerright[...] = sums_channel[LOWER_RIGHT : LOWER_RIGHT + D, :].astype(F32)
+    grad_gateright[...] = sums_channel[GATE_RIGHT : GATE_RIGHT + 192, :].astype(F32)
+    grad_liftright[...] = sums_channel[LIFT_RIGHT : LIFT_RIGHT + 192, :].astype(F32)
+    for i in range(4):
+        columns = slice(384 * i, 384 * i + 384)
+        first_row = GATE_LEFT + 192 * i
+        grad_gateleft[:, columns] = sums_channel[first_row : first_row + 192, :].astype(F32)
+        first_row = LIFT_LEFT + 192 * i
+        grad_liftleft[:, columns] = sums_channel[first_row : first_row + 192, :].astype(F32)
+    lane = lax.broadcasted_iota(jnp.int32, (384, D), 1)
+    row = lax.broadcasted_iota(jnp.int32, (384, D), 0)
+    step = jnp.where(row >= 96, 96, 0) + jnp.where(row >= 192, 96, 0) + jnp.where(row >= 288, 96, 0)
+    unselect = [mask(lane == row + step + 96 * h) for h in range(2)]
+    for first_row, target in ((VALUE_RIGHT, grad_valueright), (SHAPE_RIGHT, grad_shaperight)):
+        target[...] = mm(sums_mixer[0, first_row : first_row + 192, :], unselect[0]) + mm(
+            sums_mixer[1, first_row : first_row + 192, :], unselect[1]
+        )
+    for h in range(2):
+        columns = slice(384 * h, 384 * h + 384)
+        grad_lowerleft[:, columns] = sums_channel[
+            LOWER_LEFT + 96 * h : LOWER_LEFT + 96 * h + 96, :
+        ].astype(F32)
+        for first_row, target in (
+            (OUT_RIGHT, grad_outright),
+            (SHAPE_LEFT, grad_shapeleft),
+            (VALUE_LEFT, grad_valueleft),
+        ):
+            target[:, columns] = sums_mixer[h, first_row : first_row + 192, :].astype(F32)
+        for side in range(2):
+            at = slice(OUT_LEFT + 192 * h + 96 * side, OUT_LEFT + 192 * h + 96 * side + 96)
+            grad_outleft[96 * h : 96 * h + 96, 384 * side : 384 * side + 384] = sums_mixer[
+                0, at, :
+            ].astype(F32) + sums_mixer[1, at, :].astype(F32)
+        own = sums_mixer[h, VECTORS : VECTORS + 16, :].astype(F32)
+        both = own + sums_mixer[1 - h, VECTORS : VECTORS + 16, :].astype(F32)
+        grad_vectors[0:2, columns] = own[0:2, :]
+        grad_vectors[2:4, columns] = both[2 + 6 * h : 4 + 6 * h, :]
+        grad_vectors[4:7, columns] = own[4:7, :]
+    for i in range(3):
+        columns = slice(128 * i, 128 * i + 128)
+        grad_filter[48 * i : 48 * i + 48, :] = sums_mixer[
+            0, FILTER : FILTER + 48, columns
+        ].astype(F32) + sums_mixer[1, FILTER : FILTER + 48, columns].astype(F32)
+    count = grad_filterout.shape[1]
+    first = (lax.axis_index("wide") * 2 + lax.axis_index("narrow")) * count
+    total = jnp.zeros(grad_filterout.shape, F32)
+    row = lax.broadcasted_iota(jnp.int32, (384, count), 0)
+    lane = lax.broadcasted_iota(jnp.int32, (384, count), 1)
+    for h in range(2):
+        total += mm(
+            sums_mixer[h, FILTER_OUT : FILTER_OUT + 128, :], mask(row + 384 * h == first + lane)
+        )
+    grad_filterout[...] = total
 
 
 def transform_tables(length):
@@ -1261,24 +1550,11 @@
         out_shape=(
             out((rows, 384)),
             out((rows, 384)),
-            out((192, D)),
-            out((192, D)),
-            out((192, D)),
-            out((192, D)),
-            out((192, D)),
-            out((192, D)),
-            out(gateright.shape),
-            out(gateleft.shape),
-            out(liftright.shape),
-            out(liftleft.shape),
-            out(lowerright.shape),
-            out(lowerleft.shape),
-            out((128, D), F32),
-            out((8, D), F32),
-            out((144, 128), F32),
+            out((CHANNEL_ROWS, 384)),
+            out((2, MIXER_ROWS, 384)),
         ),
         in_specs=[vmem] * 16 + [hbm, vmem, hbm, vmem, vmem],
-        out_specs=[vmem] * 17,
+        out_specs=[vmem] * 4,
         scratch_shapes=[
             buf(D, D),
             buf(384, 512),
@@ -1303,15 +1579,13 @@
             buf(length, 128, dtype=F32),
             buf(length, 128, dtype=F32),
             buf(length, 128, dtype=F32),
-            buf(length, 128, dtype=F32),
-            buf(length, 128, dtype=F32),
             buf(2, length, PAD, dtype=F32),
-            buf(2, length, PAD, dtype=F32),
+            buf(2, length, PAD),
             buf(2, length, PAD),
             buf(2, rows, PAD),
             buf(2, rows, PAD),
             buf(2, rows, 384),
-            buf(rows, D, dtype=F32),
+            buf(TILE, D, dtype=F32),
             buf(rows, D),
             buf(rows, D),
             buf(2, TILE, D, dtype=F32),
@@ -1325,23 +1599,41 @@
             buf(2, rows, D),
             buf(2, rows, D),
             buf(rows, D),
-            buf(rows, D, dtype=F32),
-            buf(rows, D),
-            buf(rows, D),
+            buf(TILE, D, dtype=F32),
+            buf(TILE, D),
+            buf(TILE, D),
             buf(rows, 384),
             buf(2, rows, PAD),
             buf(2, rows, PAD),
             buf(length + 8, PAD, dtype=F32),
             buf(2, rows, PAD),
             buf(rows, D),
-            buf(rows, 128, dtype=F32),
-            buf(rows, 512),
-            buf(rows, 512),
+            buf(TILE, 384),
+            buf(TILE, 384),
+            buf(TILE, 384),
+            buf(rows, 384, dtype=F32),
+            buf(TILE, D),
+            buf(rows, 192),
+            buf(rows, 192),
+            buf(rows, 256),
+            buf(rows, 256),
+            buf(2, 384, 192),
+            buf(8, D, dtype=F32),
             buf(128, PAD, dtype=F32),
             buf(128, PAD, dtype=F32),
-            pltpu.SemaphoreType.DMA((13,)),
-            pltpu.SemaphoreType.DMA((13,)),
+            buf(16, 384, dtype=F32),
+            buf(144, 128, dtype=F32),
+            buf(8, D, dtype=F32),
+            pltpu.SemaphoreType.DMA((16,)),
+            pltpu.SemaphoreType.DMA((16,)),
             pltpu.SemaphoreType.DMA((4,)),
+            buf(CHANNEL_ROWS // 2, 384),
+            buf(CHANNEL_ROWS // 4, 384),
+            buf(CHANNEL_ROWS // 8, 384),
+            buf(CHANNEL_ROWS // 16, 384),
+            pltpu.SemaphoreType.DMA((36,)),
+            pltpu.SemaphoreType.DMA((36,)),
+            pltpu.SemaphoreType.REGULAR((16,)),
         ],
         compiler_params=pltpu.CompilerParams(
             collective_id=0, has_side_effects=True, vmem_limit_bytes=63 * 1024 * 1024
@@ -1369,34 +1661,49 @@
         lowerright,
         lowerleft,
     )
-    hidden_out, hidden_grad = results[:2]
-    mixer = lax.psum([grad.astype(F32) for grad in results[2:8]], ("wide", "narrow"))
-    channel = lax.psum([grad.astype(F32) for grad in results[8:14]], "wide")
-    grad_filterout, grad_vectors, grad_filter = lax.psum(results[14:17], ("wide", "narrow"))
+    hidden_out, hidden_grad, sums_channel, sums_mixer = results
     count = D // (lax.axis_size("wide") * lax.axis_size("narrow"))
-    combined = lax.axis_index("wide") * lax.axis_size("narrow") + lax.axis_index("narrow")
-    grad_filterout = lax.dynamic_slice_in_dim(grad_filterout, combined * count, count, 1)
+    grads = pl.pallas_call(
+        finish_kernel,
+        out_shape=(
+            out((8, D), F32),
+            out((192, D), F32),
+            out((192, D), F32),
+            out((192, D), F32),
+            out((192, D), F32),
+            out((144, 128), F32),
+            out((128, count), F32),
+            out((192, D), F32),
+            out((192, D), F32),
+            out(gateright.shape, F32),
+            out(gateleft.shape, F32),
+            out(liftright.shape, F32),
+            out(liftleft.shape, F32),
+            out(lowerright.shape, F32),
+            out(lowerleft.shape, F32),
+        ),
+        in_specs=[vmem] * 2,
+        out_specs=[vmem] * 15,
+        compiler_params=pltpu.CompilerParams(vmem_limit_bytes=32 * 1024 * 1024),
+    )(sums_channel, sums_mixer)
+    grad_vectors, grad_filter = grads[0], grads[5]
     return (
         hidden_out,
         hidden_grad,
         grad_vectors[0],
         grad_vectors[1],
-        mixer[0],
-        mixer[1],
-        mixer[2],
-        mixer[3],
+        *grads[1:5],
         grad_vectors[4:7],
         grad_filter[128:133],
         grad_filter[136],
         grad_filter[138],
         grad_filter[:128],
         grad_filter[137],
-        grad_filterout,
-        mixer[4],
-        mixer[5],
+        grads[6],
+        *grads[7:9],
         grad_vectors[2],
         grad_vectors[3],
-        *channel,
+        *grads[9:],
     )
 
 

time: 312 us -> 165 us (0.53)
  blocking collectives: 193 us -> 0 us
  Pallas kernels: 87.8 us -> 149 us
  between operations: 14.2 us -> 0.7 us
    psum x2 -> x0, blocking collectives: 193 us -> none  [the longest x1 104 us: pair_body(): channel = lax.psum([grad.astype(F32) for grad in results[8:14]], 'wide')]
    pallas_call x1, Pallas kernels: 87.8 us -> 145 us  [pair_body(): pl.pallas_call(whole_kernel, out_shape=(out((rows, 384)), out((rows, 384)...]
    pallas_call x0 -> x1, Pallas kernels: none -> 3.88 us  [pair_body(): pl.pallas_call(finish_kernel, out_shape=(out((8, D), F32), out((192, D),...]
    unnamed x19 -> x11, local copies, waits for them, and re-layouts: 2.21 us -> 5.49 us
  transfers between devices with their start and end apart: 1 -> 0, of which waited for: 0 -> 0; matrix products, arithmetic and copies ran while one was open for 0% -> 0% of each run, Pallas kernels for 0% -> 0%
where the time goes in v1:
time: 165 us
  Pallas kernels  149 us (90%)
  local copies, waits for them, and re-layouts  15.2 us (9%)
    pallas_call x1, Pallas kernels, pair_body(): pl.pallas_call(whole_kernel, out_shape=(out((rows, 384)), out((rows, 384)...  145 us
    unnamed x11, local copies, waits for them, and re-layouts  5.49 us
    pallas_call x1, Pallas kernels, pair_body(): pl.pallas_call(finish_kernel, out_shape=(out((8, D), F32), out((192, D),...  3.88 us

profile of v1, /device:TPU:0, one launch (start us, length us, event | category | flops | bytes accessed | tf_op | source)
XLA Modules:
  0.0 164.8 jit_solution(9828257526745442869)
XLA Ops:
  0.7 0.7 stack.21
  1.4 0.7 stack.22
  2.0 0.7 stack.23
  2.7 0.7 stack.24
  3.4 2.6 %concatenate.7.filter_vectors = f32[16,128]{1,0:T(8,128)} concatenate(f32[5,128]{1,0:T(8,128)} %param.36, f32[3,128]{1,0:T(4,128)S(1)} %broadcast_in_dim.10, f32[1,128]{1,0:T(1,128)} %bitcast.9, f32[1,128]{1,0:T(1,128)} %bitcast.10, f32[1,128]{1,0:T(1,128)} %bitcast.11, f32[5,128]{1,0:T(8,128)S(1)} %broadcast_in_dim.11), dimensions={0} | concatenate | bytes 16384 | tf_op jit(solution)/shard_map/concatenate | solution.py:1536
  6.0 1.3 concatenate.6.vectors
  7.4 145.0 %shard_map.459 = (bf16[512,384]{1,0:T(8,128)(2,1)}, bf16[512,384]{1,0:T(8,128)(2,1)}, bf16[3072,384]{1,0:T(8,128)(2,1)}, bf16[2,1536,384]{2,1,0:T(8,128)(2,1)}) custom-call(bf16[512,768]{1,0:T(8,128)(2,1)} %inputs.1, bf16[512,384]{1,0:T(8,128)(2,1)} %upstream.1, bf16[1024,1024]{1,0:T(8,128)(2,1)} %constant.5.clone.table_cos, ...), custom_call_target="tpu_custom_call" | custom-call | tf_op jit(solution)/shard_map/pallas_call | solution.py:1548
  152.4 0.0 copy-start
  152.4 1.7 %copy-done = bf16[3072,384]{1,0:T(8,128)(2,1)S(1)} copy-done((bf16[3072,384]{1,0:T(8,128)(2,1)S(1)}, bf16[3072,384]{1,0:T(8,128)(2,1)}, u32[]{:S(2)}) %copy-start) | copy-done | bytes 2359320
  154.1 0.0 copy-start.1
  154.1 1.7 %copy-done.1 = bf16[2,1536,384]{2,1,0:T(8,128)(2,1)S(1)} copy-done((bf16[2,1536,384]{2,1,0:T(8,128)(2,1)S(1)}, bf16[2,1536,384]{2,1,0:T(8,128)(2,1)}, u32[]{:S(2)}) %copy-start.1) | copy-done | bytes 2359320
  155.7 0.0 copy-start.3
  155.7 0.0 copy-start.2
  155.7 3.9 %shard_map.460 = (f32[8,768]{1,0:T(8,128)S(1)}, f32[192,768]{1,0:T(8,128)}, f32[192,768]{1,0:T(8,128)}, f32[192,768]{1,0:T(8,128)}, f32[192,768]{1,0:T(8,128)}, ...) custom-call(bf16[3072,384]{1,0:T(8,128)(2,1)S(1)} %copy-done, ...), custom_call_target="tpu_custom_call" | custom-call | tf_op jit(solution)/shard_map/pallas_call | solution.py:1666
  159.6 0.5 slice_bitcast_fusion
  160.1 0.6 slice.33
  160.7 0.6 slice.36
  161.4 0.7 copy.53
  162.0 0.6 slice.32
  162.6 0.6 slice_reduce_fusion
  163.3 0.0 copy-done.3
  163.3 0.7 copy.56
  164.0 0.0 copy-done.2
  164.0 0.7 copy.57
  (3 shorter events, 0.0 us)
Async XLA Ops:
  152.4 1.7 %copy-start = (bf16[3072,384]{1,0:T(8,128)(2,1)S(1)}, bf16[3072,384]{1,0:T(8,128)(2,1)}, u32[]{:S(2)}) copy-start(bf16[3072,384]{1,0:T(8,128)(2,1)} %get-tuple-element.46.sums_channel) | copy-start | bytes 7077892
  154.1 1.7 %copy-start.1 = (bf16[2,1536,384]{2,1,0:T(8,128)(2,1)S(1)}, bf16[2,1536,384]{2,1,0:T(8,128)(2,1)}, u32[]{:S(2)}) copy-start(bf16[2,1536,384]{2,1,0:T(8,128)(2,1)} %get-tuple-element.47.sums_mixer) | copy-start | bytes 7077892
  155.7 7.5 %copy-start.3 = (bf16[512,384]{1,0:T(8,128)(2,1)S(1)}, bf16[512,384]{1,0:T(8,128)(2,1)}, u32[]{:S(2)}) copy-start(bf16[512,384]{1,0:T(8,128)(2,1)} %get-tuple-element.120) | copy-start | bytes 1179652
  155.7 8.3 %copy-start.2 = (bf16[512,384]{1,0:T(8,128)(2,1)S(1)}, bf16[512,384]{1,0:T(8,128)(2,1)}, u32[]{:S(2)}) copy-start(bf16[512,384]{1,0:T(8,128)(2,1)} %get-tuple-element.121) | copy-start | bytes 1179652

commit v2 on v1

--- a/solution.py
+++ b/solution.py
@@ -533,7 +533,10 @@
 
 
 STRIDES = (1, 2, 4, 8)
-ORDERS = ((0, 1, 2, 3), (0, 2, 3, 1))
+PART = 768
+STEP_ROWS = (0, 384, 576, 672, 720)
+ORDERS = ((0, 1, 2, 3), (0, 2, 3, 1), (0, 1, 2, 3), (0, 1, 2, 3), (0, 1, 2, 3))
+CHUNK = 48
 LOWER_RIGHT, LOWER_LEFT, GATE_RIGHT, LIFT_RIGHT, GATE_LEFT, LIFT_LEFT, CHANNEL_ROWS = (
     0,
     768,
@@ -541,20 +544,10 @@
     1152,
     1344,
     2112,
-    3072,
+    4 * PART,
 )
-(
-    OUT_RIGHT,
-    OUT_LEFT,
-    SHAPE_RIGHT,
-    SHAPE_LEFT,
-    VALUE_RIGHT,
-    VALUE_LEFT,
-    FILTER_OUT,
-    VECTORS,
-    FILTER,
-    MIXER_ROWS,
-) = (0, 192, 576, 768, 960, 1152, 1344, 1472, 1488, 1536)
+OUT_LEFT, SHAPE_RIGHT, SHAPE_LEFT = (0, 384, 576)
+VALUE_RIGHT, VALUE_LEFT, FILTER_OUT, VECTORS, FILTER, OUT_RIGHT = (0, 192, 384, 512, 528, 576)
 
 
 def tile_rows(index, size=TILE):
@@ -562,13 +555,21 @@
 
 
 def whole_kernel(
-    inputs,
+    hidden_in,
     upstream,
-    table_cos,
-    table_sin,
+    hbm_cos,
+    hbm_sin,
     place,
-    vectors,
-    filter_vectors,
+    place_parts,
+    gainfirst,
+    shiftfirst,
+    gainsecond,
+    shiftsecond,
+    convtaps,
+    posweight,
+    posbias,
+    midbias,
+    sinefreq,
     midweight,
     filterout,
     valueright,
@@ -587,6 +588,11 @@
     hidden_grad,
     sums_channel,
     sums_mixer,
+    inputs,
+    table_cos,
+    table_sin,
+    vectors,
+    filter_vectors,
     w_first,
     w_value,
     w_shape,
@@ -608,8 +614,10 @@
     short,
     act_one,
     cos_one,
+    lin_one,
     act_two,
     cos_two,
+    lin_two,
     fil_spec,
     sig_spec,
     prod_spec,
@@ -658,16 +666,17 @@
     send_sem,
     recv_sem,
     load_sem,
-    got_core,
-    got_one,
-    got_two,
-    got_three,
+    got,
     sum_send,
     sum_recv,
     sum_free,
+    late,
+    late_core,
+    late_slots,
+    late_send,
+    late_recv,
 ):
     rows = inputs.shape[0]
-    half = rows // 2
     tiles = rows // TILE
     length = 2 * rows
     spans = length // TILE
@@ -681,11 +690,50 @@
     own_half = pl.ds(pl.multiple_of(narrow * 384, 384), 384)
     other_half = pl.ds(pl.multiple_of((1 - narrow) * 384, 384), 384)
 
+    loads = {}
+
+    def load(name, source, target):
+        loads[name] = pltpu.make_async_copy(source, target, load_sem.at[len(loads)])
+        loads[name].start()
+
+    load("inputs", hidden_in, inputs)
+    load("valueright", valueright, hid.at[0, pl.ds(0, 192)])
+    load("shaperight", shaperight, hid.at[0, pl.ds(192, 192)])
+    load("valueleft", valueleft, hid.at[1, pl.ds(0, 192)])
+    load("shapeleft", shapeleft, hid.at[1, pl.ds(192, 192)])
+    load("filterout", filterout, factor_gate.at[0, pl.ds(0, 128)])
+    load("cos", hbm_cos, table_cos)
+    load("sin", hbm_sin, table_sin)
+    load("outright", outright, d_gate.at[0, pl.ds(0, 192)])
+    load("outleft", outleft, d_gate.at[0, pl.ds(192, 192)])
+    load("gateright", gateright, d_lift.at[1, pl.ds(96, 192), pl.ds(0, 384)])
+    load("liftright", liftright, d_lift.at[1, pl.ds(96, 192), pl.ds(384, 384)])
+    load("lowerleft", lowerleft, d_lift.at[1, pl.ds(0, 96)])
+    load("lower_top", lowerright.at[pl.ds(0, 512)], d_lift.at[0, :, pl.ds(0, 384)])
+    load("lower_end", lowerright.at[pl.ds(512, 256)], d_lift.at[0, pl.ds(0, 256), pl.ds(384, 384)])
+    for k in range(2):
+        at = pl.ds(64 * k, 192)
+        load(("gate", k), gateleft.at[:, pl.ds(D * k, D)], w_gate.at[k, at])
+        load(("lift", k), liftleft.at[:, pl.ds(D * k, D)], w_lift.at[k, at])
+    load("upstream", upstream, up_halves.at[narrow])
+
     barrier = pltpu.get_barrier_semaphore()
     others = [(wide + stride * (1 - 2 * bit), narrow) for stride, bit in zip(STRIDES, bits)]
-    for device in others + [partner]:
+    chip = wide // 2
+    fellows = [(2 * lax.rem(chip + t, 8) + core, narrow) for t in range(8)]
+    for device in [sibling, partner] + fellows[1:]:
         pl.semaphore_signal(barrier, inc=1, device_id=device, device_id_type=MESH)
-    pl.semaphore_wait(barrier, len(others) + 1)
+
+    for i, source in enumerate((gainfirst, shiftfirst, gainsecond, shiftsecond)):
+        vectors[i : i + 1, :] = source[...].reshape(1, D)
+    vectors[4:7, :] = convtaps[...]
+    vectors[7:8, :] = jnp.zeros((1, D), F32)
+    filter_vectors[...] = jnp.zeros(filter_vectors.shape, F32)
+    filter_vectors[0:5, :] = posweight[...]
+    for i, source in enumerate((posbias, midbias, sinefreq)):
+        filter_vectors[8 + i : 9 + i, :] = source[...].reshape(1, 128)
+
+    pl.semaphore_wait(barrier, 9)
 
     def send(source, target, device, index):
         return pltpu.make_async_remote_copy(
@@ -697,101 +745,87 @@
             device_id_type=MESH,
         )
 
-    received = (got_core, got_one, got_two, got_three)
-
-    def summing(slab, first_sem):
-        part = slab.shape[0] // 2
-        offsets = [[0], [part]]
-        for i in range(2):
-            for step in range(4):
-                move = bits[ORDERS[i][step]] * (part >> (step + 1))
-                offsets[i].append(pl.multiple_of(offsets[i][step] + move, 16))
-
-        def copy(source, target, i, step, back):
-            index = first_sem + 8 * back + 2 * step + i
-            return pltpu.make_async_remote_copy(
-                src_ref=source,
-                dst_ref=target,
-                send_sem=sum_send.at[index],
-                recv_sem=sum_recv.at[index],
-                device_id=others[ORDERS[i][step]],
-                device_id_type=MESH,
-            )
-
-        def scatter(i, step):
-            size = part >> (step + 1)
-            away = (1 - bits[ORDERS[i][step]]) * size
-            away = pl.multiple_of(offsets[i][step] + away, 16)
-            return copy(
-                slab.at[pl.ds(away, size)], received[step].at[pl.ds(i * size, size)], i, step, 0
-            )
-
-        def gather(i, step):
-            at = pl.ds(offsets[i][step + 1], part >> (step + 1))
-            return copy(slab.at[at], slab.at[at], i, step, 1)
-
-        def start(step):
-            for i in range(2):
-                scatter(i, step).start()
-
-        def add(step):
-            size = part >> (step + 1)
-            for i in range(2):
-                scatter(i, step).wait()
-
-                @pl.loop(0, size // 48)
-                def _(index):
-                    own = pl.ds(pl.multiple_of(offsets[i][step + 1] + index * 48, 16), 48)
-                    came = received[step][pl.ds(pl.multiple_of(i * size + index * 48, 16), 48), :]
-                    slab[own, :] = (slab[own, :].astype(F32) + came.astype(F32)).astype(BF16)
-
-            for i in range(2):
-                pl.semaphore_signal(
-                    sum_free.at[first_sem // 2 + 2 * step + i],
-                    inc=1,
-                    device_id=others[ORDERS[i][step]],
-                    device_id_type=MESH,
-                )
-
-        def clear(step):
-            for i in range(2):
-                pl.semaphore_wait(sum_free.at[first_sem // 2 + 2 * step + i], 1)
-
-        def back(step):
-            for i in range(2):
-                gather(i, step).start()
-
-        def take(step):
-            for i in range(2):
-                gather(i, step).wait()
-
-        return (start, add, clear, back, take, offsets)
-
     mixer_slab = sums_mixer.at[narrow]
-    channel_start, channel_add, channel_clear, channel_back, channel_take, _ = summing(sums_channel, 0)
-    mixer_start, mixer_add, mixer_clear, mixer_back, mixer_take, mixer_offsets = summing(mixer_slab, 16)
-
-    load_copies = []
-    for source, target in ((gateleft, w_gate), (liftleft, w_lift)):
-        for k in range(2):
-            copy = pltpu.make_async_copy(
-                source.at[:, pl.ds(D * k, D)],
-                target.at[k, pl.ds(64 * k, 192)],
-                load_sem.at[len(load_copies)],
-            )
-            copy.start()
-            load_copies.append(copy)
+    parts_of = [sums_channel.at[pl.ds(PART * i, PART)] for i in range(4)] + [mixer_slab.at[pl.ds(0, PART)]]
+    offsets = []
+    for order in ORDERS:
+        found = [0]
+        for step in range(4):
+            found.append(pl.multiple_of(found[step] + bits[order[step]] * (PART >> (step + 1)), 16))
+        offsets.append(found)
+
+    def sum_copy(source, target, i, step, back):
+        index = 8 * i + 4 * back + step
+        return pltpu.make_async_remote_copy(
+            src_ref=source,
+            dst_ref=target,
+            send_sem=sum_send.at[index],
+            recv_sem=sum_recv.at[index],
+            device_id=others[ORDERS[i][step]],
+            device_id_type=MESH,
+        )
+
+    def scatter(i, step):
+        size = PART >> (step + 1)
+        away = pl.multiple_of(offsets[i][step] + (1 - bits[ORDERS[i][step]]) * size, 16)
+        return sum_copy(
+            parts_of[i].at[pl.ds(away, size)], got.at[i, pl.ds(STEP_ROWS[step], size)], i, step, 0
+        )
+
+    def gather(i, step):
+        at = pl.ds(offsets[i][step + 1], PART >> (step + 1))
+        return sum_copy(parts_of[i].at[at], parts_of[i].at[at], i, step, 1)
+
+    def hand_back(i, step):
+        pl.semaphore_wait(sum_free.at[4 * i + step], 1)
+        gather(i, step).start()
+
+    def advance(i, step):
+        scatter(i, step).wait()
+
+        @pl.loop(0, (PART >> (step + 1)) // CHUNK)
+        def _(index):
+            own = pl.ds(pl.multiple_of(offsets[i][step + 1] + index * CHUNK, 16), CHUNK)
+            came = got[i, pl.ds(pl.multiple_of(STEP_ROWS[step] + index * CHUNK, 16), CHUNK), :]
+            parts_of[i][own, :] = (parts_of[i][own, :].astype(F32) + came.astype(F32)).astype(BF16)
+
+        pl.semaphore_signal(
+            sum_free.at[4 * i + step],
+            inc=1,
+            device_id=others[ORDERS[i][step]],
+            device_id_type=MESH,
+        )
+        if step < 3:
+            scatter(i, step + 1).start()
+        else:
+            hand_back(i, 3)
+
+    def retreat(i, step):
+        gather(i, step).wait()
+        if step > 0:
+            hand_back(i, step - 1)
+
+    def late_copy(source, target, device, index):
+        return pltpu.make_async_remote_copy(
+            src_ref=source,
+            dst_ref=target,
+            send_sem=late_send.at[index],
+            recv_sem=late_recv.at[index],
+            device_id=device,
+            device_id_type=MESH,
+        )
 
     up_copy = send(upstream, up_halves.at[narrow], partner, 0)
     up_copy.start()
-    up_halves[narrow] = upstream[...]
 
     row = lax.broadcasted_iota(jnp.int32, (D, 384), 0)
     lane = lax.broadcasted_iota(jnp.int32, (D, 384), 1)
     step = jnp.where(lane >= 96, 96, 0) + jnp.where(lane >= 192, 96, 0) + jnp.where(lane >= 288, 96, 0)
     select = mask(row == lane + step + narrow * 96)
-    right_half = mm(valueright[...], select).astype(BF16)
-    shape_half = mm(shaperight[...], select).astype(BF16)
+    for name in ("valueright", "shaperight", "valueleft", "shapeleft"):
+        loads[name].wait()
+    right_half = mm(hid[0, 0:192, :], select).astype(BF16)
+    shape_half = mm(hid[0, 192:384, :], select).astype(BF16)
     for b in range(4):
         kept = between(384, 96 * b, 96 * b + 96)
         w_first[192 * b : 192 * b + 192, 0:384] = right_half * kept
@@ -801,8 +835,8 @@
     group = jnp.where(lane >= PAD, 1, 0)
     entry = lane - PAD * group
     spread = mask((row == (2 * narrow + group) * 192 + entry) & (entry < 192))
-    for source, target in ((valueleft, w_value), (shapeleft, w_shape)):
-        wider = mm(source[...], spread).astype(BF16)
+    for source, target in ((0, w_value), (192, w_shape)):
+        wider = mm(hid[1, source : source + 192, :], spread).astype(BF16)
         for b in range(4):
             for k in range(2):
                 target[96 * b + 48 * k : 96 * b + 48 * k + 48, :] = wider[
@@ -812,8 +846,8 @@
     lane = lax.broadcasted_iota(jnp.int32, (D, 192), 1)
     start = (2 * narrow) * 192 + (1 - narrow) * 96
     cross = mask(row == start + lane + jnp.where(lane >= 96, 96, 0))
-    for i, source in enumerate((valueright, shaperight)):
-        part = mm(source[...], cross).astype(BF16)
+    for i in range(2):
+        part = mm(hid[0, 192 * i : 192 * i + 192, :], cross).astype(BF16)
         for b in range(2):
             w_cross[i, 192 * b : 192 * b + 192, :] = part * between(192, 96 * b, 96 * b + 96)
     first = vectors[0:1, :]
@@ -822,6 +856,7 @@
     coarse = vectors[...].astype(BF16)
     fine = (vectors[...] - coarse.astype(F32)).astype(BF16)
     through[...] = mm(coarse, w_first[...]) + mm(fine, w_first[...])
+    loads["inputs"].wait()
 
     @pl.loop(0, tiles)
     def _(index):
@@ -850,12 +885,19 @@
 
     row = lax.broadcasted_iota(jnp.int32, (D, PAD), 0)
     lane = lax.broadcasted_iota(jnp.int32, (D, PAD), 1)
-    pick = mask((row == quarter * 192 + lane) & (lane < 192), F32)
-    conv = mm(vectors[...], pick, HIGHEST)
-    own_out[...] = mm(filterout[...], pick, HIGHEST)
+    pick = mask((row == quarter * 192 + lane) & (lane < 192))
+    conv = mm(coarse, pick) + mm(fine, pick)
+    loads["filterout"].wait()
+    own_out[...] = mm(factor_gate[0, 0:128, :].astype(BF16), pick).astype(BF16)
     pos_bias = filter_vectors[8:9, :]
     mid_bias = filter_vectors[9:10, :]
     frequency = filter_vectors[10:11, :]
+    mid_high = midweight[...].astype(BF16)
+    mid_low = (midweight[...] - mid_high.astype(F32)).astype(BF16)
+    pos_high = filter_vectors[0:8, :].astype(BF16).astype(F32)
+    pos_parts = jnp.concatenate(
+        [pos_high, pos_high, filter_vectors[0:8, :] - pos_high, jnp.zeros((8, 128), F32)], axis=0
+    ).astype(BF16)
     ranks = 5 * (quarter * 192 + lanes(PAD))
     for bound in range(5):
         ranks = jnp.where(ranks >= D, ranks - D, ranks)
@@ -871,15 +913,23 @@
     @pl.loop(0, spans)
     def _(index):
         at = tile_rows(index)
-        one = mm(place[at, :], filter_vectors[0:8, :], HIGHEST) + pos_bias
+        one = mm(place_parts[at, :], pos_parts) + pos_bias
         sine, cosine = sine_cosine(frequency * one)
-        act_one[at, :] = sine
-        cos_one[at, :] = cosine
-        two = mm(sine, midweight[...], HIGHEST) + mid_bias
+        high = sine.astype(BF16)
+        low = (sine - high.astype(F32)).astype(BF16)
+        lin_one[at, :] = one.astype(BF16)
+        act_one[at, :] = high
+        cos_one[at, :] = cosine.astype(BF16)
+        two = mm(high, mid_high) + mm(low, mid_high) + mm(high, mid_low) + mid_bias
         sine, cosine = sine_cosine(frequency * two)
-        act_two[at, :] = sine
-        cos_two[at, :] = cosine
-        short[at, :] = (mm(sine, own_out[...], HIGHEST) * decay(index)).astype(BF16)
+        high = sine.astype(BF16)
+        lin_two[at, :] = two.astype(BF16)
+        act_two[at, :] = high
+        cos_two[at, :] = cosine.astype(BF16)
+        short[at, :] = (mm(high, own_out[...]) * decay(index)).astype(BF16)
+
+    loads["cos"].wait()
+    loads["sin"].wait()
 
     @pl.loop(0, spans)
     def _(index):
@@ -891,31 +941,35 @@
         fil_spec[0, at, :] = real * turn_cos + imag * turn_sin
         fil_spec[1, at, :] = imag * turn_cos - real * turn_sin
 
-    out_half = outright[:, own_half]
+    for name in ("outright", "outleft", "gateright", "liftright", "lowerleft", "lower_top", "lower_end"):
+        loads[name].wait()
+    out_half = d_gate[0, 0:192, own_half]
     w_out_first[0:192, :] = out_half * between(384, 0, 192)
     w_out_first[192:256, :] = jnp.zeros((64, 384), BF16)
     w_out_first[256:448, :] = out_half * between(384, 192, 384)
     w_out_first[448:512, :] = jnp.zeros((64, 384), BF16)
     for b in range(4):
         for k in range(4):
-            w_out_second[b // 2, 192 * (b % 2) + 48 * k : 192 * (b % 2) + 48 * k + 48, :] = outleft[
-                48 * b : 48 * b + 48, :
+            w_out_second[b // 2, 192 * (b % 2) + 48 * k : 192 * (b % 2) + 48 * k + 48, :] = d_gate[
+                0, 192 + 48 * b : 240 + 48 * b, :
             ] * between(D, 192 * k, 192 * k + 192)
     lane = lanes(384)
     inside = lane - jnp.where(lane >= 192, 192, 0)
     for b in range(4):
         kept = mask((inside >= 48 * b) & (inside < 48 * b + 48))
-        w_glu[192 * b : 192 * b + 192, 0:384] = gateright[...] * kept
-        w_glu[192 * b : 192 * b + 192, 384:768] = liftright[...] * kept
+        w_glu[192 * b : 192 * b + 192, 0:384] = d_lift[1, 96:288, 0:384] * kept
+        w_glu[192 * b : 192 * b + 192, 384:768] = d_lift[1, 96:288, 384:768] * kept
     for target in (w_gate, w_lift):
         target[0, 192:256, :] = jnp.zeros((64, D), BF16)
         target[1, 0:64, :] = jnp.zeros((64, D), BF16)
-    w_lower[0] = lowerright[:, 0:256] * between(256, 0, 192)
-    w_lower[1] = lowerright[:, 128:384] * between(256, 64, 256)
+    w_lower[0, 0:512, :] = d_lift[0, :, 0:256] * between(256, 0, 192)
+    w_lower[0, 512:768, :] = d_lift[0, 0:256, 384:640] * between(256, 0, 192)
+    w_lower[1, 0:512, :] = d_lift[0, :, 128:384] * between(256, 64, 256)
+    w_lower[1, 512:768, :] = d_lift[0, 0:256, 512:768] * between(256, 64, 256)
     for b in range(2):
         for k in range(4):
-            w_lower_second[192 * b + 48 * k : 192 * b + 48 * k + 48, :] = lowerleft[
-                48 * b : 48 * b + 48, :
+            w_lower_second[192 * b + 48 * k : 192 * b + 48 * k + 48, :] = d_lift[
+                1, 48 * b : 48 * b + 48, :
             ] * between(D, 192 * k, 192 * k + 192)
 
     sig_copy.wait_recv()
@@ -993,8 +1047,10 @@
         inner_copy(index).start()
 
     up_copy.wait_recv()
-    for copy in load_copies:
-        copy.wait()
+    for k in range(2):
+        loads["gate", k].wait()
+        loads["lift", k].wait()
+    loads["upstream"].wait()
 
     gain_second = vectors[2:3, :]
     shift_second = vectors[3:4, :]
@@ -1105,7 +1161,8 @@
         sums_channel[target : target + 192, :] = total.astype(BF16)
 
     sums_channel[2880:3072, :] = jnp.zeros((192, 384), BF16)
-    channel_start(0)
+    for i in range(4):
+        scatter(i, 0).start()
 
     dn_copy.wait_recv()
     into = dn_own[...] + dn_recv[...].astype(F32)
@@ -1126,6 +1183,8 @@
     mid_send[...] = hat_two[:, other_half].astype(BF16)
     middle_copy.start()
     d_inner_out[own_rows, :] = mm_nt(branch[...], w_out_second[narrow]).astype(BF16)
+    for i in range(4):
+        advance(i, 0)
 
     @pl.loop(0, tiles)
     def _(order):
@@ -1156,9 +1215,6 @@
         ).astype(BF16)
         shape_copy(index).start()
 
-
-    channel_add(0)
-    channel_start(1)
     for h in range(2):
         for side in range(2):
             columns = slice(384 * side, 384 * side + 384)
@@ -1166,11 +1222,40 @@
             for b in range(2):
                 first_row = OUT_LEFT + 192 * h + 96 * side + 48 * b
                 mixer_slab[first_row : first_row + 48, :] = folded[b].astype(BF16)
+    lane = lax.broadcasted_iota(jnp.int32, (2 * PAD, 384), 1)
+    row = lax.broadcasted_iota(jnp.int32, (2 * PAD, 384), 0)
+    squeeze = mask(row == lane + jnp.where(lane >= 192, 64, 0))
+
+    def first_gradient(offset):
+        whole = mm_tn(norm_one[...], d_inner_one[:, offset : offset + 384])
+        total = None
+        for b in range(4):
+            term = whole[192 * b : 192 * b + 192, :] * between(384, 96 * b, 96 * b + 96, F32)
+            total = term if total is None else total + term
+        return total.astype(BF16)
+
+    def second_gradient(offset, upper):
+        above = jnp.concatenate([upper[0], upper[1]], axis=1)
+        whole = mm_tn(inner_one[:, offset : offset + 384], above)
+        pieces = []
+        for b in range(4):
+            total = None
+            for k in range(2):
+                term = whole[96 * b + 48 * k : 96 * b + 48 * k + 48, :] * between(
+                    2 * PAD, PAD * k, PAD * k + PAD, F32
+                )
+                total = term if total is None else total + term
+            pieces.append(total)
+        return mm(jnp.concatenate(pieces, axis=0).astype(BF16), squeeze).astype(BF16)
+
+    mixer_slab[SHAPE_RIGHT : SHAPE_RIGHT + 192, :] = first_gradient(384)
+    mixer_slab[SHAPE_LEFT : SHAPE_LEFT + 192, :] = second_gradient(384, d_shaping)
+    scatter(4, 0).start()
     parts = []
     for k in range(2):
         product = (shaping[k] * long_halves[k].astype(F32)).astype(BF16)
         parts.append(mm_tn(product, d_inner_out[...]))
-    mixer_slab[OUT_RIGHT : OUT_RIGHT + 192, :] = jnp.where(
+    late[OUT_RIGHT : OUT_RIGHT + 192, :] = jnp.where(
         lanes(384) < 192, parts[0][0:192, :], parts[1][0:192, :]
     ).astype(BF16)
 
@@ -1214,8 +1299,9 @@
     ds_copy.start()
     ds_halves[core] = long_rows[core]
 
-    channel_add(1)
-    channel_start(2)
+    advance(4, 0)
+    advance(1, 1)
+    advance(0, 1)
     grad_vectors[...] = jnp.zeros(grad_vectors.shape, F32)
     sums = [jnp.zeros((1, PAD), F32) for _ in range(3)]
     for index in range(spans):
@@ -1240,25 +1326,29 @@
         at = tile_rows(index)
         d_taps = mm(table_cos[at, :], sig_spec[0]) + mm(table_sin[at, :], sig_spec[1])
         d_mod = d_taps * decay(index)
-        d_lin[...] += mm_tn(act_two[at, :], d_mod, HIGHEST)
-        two = mm_nt(d_mod, own_out[...], HIGHEST) * cos_two[at, :]
+        d_mod = d_mod.astype(BF16)
+        d_lin[...] += mm_tn(act_two[at, :], d_mod)
+        two = mm_nt(d_mod, own_out[...]) * cos_two[at, :].astype(F32)
         scaled_two = two * frequency
-        grad_filter[0:128, :] += mm_tn(act_one[at, :], scaled_two, HIGHEST)
-        one = mm_nt(scaled_two, midweight[...], HIGHEST) * cos_one[at, :]
+        coarse_two = scaled_two.astype(BF16)
+        grad_filter[0:128, :] += mm_tn(act_one[at, :], coarse_two)
+        one = mm_nt(coarse_two, mid_high) * cos_one[at, :].astype(F32)
         scaled_one = one * frequency
-        grad_filter[128:136, :] += mm_tn(place[at, :], scaled_one, HIGHEST)
+        grad_filter[128:136, :] += mm_tn(place_parts[at, :], scaled_one.astype(BF16))[0:8, :]
         grad_filter[136:137, :] += jnp.sum(scaled_one, axis=0, keepdims=True)
         grad_filter[137:138, :] += jnp.sum(scaled_two, axis=0, keepdims=True)
-        lin_one = mm(place[at, :], filter_vectors[0:8, :], HIGHEST) + pos_bias
-        lin_two = mm(act_one[at, :], midweight[...], HIGHEST) + mid_bias
-        grad_filter[138:139, :] += jnp.sum(one * lin_one + two * lin_two, axis=0, keepdims=True)
-
-    mixer_slab[FILTER_OUT : FILTER_OUT + 128, :] = mm(d_lin[...].astype(BF16), place_core).astype(BF16)
+        grad_filter[138:139, :] += jnp.sum(
+            one * lin_one[at, :].astype(F32) + two * lin_two[at, :].astype(F32), axis=0, keepdims=True
+        )
+
+    late[FILTER_OUT : FILTER_OUT + 128, :] = mm(d_lin[...].astype(BF16), place_core).astype(BF16)
     for i in range(3):
-        mixer_slab[FILTER : FILTER + 48, 128 * i : 128 * i + 128] = grad_filter[48 * i : 48 * i + 48, :].astype(BF16)
-
-    channel_add(2)
-    channel_start(3)
+        late[FILTER : FILTER + 48, 128 * i : 128 * i + 128] = grad_filter[
+            48 * i : 48 * i + 48, :
+        ].astype(BF16)
+
+    advance(2, 1)
+    advance(1, 2)
 
     ds_copy.wait_recv()
     other_blocks = pl.ds(pl.multiple_of((1 - narrow) * 192, 192), 192)
@@ -1283,39 +1373,14 @@
         value_send[at, 192:256] = tail[:, 64:128].astype(BF16)
         value_copy(index).start()
 
-    channel_add(3)
-    for step in range(4):
-        channel_clear(step)
-    channel_back(3)
-    for offset, target in ((0, VALUE_RIGHT), (384, SHAPE_RIGHT)):
-        whole = mm_tn(norm_one[...], d_inner_one[:, offset : offset + 384])
-        total = None
-        for b in range(4):
-            term = whole[192 * b : 192 * b + 192, :] * between(
-                384, 96 * b, 96 * b + 96, F32
-            )
-            total = term if total is None else total + term
-        mixer_slab[target : target + 192, :] = total.astype(BF16)
-    lane = lax.broadcasted_iota(jnp.int32, (2 * PAD, 384), 1)
-    row = lax.broadcasted_iota(jnp.int32, (2 * PAD, 384), 0)
-    squeeze = mask(row == lane + jnp.where(lane >= 192, 64, 0))
-    for offset, upper, target in ((0, ds_halves, VALUE_LEFT), (384, d_shaping, SHAPE_LEFT)):
-        above = jnp.concatenate([upper[0], upper[1]], axis=1)
-        whole = mm_tn(inner_one[:, offset : offset + 384], above)
-        pieces = []
-        for b in range(4):
-            total = None
-            for k in range(2):
-                term = whole[96 * b + 48 * k : 96 * b + 48 * k + 48, :] * between(
-                    2 * PAD, PAD * k, PAD * k + PAD, F32
-                )
-                total = term if total is None else total + term
-            pieces.append(total)
-        total = jnp.concatenate(pieces, axis=0).astype(BF16)
-        mixer_slab[target : target + 192, :] = mm(total, squeeze).astype(BF16)
-
-    channel_take(3)
-    channel_back(2)
+    advance(3, 1)
+    advance(0, 2)
+    late[VALUE_RIGHT : VALUE_RIGHT + 192, :] = first_gradient(0)
+    late[VALUE_LEFT : VALUE_LEFT + 192, :] = second_gradient(0, ds_halves)
+    advance(4, 1)
+    advance(1, 3)
+    advance(2, 2)
+    advance(0, 3)
 
     first_half = vectors[0:1, own_half]
     middle_copy.wait_recv()
@@ -1342,57 +1407,91 @@
 
     grad_vectors[2:4, :] = gain_sums[0:2, 0:384]
     grad_vectors[8:10, :] = gain_sums[0:2, 384:768]
-    mixer_slab[VECTORS : VECTORS + 16, :] = grad_vectors[...].astype(BF16)
-    mixer_start(0)
-    channel_take(2)
-    channel_back(1)
-    mixer_add(0)
-    for step in range(1, 4):
-        mixer_start(step)
-        mixer_add(step)
-    for step in range(4):
-        mixer_clear(step)
-    mixer_back(3)
-    channel_take(1)
-    channel_back(0)
-    for step in (3, 2, 1):
-        mixer_take(step)
-        if step > 1:
-            mixer_back(step - 1)
-    size = MIXER_ROWS // 4
+    late[VECTORS : VECTORS + 16, :] = grad_vectors[...].astype(BF16)
+
+    core_rows = pl.ds(pl.multiple_of(core * 384, 16), 384)
+    to_core = late_copy(
+        late.at[pl.ds(pl.multiple_of((1 - core) * 384, 16), 384)], late_core, sibling, 0
+    )
+    to_core.start()
+    advance(3, 2)
+    advance(4, 2)
+    to_core.wait()
+
+    @pl.loop(0, 384 // CHUNK)
+    def _(index):
+        at = pl.ds(pl.multiple_of(core * 384 + index * CHUNK, 16), CHUNK)
+        came = late_core[pl.ds(pl.multiple_of(index * CHUNK, 16), CHUNK), :]
+        late[at, :] = (late[at, :].astype(F32) + came.astype(F32)).astype(BF16)
+
+    def share(t):
+        return pl.multiple_of(core * 384 + lax.rem(chip + 8 - t, 8) * CHUNK, 16)
+
+    direct = [
+        late_copy(late.at[pl.ds(share(8 - t), CHUNK)], late_slots.at[t - 1], fellows[t], t)
+        for t in range(1, 8)
+    ]
+    for copy in direct:
+        copy.start()
+    advance(2, 3)
+    retreat(1, 3)
+    advance(3, 3)
+    advance(4, 3)
+    retreat(0, 3)
+    total = late[pl.ds(share(0), CHUNK), :].astype(F32)
+    for t in range(1, 8):
+        direct[t - 1].wait()
+        total += late_slots[t - 1].astype(F32)
+    own_share = pl.ds(pl.multiple_of(PART + share(0), 16), CHUNK)
+    mixer_slab[own_share, :] = total.astype(BF16)
+    spread_out = [
+        late_copy(mixer_slab.at[own_share], mixer_slab.at[own_share], fellows[t], 8 + t)
+        for t in range(1, 8)
+    ]
+    for copy in spread_out:
+        copy.start()
+    retreat(2, 3)
+    retreat(1, 2)
+    retreat(0, 2)
+    retreat(3, 3)
+    retreat(4, 3)
     across = []
-    for i in range(2):
-        at = pl.ds(mixer_offsets[i][1], size)
-        across.append(
-            pltpu.make_async_remote_copy(
-                src_ref=mixer_slab.at[at],
-                dst_ref=mixer_slab.at[at],
-                send_sem=sum_send.at[32 + i],
-                recv_sem=sum_recv.at[32 + i],
-                device_id=partner,
-                device_id_type=MESH,
-            )
-        )
-        across[i].start()
-    mixer_back(0)
-    for i in range(2):
-        across[i].wait()
-        at = pl.ds(mixer_offsets[i][1], size)
-        across.append(
-            pltpu.make_async_remote_copy(
-                src_ref=sums_mixer.at[1 - narrow, at],
-                dst_ref=sums_mixer.at[1 - narrow, at],
-                send_sem=sum_send.at[34 + i],
-                recv_sem=sum_recv.at[34 + i],
-                device_id=sibling,
-                device_id_type=MESH,
-            )
-        )
-        across[2 + i].start()
-    for i in range(2):
-        across[2 + i].wait()
-    mixer_take(0)
-    channel_take(0)
+    along_own = []
+    for t in range(8):
+        if t > 0:
+            spread_out[t - 1].wait()
+        at = pl.ds(pl.multiple_of(PART + share(t), 16), CHUNK)
+        across.append(late_copy(mixer_slab.at[at], mixer_slab.at[at], partner, 16 + t))
+        across[t].start()
+        along_own.append(late_copy(mixer_slab.at[at], mixer_slab.at[at], sibling, 24 + t))
+        along_own[t].start()
+    retreat(1, 1)
+    retreat(2, 2)
+    retreat(0, 1)
+    retreat(3, 2)
+    retreat(4, 2)
+    retreat(2, 1)
+    retreat(3, 1)
+    retreat(4, 1)
+    early_rows = pl.ds(offsets[4][1], PART // 2)
+    across_early = late_copy(mixer_slab.at[early_rows], mixer_slab.at[early_rows], partner, 40)
+    across_early.start()
+    along_other = []
+    for t in range(8):
+        across[t].wait()
+        at = pl.ds(pl.multiple_of(PART + share(t), 16), CHUNK)
+        other = sums_mixer.at[1 - narrow, at]
+        along_other.append(late_copy(other, other, sibling, 32 + t))
+        along_other[t].start()
+    for i in range(4):
+        retreat(i, 0)
+    across_early.wait()
+    other = sums_mixer.at[1 - narrow, early_rows]
+    along_early = late_copy(other, other, sibling, 41)
+    along_early.start()
+    retreat(4, 0)
+    for copy in along_own + along_other + [along_early]:
+        copy.wait()
 
     for copy in (up_copy, dl_copy, ds_copy, dn_copy, cross_copy, middle_copy):
         copy.wait_send()
@@ -1404,67 +1503,129 @@
 
 
 def finish_kernel(
-    sums_channel,
-    sums_mixer,
-    grad_vectors,
+    hidden_in,
+    hidden_grad_in,
+    hbm_channel,
+    hbm_mixer,
+    hidden_out,
+    hidden_grad,
+    grad_gainfirst,
+    grad_shiftfirst,
     grad_valueright,
     grad_valueleft,
     grad_shaperight,
     grad_shapeleft,
-    grad_filter,
+    grad_convtaps,
+    grad_posweight,
+    grad_posbias,
+    grad_sinefreq,
+    grad_midweight,
+    grad_midbias,
     grad_filterout,
     grad_outright,
     grad_outleft,
+    grad_gainsecond,
+    grad_shiftsecond,
     grad_gateright,
     grad_gateleft,
     grad_liftright,
     grad_liftleft,
     grad_lowerright,
     grad_lowerleft,
+    channel,
+    mixer,
+    gateright,
+    gateleft,
+    liftright,
+    liftleft,
+    lowerright,
+    lowerleft,
+    both_filter,
+    in_sem,
+    out_sem,
 ):
-    grad_lowerright[...] = sums_channel[LOWER_RIGHT : LOWER_RIGHT + D, :].astype(F32)
-    grad_gateright[...] = sums_channel[GATE_RIGHT : GATE_RIGHT + 192, :].astype(F32)
-    grad_liftright[...] = sums_channel[LIFT_RIGHT : LIFT_RIGHT + 192, :].astype(F32)
+    ins = []
+    outs = []
+
+    def fetch(source, target):
+        ins.append(pltpu.make_async_copy(source, target, in_sem.at[len(ins)]))
+        ins[-1].start()
+
+    def store(source, target):
+        outs.append(pltpu.make_async_copy(source, target, out_sem.at[len(outs)]))
+        outs[-1].start()
+
     for i in range(4):
-        columns = slice(384 * i, 384 * i + 384)
+        at = pl.ds(PART * i, PART)
+        fetch(hbm_channel.at[at], channel.at[at])
+    fetch(hbm_mixer, mixer)
+    hidden_out[...] = hidden_in[...]
+    hidden_grad[...] = hidden_grad_in[...]
+
+    ins[0].wait()
+    lowerright[...] = channel[LOWER_RIGHT : LOWER_RIGHT + D, :].astype(F32)
+    store(lowerright, grad_lowerright)
+    ins[1].wait()
+    for h in range(2):
+        columns = slice(384 * h, 384 * h + 384)
+        lowerleft[:, columns] = channel[LOWER_LEFT + 96 * h : LOWER_LEFT + 96 * h + 96, :].astype(F32)
+    gateright[...] = channel[GATE_RIGHT : GATE_RIGHT + 192, :].astype(F32)
+    liftright[...] = channel[LIFT_RIGHT : LIFT_RIGHT + 192, :].astype(F32)
+    store(lowerleft, grad_lowerleft)
+    store(gateright, grad_gateright)
+    store(liftright, grad_liftright)
+    ins[2].wait()
+    for i in range(4):
         first_row = GATE_LEFT + 192 * i
-        grad_gateleft[:, columns] = sums_channel[first_row : first_row + 192, :].astype(F32)
+        gateleft[:, 384 * i : 384 * i + 384] = channel[first_row : first_row + 192, :].astype(F32)
+    store(gateleft, grad_gateleft)
+    ins[3].wait()
+    for i in range(4):
         first_row = LIFT_LEFT + 192 * i
-        grad_liftleft[:, columns] = sums_channel[first_row : first_row + 192, :].astype(F32)
+        liftleft[:, 384 * i : 384 * i + 384] = channel[first_row : first_row + 192, :].astype(F32)
+    store(liftleft, grad_liftleft)
+    ins[4].wait()
+
     lane = lax.broadcasted_iota(jnp.int32, (384, D), 1)
     row = lax.broadcasted_iota(jnp.int32, (384, D), 0)
     step = jnp.where(row >= 96, 96, 0) + jnp.where(row >= 192, 96, 0) + jnp.where(row >= 288, 96, 0)
     unselect = [mask(lane == row + step + 96 * h) for h in range(2)]
-    for first_row, target in ((VALUE_RIGHT, grad_valueright), (SHAPE_RIGHT, grad_shaperight)):
-        target[...] = mm(sums_mixer[0, first_row : first_row + 192, :], unselect[0]) + mm(
-            sums_mixer[1, first_row : first_row + 192, :], unselect[1]
+    for first_row, target in ((PART + VALUE_RIGHT, grad_valueright), (SHAPE_RIGHT, grad_shaperight)):
+        target[...] = mm(mixer[0, first_row : first_row + 192, :], unselect[0]) + mm(
+            mixer[1, first_row : first_row + 192, :], unselect[1]
         )
     for h in range(2):
         columns = slice(384 * h, 384 * h + 384)
-        grad_lowerleft[:, columns] = sums_channel[
-            LOWER_LEFT + 96 * h : LOWER_LEFT + 96 * h + 96, :
-        ].astype(F32)
         for first_row, target in (
-            (OUT_RIGHT, grad_outright),
+            (PART + OUT_RIGHT, grad_outright),
             (SHAPE_LEFT, grad_shapeleft),
-            (VALUE_LEFT, grad_valueleft),
+            (PART + VALUE_LEFT, grad_valueleft),
         ):
-            target[:, columns] = sums_mixer[h, first_row : first_row + 192, :].astype(F32)
+            target[:, columns] = mixer[h, first_row : first_row + 192, :].astype(F32)
         for side in range(2):
             at = slice(OUT_LEFT + 192 * h + 96 * side, OUT_LEFT + 192 * h + 96 * side + 96)
-            grad_outleft[96 * h : 96 * h + 96, 384 * side : 384 * side + 384] = sums_mixer[
+            grad_outleft[96 * h : 96 * h + 96, 384 * side : 384 * side + 384] = mixer[
                 0, at, :
-            ].astype(F32) + sums_mixer[1, at, :].astype(F32)
-        own = sums_mixer[h, VECTORS : VECTORS + 16, :].astype(F32)
-        both = own + sums_mixer[1 - h, VECTORS : VECTORS + 16, :].astype(F32)
-        grad_vectors[0:2, columns] = own[0:2, :]
-        grad_vectors[2:4, columns] = both[2 + 6 * h : 4 + 6 * h, :]
-        grad_vectors[4:7, columns] = own[4:7, :]
+            ].astype(F32) + mixer[1, at, :].astype(F32)
+    vectors = [mixer[h, PART + VECTORS : PART + VECTORS + 16, :].astype(F32) for h in range(2)]
+    whole = jnp.concatenate(vectors, axis=1)
+    both = vectors[0] + vectors[1]
+    grad_gainfirst[...] = whole[0:1, :].reshape(D)
+    grad_shiftfirst[...] = whole[1:2, :].reshape(D)
+    grad_convtaps[...] = whole[4:7, :]
+    grad_gainsecond[...] = jnp.concatenate([both[2:3, :], both[8:9, :]], axis=1).reshape(D)
+    grad_shiftsecond[...] = jnp.concatenate([both[3:4, :], both[9:10, :]], axis=1).reshape(D)
     for i in range(3):
         columns = slice(128 * i, 128 * i + 128)
-        grad_filter[48 * i : 48 * i + 48, :] = sums_mixer[
-            0, FILTER : FILTER + 48, columns
-        ].astype(F32) + sums_mixer[1, FILTER : FILTER + 48, columns].astype(F32)
+        at = slice(PART + FILTER, PART + FILTER + 48)
+        both_filter[48 * i : 48 * i + 48, :] = mixer[0, at, columns].astype(F32) + mixer[
+            1, at, columns
+        ].astype(F32)
+    grad_midweight[...] = both_filter[0:128, :]
+    grad_posweight[...] = both_filter[128:133, :]
+    grad_posbias[...] = both_filter[136:137, :].reshape(128)
+    grad_midbias[...] = both_filter[137:138, :].reshape(128)
+    grad_sinefreq[...] = both_filter[138:139, :].reshape(128)
     count = grad_filterout.shape[1]
     first = (lax.axis_index("wide") * 2 + lax.axis_index("narrow")) * count
     total = jnp.zeros(grad_filterout.shape, F32)
@@ -1472,9 +1633,12 @@
     lane = lax.broadcasted_iota(jnp.int32, (384, count), 1)
     for h in range(2):
         total += mm(
-            sums_mixer[h, FILTER_OUT : FILTER_OUT + 128, :], mask(row + 384 * h == first + lane)
+            mixer[h, PART + FILTER_OUT : PART + FILTER_OUT + 128, :],
+            mask(row + 384 * h == first + lane),
         )
     grad_filterout[...] = total
+    for copy in outs:
+        copy.wait()
 
 
 def transform_tables(length):
@@ -1497,7 +1661,11 @@
         np.sin(turn),
         np.zeros(length),
     ]
-    return np.stack(columns, axis=1).astype(np.float32)
+    table = np.stack(columns, axis=1).astype(np.float32)
+    feats = np.concatenate([table[:, :5], np.zeros((length, 3), np.float32)], axis=1)
+    high = feats.astype(jnp.bfloat16)
+    low = (feats - high.astype(np.float32)).astype(jnp.bfloat16)
+    return (table, np.concatenate([high, low, high, np.zeros_like(high)], axis=1))
 
 
 def pair_body(
@@ -1530,13 +1698,6 @@
     rows = hidden_in.shape[0]
     length = 2 * rows
     table_cos, table_sin = transform_tables(length)
-    vectors = jnp.concatenate(
-        [jnp.stack([gainfirst, shiftfirst, gainsecond, shiftsecond]), convtaps, jnp.zeros((1, D), F32)]
-    )
-    filter_vectors = jnp.concatenate(
-        [posweight, jnp.zeros((3, 128), F32), jnp.stack([posbias, midbias, sinefreq]), jnp.zeros((5, 128), F32)]
-    )
-
     def out(extent, dtype=BF16):
         return jax.ShapeDtypeStruct(extent, dtype)
 
@@ -1551,11 +1712,16 @@
             out((rows, 384)),
             out((rows, 384)),
             out((CHANNEL_ROWS, 384)),
-            out((2, MIXER_ROWS, 384)),
+            out((2, 2 * PART, 384)),
         ),
-        in_specs=[vmem] * 16 + [hbm, vmem, hbm, vmem, vmem],
+        in_specs=[hbm] * 4 + [vmem] * 12 + [hbm] * 13,
         out_specs=[vmem] * 4,
         scratch_shapes=[
+            buf(rows, D),
+            buf(length, length),
+            buf(length, length),
+            buf(8, D, dtype=F32),
+            buf(16, 128, dtype=F32),
             buf(D, D),
             buf(384, 512),
             buf(384, 512),
@@ -1575,10 +1741,12 @@
             buf(2, rows, PAD, dtype=F32),
             buf(length + 8, PAD, dtype=F32),
             buf(length, PAD),
-            buf(length, 128, dtype=F32),
-            buf(length, 128, dtype=F32),
-            buf(length, 128, dtype=F32),
-            buf(length, 128, dtype=F32),
+            buf(length, 128),
+            buf(length, 128),
+            buf(length, 128),
+            buf(length, 128),
+            buf(length, 128),
+            buf(length, 128),
             buf(2, length, PAD, dtype=F32),
             buf(2, length, PAD),
             buf(2, length, PAD),
@@ -1620,20 +1788,22 @@
             buf(2, 384, 192),
             buf(8, D, dtype=F32),
             buf(128, PAD, dtype=F32),
-            buf(128, PAD, dtype=F32),
+            buf(128, PAD),
             buf(16, 384, dtype=F32),
             buf(144, 128, dtype=F32),
             buf(8, D, dtype=F32),
             pltpu.SemaphoreType.DMA((16,)),
             pltpu.SemaphoreType.DMA((16,)),
-            pltpu.SemaphoreType.DMA((4,)),
-            buf(CHANNEL_ROWS // 2, 384),
-            buf(CHANNEL_ROWS // 4, 384),
-            buf(CHANNEL_ROWS // 8, 384),
-            buf(CHANNEL_ROWS // 16, 384),
-            pltpu.SemaphoreType.DMA((36,)),
-            pltpu.SemaphoreType.DMA((36,)),
-            pltpu.SemaphoreType.REGULAR((16,)),
+            pltpu.SemaphoreType.DMA((20,)),
+            buf(5, STEP_ROWS[4], 384),
+            pltpu.SemaphoreType.DMA((40,)),
+            pltpu.SemaphoreType.DMA((40,)),
+            pltpu.SemaphoreType.REGULAR((20,)),
+            buf(PART, 384),
+            buf(PART // 2, 384),
+            buf(7, CHUNK, 384),
+            pltpu.SemaphoreType.DMA((42,)),
+            pltpu.SemaphoreType.DMA((42,)),
         ],
         compiler_params=pltpu.CompilerParams(
             collective_id=0, has_side_effects=True, vmem_limit_bytes=63 * 1024 * 1024
@@ -1643,9 +1813,16 @@
         grad_out,
         table_cos,
         table_sin,
-        place_table(length),
-        vectors,
-        filter_vectors,
+        *place_table(length),
+        gainfirst,
+        shiftfirst,
+        gainsecond,
+        shiftsecond,
+        convtaps,
+        posweight,
+        posbias,
+        midbias,
+        sinefreq,
         midweight,
         filterout,
         valueright,
@@ -1661,20 +1838,30 @@
         lowerright,
         lowerleft,
     )
-    hidden_out, hidden_grad, sums_channel, sums_mixer = results
     count = D // (lax.axis_size("wide") * lax.axis_size("narrow"))
-    grads = pl.pallas_call(
+    square = out((192, D), F32)
+    return pl.pallas_call(
         finish_kernel,
         out_shape=(
-            out((8, D), F32),
-            out((192, D), F32),
-            out((192, D), F32),
-            out((192, D), F32),
-            out((192, D), F32),
-            out((144, 128), F32),
+            out((rows, 384)),
+            out((rows, 384)),
+            out((D,), F32),
+            out((D,), F32),
+            square,
+            square,
+            square,
+            square,
+            out((3, D), F32),
+            out((5, 128), F32),
+            out((128,), F32),
+            out((128,), F32),
+            out((128, 128), F32),
+            out((128,), F32),
             out((128, count), F32),
-            out((192, D), F32),
-            out((192, D), F32),
+            square,
+            square,
+            out((D,), F32),
+            out((D,), F32),
             out(gateright.shape, F32),
             out(gateleft.shape, F32),
             out(liftright.shape, F32),
@@ -1682,29 +1869,23 @@
             out(lowerright.shape, F32),
             out(lowerleft.shape, F32),
         ),
-        in_specs=[vmem] * 2,
-        out_specs=[vmem] * 15,
-        compiler_params=pltpu.CompilerParams(vmem_limit_bytes=32 * 1024 * 1024),
-    )(sums_channel, sums_mixer)
-    grad_vectors, grad_filter = grads[0], grads[5]
-    return (
-        hidden_out,
-        hidden_grad,
-        grad_vectors[0],
-        grad_vectors[1],
-        *grads[1:5],
-        grad_vectors[4:7],
-        grad_filter[128:133],
-        grad_filter[136],
-        grad_filter[138],
-        grad_filter[:128],
-        grad_filter[137],
-        grads[6],
-        *grads[7:9],
-        grad_vectors[2],
-        grad_vectors[3],
-        *grads[9:],
-    )
+        in_specs=[vmem] * 2 + [hbm] * 2,
+        out_specs=[vmem] * 19 + [hbm] * 6,
+        scratch_shapes=[
+            buf(CHANNEL_ROWS, 384),
+            buf(2, 2 * PART, 384),
+            buf(*gateright.shape, dtype=F32),
+            buf(*gateleft.shape, dtype=F32),
+            buf(*liftright.shape, dtype=F32),
+            buf(*liftleft.shape, dtype=F32),
+            buf(*lowerright.shape, dtype=F32),
+            buf(*lowerleft.shape, dtype=F32),
+            buf(144, 128, dtype=F32),
+            pltpu.SemaphoreType.DMA((5,)),
+            pltpu.SemaphoreType.DMA((6,)),
+        ],
+        compiler_params=pltpu.CompilerParams(vmem_limit_bytes=60 * 1024 * 1024),
+    )(*results)
 
 
 def solution(mesh):

time: 165 us -> 139 us (0.84)
  local copies, waits for them, and re-layouts: 15.2 us -> 1.51 us
  Pallas kernels: 149 us -> 137 us
    pallas_call x1, Pallas kernels: 145 us -> 130 us  [pair_body(): pl.pallas_call(whole_kernel, out_shape=(out((rows, 384)), out((rows, 384)...]
    unnamed x11 -> x0, local copies, waits for them, and re-layouts: 5.49 us -> none
    concatenate x2 -> x0, local copies, waits for them, and re-layouts: 3.92 us -> none  [the longest x1 2.58 us: pair_body(): jnp.concatenate([posweight, jnp.zeros((3, 128), F32), jnp.stack([posbias,...]
    pallas_call x1, Pallas kernels: 3.88 us -> 7.36 us  [pair_body(): pl.pallas_call(finish_kernel, out_shape=(out((rows, 384)), out((rows, 384...]
    another operation x4 -> x0, local copies, waits for them, and re-layouts: 2.76 us -> none  [pair_body(): jnp.stack([gainfirst, shiftfirst, gainsecond, shiftsecond])]
    slice x4 -> x0, local copies, waits for them, and re-layouts: 2.46 us -> none  [the longest x1 0.63 us: pair_body(): grad_filter[:128]]
where the time goes in v2:
time: 139 us
  Pallas kernels  137 us (99%)
  local copies, waits for them, and re-layouts  1.51 us (1%)
    pallas_call x1, Pallas kernels, pair_body(): pl.pallas_call(whole_kernel, out_shape=(out((rows, 384)), out((rows, 384)...  130 us
    pallas_call x1, Pallas kernels, pair_body(): pl.pallas_call(finish_kernel, out_shape=(out((rows, 384)), out((rows, 384...  7.36 us

profile of v2, /device:TPU:0, one launch (start us, length us, event | category | flops | bytes accessed | tf_op | source)
XLA Modules:
  0.0 139.1 jit_solution(16460721017281774731)
XLA Ops:
  0.7 129.6 %shard_map.468 = (bf16[512,384]{1,0:T(8,128)(2,1)}, bf16[512,384]{1,0:T(8,128)(2,1)}, bf16[3072,384]{1,0:T(8,128)(2,1)}, bf16[2,1536,384]{2,1,0:T(8,128)(2,1)}) custom-call(bf16[512,768]{1,0:T(8,128)(2,1)} %hidden_in.1, bf16[512,384]{1,0:T(8,128)(2,1)} %upstream.1, bf16[1024,1024]{1,0:T(8,128)(2,1)} %constant.8.clone.hbm_cos, ...), custom_call_target="tpu_custom_call" | custom-call | tf_op jit(solution)/shard_map/pallas_call | solution.py:1709
  130.3 7.4 %shard_map.469 = (bf16[512,384]{1,0:T(8,128)(2,1)}, bf16[512,384]{1,0:T(8,128)(2,1)}, f32[768]{0:T(1024)}, f32[768]{0:T(1024)}, f32[192,768]{1,0:T(8,128)}, /*in...) custom-call(bf16[512,384]{1,0:T(8,128)(2,1)} %get-tuple-element.29.h, ...), custom_call_target="tpu_custom_call" | custom-call | tf_op jit(solution)/shard_map/pallas_call | solution.py:1843
  137.6 1.5 %copy.54 = f32[128,24]{0,1:T(8,128)} copy(f32[128,24]{1,0:T(8,128)} %get-tuple-element.47) | data formatting | bytes 24576 | tf_op jit(solution)/shard_map/pallas_call | solution.py:1843

commit v3 on v2

--- a/solution.py
+++ b/solution.py
@@ -1044,6 +1044,11 @@
             term = mm(product, w_out_first[k * PAD : k * PAD + PAD, :])
             inner = term if inner is None else inner + term
         inner_out[narrow, at, :] = inner.astype(BF16)
+
+        @pl.when(order == 1)
+        def _():
+            inner_copy(narrow).wait_send()
+
         inner_copy(index).start()
 
     up_copy.wait_recv()
@@ -1118,16 +1123,6 @@
             dn_send[...] = dn_own[...].astype(BF16)
             dn_copy.start()
 
-    @pl.loop(0, tiles)
-    def _(index):
-        part_copy(index).start()
-
-    for side in range(2):
-        columns = slice(384 * side, 384 * side + 384)
-        folded = fold(mm_tn(inner_lower[...], up_halves[side]), side)
-        for b in range(2):
-            first_row = LOWER_LEFT + 96 * side + 48 * b
-            sums_channel[first_row : first_row + 48, :] = folded[b].astype(BF16)
     low_lanes = lanes(128) < 64
     for columns in (slice(0, 384), slice(384, 768)):
         columns_at = slice(LOWER_RIGHT + columns.start, LOWER_RIGHT + columns.stop)
@@ -1139,6 +1134,23 @@
             low_lanes, parts[0][:, 128:256], parts[1][:, 0:128]
         ).astype(BF16)
         sums_channel[columns_at, 256:384] = parts[1][:, 128:256].astype(BF16)
+    scatter(0, 0).start()
+    for side in range(2):
+        columns = slice(384 * side, 384 * side + 384)
+        folded = fold(mm_tn(inner_lower[...], up_halves[side]), side)
+        for b in range(2):
+            first_row = LOWER_LEFT + 96 * side + 48 * b
+            sums_channel[first_row : first_row + 48, :] = folded[b].astype(BF16)
+    for offset, target in ((0, GATE_RIGHT), (384, LIFT_RIGHT)):
+        whole = mm_tn(norm_two[...], d_inner_glu[:, offset : offset + 384])
+        total = None
+        for b in range(4):
+            term = whole[192 * b : 192 * b + 192, :] * mask(
+                (inside >= 48 * b) & (inside < 48 * b + 48), F32
+            )
+            total = term if total is None else total + term
+        sums_channel[target : target + 192, :] = total.astype(BF16)
+
     for offset, upper, target in ((0, d_gate, GATE_LEFT), (384, d_lift, LIFT_LEFT)):
         for k in range(2):
             for start in (0, 384):
@@ -1150,23 +1162,16 @@
                 sums_channel[first_row : first_row + 192, :] = whole[
                     64 * k : 64 * k + 192, :
                 ].astype(BF16)
-    for offset, target in ((0, GATE_RIGHT), (384, LIFT_RIGHT)):
-        whole = mm_tn(norm_two[...], d_inner_glu[:, offset : offset + 384])
-        total = None
-        for b in range(4):
-            term = whole[192 * b : 192 * b + 192, :] * mask(
-                (inside >= 48 * b) & (inside < 48 * b + 48), F32
-            )
-            total = term if total is None else total + term
-        sums_channel[target : target + 192, :] = total.astype(BF16)
-
+        if upper is d_gate:
+            scatter(1, 0).start()
     sums_channel[2880:3072, :] = jnp.zeros((192, 384), BF16)
-    for i in range(4):
-        scatter(i, 0).start()
+    scatter(2, 0).start()
+    scatter(3, 0).start()
 
     dn_copy.wait_recv()
     into = dn_own[...] + dn_recv[...].astype(F32)
     hat = hat_two[...]
+    gain_sums[...] = jnp.zeros(gain_sums.shape, F32)
     gain_sums[0:1, :] = jnp.sum(into * hat, axis=0, keepdims=True)
     gain_sums[1:2, :] = jnp.sum(into, axis=0, keepdims=True)
     scaled = into * gain_second
@@ -1181,10 +1186,16 @@
     cross_send[...] = mm_nt(branch[...], w_out_second[1 - narrow]).astype(BF16)
     cross_copy.start()
     mid_send[...] = hat_two[:, other_half].astype(BF16)
-    middle_copy.start()
     d_inner_out[own_rows, :] = mm_nt(branch[...], w_out_second[narrow]).astype(BF16)
     for i in range(4):
         advance(i, 0)
+    for h in range(2):
+        for side in range(2):
+            columns = slice(384 * side, 384 * side + 384)
+            folded = fold(mm_tn(inner_out[h, own_rows, :], branch[:, columns]), side)
+            for b in range(2):
+                first_row = OUT_LEFT + 192 * h + 96 * side + 48 * b
+                mixer_slab[first_row : first_row + 48, :] = folded[b].astype(BF16)
 
     @pl.loop(0, tiles)
     def _(order):
@@ -1194,6 +1205,7 @@
         @pl.when(order == 1)
         def _():
             cross_copy.wait_recv()
+            middle_copy.start()
 
         d_inner = d_inner_out[at, :]
         for k in range(2):
@@ -1215,13 +1227,13 @@
         ).astype(BF16)
         shape_copy(index).start()
 
-    for h in range(2):
-        for side in range(2):
-            columns = slice(384 * side, 384 * side + 384)
-            folded = fold(mm_tn(inner_out[h, own_rows, :], branch[:, columns]), side)
-            for b in range(2):
-                first_row = OUT_LEFT + 192 * h + 96 * side + 48 * b
-                mixer_slab[first_row : first_row + 48, :] = folded[b].astype(BF16)
+    @pl.loop(0, tiles)
+    def _(index):
+        part_copy(index).start()
+
+    advance(1, 1)
+    advance(0, 1)
+
     lane = lax.broadcasted_iota(jnp.int32, (2 * PAD, 384), 1)
     row = lax.broadcasted_iota(jnp.int32, (2 * PAD, 384), 0)
     squeeze = mask(row == lane + jnp.where(lane >= 192, 64, 0))
@@ -1258,6 +1270,9 @@
     late[OUT_RIGHT : OUT_RIGHT + 192, :] = jnp.where(
         lanes(384) < 192, parts[0][0:192, :], parts[1][0:192, :]
     ).astype(BF16)
+    advance(2, 1)
+    advance(1, 2)
+    advance(0, 2)
 
     dl_copy.wait_recv()
 
@@ -1280,6 +1295,11 @@
         sig_spec[0, at, :] = (both_re * turn_cos - both_im * turn_sin).astype(BF16)
         sig_spec[1, at, :] = (both_im * turn_cos + both_re * turn_sin).astype(BF16)
 
+    advance(4, 0)
+    advance(3, 1)
+    advance(1, 3)
+    advance(2, 2)
+    advance(0, 3)
     ds_pad[length : length + 8, :] = jnp.zeros((8, PAD), F32)
 
     @pl.loop(0, spans)
@@ -1299,9 +1319,10 @@
     ds_copy.start()
     ds_halves[core] = long_rows[core]
 
-    advance(4, 0)
-    advance(1, 1)
-    advance(0, 1)
+    advance(3, 2)
+    advance(2, 3)
+    retreat(1, 3)
+    retreat(0, 3)
     grad_vectors[...] = jnp.zeros(grad_vectors.shape, F32)
     sums = [jnp.zeros((1, PAD), F32) for _ in range(3)]
     for index in range(spans):
@@ -1321,8 +1342,7 @@
     d_lin[...] = jnp.zeros(d_lin.shape, F32)
     grad_filter[...] = jnp.zeros(grad_filter.shape, F32)
 
-    @pl.loop(0, spans)
-    def _(index):
+    def filter_back(index):
         at = tile_rows(index)
         d_taps = mm(table_cos[at, :], sig_spec[0]) + mm(table_sin[at, :], sig_spec[1])
         d_mod = d_taps * decay(index)
@@ -1341,14 +1361,21 @@
             one * lin_one[at, :].astype(F32) + two * lin_two[at, :].astype(F32), axis=0, keepdims=True
         )
 
+    pl.loop(0, spans // 2)(filter_back)
+    advance(4, 1)
+    retreat(1, 2)
+    pl.loop(spans // 2, spans)(filter_back)
     late[FILTER_OUT : FILTER_OUT + 128, :] = mm(d_lin[...].astype(BF16), place_core).astype(BF16)
     for i in range(3):
         late[FILTER : FILTER + 48, 128 * i : 128 * i + 128] = grad_filter[
             48 * i : 48 * i + 48, :
         ].astype(BF16)
 
-    advance(2, 1)
-    advance(1, 2)
+
+    advance(4, 2)
+    advance(3, 3)
+    retreat(0, 2)
+    retreat(2, 3)
 
     ds_copy.wait_recv()
     other_blocks = pl.ds(pl.multiple_of((1 - narrow) * 192, 192), 192)
@@ -1373,14 +1400,44 @@
         value_send[at, 192:256] = tail[:, 64:128].astype(BF16)
         value_copy(index).start()
 
-    advance(3, 1)
-    advance(0, 2)
+    @pl.loop(0, tiles)
+    def _(index):
+        at = tile_rows(index)
+        into = mm_nt(d_inner_one[at, :], w_first[...])
+        hat = (inputs[at, :].astype(F32) - stats[at, 0:1]) * stats[at, 1:2]
+        gain_sums[2:3, :] += jnp.sum(into * hat, axis=0, keepdims=True)
+        gain_sums[3:4, :] += jnp.sum(into, axis=0, keepdims=True)
+
+    advance(4, 3)
+    retreat(3, 3)
     late[VALUE_RIGHT : VALUE_RIGHT + 192, :] = first_gradient(0)
     late[VALUE_LEFT : VALUE_LEFT + 192, :] = second_gradient(0, ds_halves)
-    advance(4, 1)
-    advance(1, 3)
-    advance(2, 2)
-    advance(0, 3)
+    grad_vectors[0:4, :] = gain_sums[0:4, 0:384]
+    grad_vectors[8:12, :] = gain_sums[0:4, 384:768]
+    late[VECTORS : VECTORS + 16, :] = grad_vectors[...].astype(BF16)
+
+    to_core = late_copy(
+        late.at[pl.ds(pl.multiple_of((1 - core) * 384, 16), 384)], late_core, sibling, 0
+    )
+    to_core.start()
+    retreat(4, 3)
+    to_core.wait()
+
+    @pl.loop(0, 384 // CHUNK)
+    def _(index):
+        at = pl.ds(pl.multiple_of(core * 384 + index * CHUNK, 16), CHUNK)
+        came = late_core[pl.ds(pl.multiple_of(index * CHUNK, 16), CHUNK), :]
+        late[at, :] = (late[at, :].astype(F32) + came.astype(F32)).astype(BF16)
+
+    def share(t):
+        return pl.multiple_of(core * 384 + lax.rem(chip + 8 - t, 8) * CHUNK, 16)
+
+    direct = [
+        late_copy(late.at[pl.ds(share(8 - t), CHUNK)], late_slots.at[t - 1], fellows[t], t)
+        for t in range(1, 8)
+    ]
+    for copy in direct:
+        copy.start()
 
     first_half = vectors[0:1, own_half]
     middle_copy.wait_recv()
@@ -1399,45 +1456,13 @@
         plain = (stats[at, 2:3] + value_recv[at, 192:193].astype(F32)) * (1.0 / D)
         along = (stats[at, 3:4] + value_recv[at, 193:194].astype(F32)) * (1.0 / D)
         hat = (inputs[at, own_half].astype(F32) - stats[at, 0:1]) * stats[at, 1:2]
-        grad_vectors[0:1, :] += jnp.sum(into * hat, axis=0, keepdims=True)
-        grad_vectors[1:2, :] += jnp.sum(into, axis=0, keepdims=True)
         hidden_grad[at, :] = (
             d_middle[at, :] + stats[at, 1:2] * (into * first_half - plain - hat * along)
         ).astype(BF16)
 
-    grad_vectors[2:4, :] = gain_sums[0:2, 0:384]
-    grad_vectors[8:10, :] = gain_sums[0:2, 384:768]
-    late[VECTORS : VECTORS + 16, :] = grad_vectors[...].astype(BF16)
-
-    core_rows = pl.ds(pl.multiple_of(core * 384, 16), 384)
-    to_core = late_copy(
-        late.at[pl.ds(pl.multiple_of((1 - core) * 384, 16), 384)], late_core, sibling, 0
-    )
-    to_core.start()
-    advance(3, 2)
-    advance(4, 2)
-    to_core.wait()
-
-    @pl.loop(0, 384 // CHUNK)
-    def _(index):
-        at = pl.ds(pl.multiple_of(core * 384 + index * CHUNK, 16), CHUNK)
-        came = late_core[pl.ds(pl.multiple_of(index * CHUNK, 16), CHUNK), :]
-        late[at, :] = (late[at, :].astype(F32) + came.astype(F32)).astype(BF16)
-
-    def share(t):
-        return pl.multiple_of(core * 384 + lax.rem(chip + 8 - t, 8) * CHUNK, 16)
-
-    direct = [
-        late_copy(late.at[pl.ds(share(8 - t), CHUNK)], late_slots.at[t - 1], fellows[t], t)
-        for t in range(1, 8)
-    ]
-    for copy in direct:
-        copy.start()
-    advance(2, 3)
-    retreat(1, 3)
-    advance(3, 3)
-    advance(4, 3)
-    retreat(0, 3)
+    retreat(4, 2)
+    retreat(1, 1)
+    retreat(0, 1)
     total = late[pl.ds(share(0), CHUNK), :].astype(F32)
     for t in range(1, 8):
         direct[t - 1].wait()
@@ -1450,11 +1475,12 @@
     ]
     for copy in spread_out:
         copy.start()
-    retreat(2, 3)
-    retreat(1, 2)
-    retreat(0, 2)
-    retreat(3, 3)
-    retreat(4, 3)
+    retreat(4, 1)
+    early_rows = pl.ds(offsets[4][1], PART // 2)
+    across_early = late_copy(mixer_slab.at[early_rows], mixer_slab.at[early_rows], partner, 40)
+    across_early.start()
+    retreat(2, 2)
+    retreat(3, 2)
     across = []
     along_own = []
     for t in range(8):
@@ -1465,17 +1491,11 @@
         across[t].start()
         along_own.append(late_copy(mixer_slab.at[at], mixer_slab.at[at], sibling, 24 + t))
         along_own[t].start()
-    retreat(1, 1)
-    retreat(2, 2)
-    retreat(0, 1)
-    retreat(3, 2)
-    retreat(4, 2)
+    across_early.wait()
+    other = sums_mixer.at[1 - narrow, early_rows]
+    along_early = late_copy(other, other, sibling, 41)
+    along_early.start()
     retreat(2, 1)
-    retreat(3, 1)
-    retreat(4, 1)
-    early_rows = pl.ds(offsets[4][1], PART // 2)
-    across_early = late_copy(mixer_slab.at[early_rows], mixer_slab.at[early_rows], partner, 40)
-    across_early.start()
     along_other = []
     for t in range(8):
         across[t].wait()
@@ -1483,22 +1503,19 @@
         other = sums_mixer.at[1 - narrow, at]
         along_other.append(late_copy(other, other, sibling, 32 + t))
         along_other[t].start()
-    for i in range(4):
+    retreat(3, 1)
+    for i in range(5):
         retreat(i, 0)
-    across_early.wait()
-    other = sums_mixer.at[1 - narrow, early_rows]
-    along_early = late_copy(other, other, sibling, 41)
-    along_early.start()
-    retreat(4, 0)
     for copy in along_own + along_other + [along_early]:
         copy.wait()
 
+    inner_copy(1 - narrow).wait_send()
     for copy in (up_copy, dl_copy, ds_copy, dn_copy, cross_copy, middle_copy):
         copy.wait_send()
 
     @pl.loop(0, tiles)
     def _(index):
-        for copy in (inner_copy, part_copy, shape_copy, value_copy):
+        for copy in (part_copy, shape_copy, value_copy):
             copy(index).wait_send()
 
 
@@ -1610,11 +1627,9 @@
     vectors = [mixer[h, PART + VECTORS : PART + VECTORS + 16, :].astype(F32) for h in range(2)]
     whole = jnp.concatenate(vectors, axis=1)
     both = vectors[0] + vectors[1]
-    grad_gainfirst[...] = whole[0:1, :].reshape(D)
-    grad_shiftfirst[...] = whole[1:2, :].reshape(D)
     grad_convtaps[...] = whole[4:7, :]
-    grad_gainsecond[...] = jnp.concatenate([both[2:3, :], both[8:9, :]], axis=1).reshape(D)
-    grad_shiftsecond[...] = jnp.concatenate([both[3:4, :], both[9:10, :]], axis=1).reshape(D)
+    for i, target in enumerate((grad_gainsecond, grad_shiftsecond, grad_gainfirst, grad_shiftfirst)):
+        target[...] = jnp.concatenate([both[i : i + 1, :], both[8 + i : 9 + i, :]], axis=1).reshape(D)
     for i in range(3):
         columns = slice(128 * i, 128 * i + 128)
         at = slice(PART + FILTER, PART + FILTER + 48)
@@ -1626,15 +1641,15 @@
     grad_posbias[...] = both_filter[136:137, :].reshape(128)
     grad_midbias[...] = both_filter[137:138, :].reshape(128)
     grad_sinefreq[...] = both_filter[138:139, :].reshape(128)
-    count = grad_filterout.shape[1]
+    count = grad_filterout.shape[0]
     first = (lax.axis_index("wide") * 2 + lax.axis_index("narrow")) * count
     total = jnp.zeros(grad_filterout.shape, F32)
-    row = lax.broadcasted_iota(jnp.int32, (384, count), 0)
-    lane = lax.broadcasted_iota(jnp.int32, (384, count), 1)
+    row = lax.broadcasted_iota(jnp.int32, (count, 384), 0)
+    lane = lax.broadcasted_iota(jnp.int32, (count, 384), 1)
     for h in range(2):
-        total += mm(
+        total += mm_nt(
+            mask(lane + 384 * h == first + row),
             mixer[h, PART + FILTER_OUT : PART + FILTER_OUT + 128, :],
-            mask(row + 384 * h == first + lane),
         )
     grad_filterout[...] = total
     for copy in outs:
@@ -1840,7 +1855,7 @@
     )
     count = D // (lax.axis_size("wide") * lax.axis_size("narrow"))
     square = out((192, D), F32)
-    return pl.pallas_call(
+    grads = pl.pallas_call(
         finish_kernel,
         out_shape=(
             out((rows, 384)),
@@ -1857,7 +1872,7 @@
             out((128,), F32),
             out((128, 128), F32),
             out((128,), F32),
-            out((128, count), F32),
+            out((count, 128), F32),
             square,
             square,
             out((D,), F32),
@@ -1886,6 +1901,7 @@
         ],
         compiler_params=pltpu.CompilerParams(vmem_limit_bytes=60 * 1024 * 1024),
     )(*results)
+    return (*grads[:14], grads[14].T, *grads[15:])
 
 
 def solution(mesh):

time: 139 us -> 117 us (0.84)
  Pallas kernels: 137 us -> 116 us
  local copies, waits for them, and re-layouts: 1.51 us -> 0 us
    pallas_call x1, Pallas kernels: 130 us -> 109 us  [pair_body(): pl.pallas_call(whole_kernel, out_shape=(out((rows, 384)), out((rows, 384)...]
    pallas_call x1 -> x0, local copies, waits for them, and re-layouts: 1.51 us -> none  [pair_body(): pl.pallas_call(finish_kernel, out_shape=(out((rows, 384)), out((rows, 384...]
where the time goes in v3:
time: 117 us
  Pallas kernels  116 us (99%)
    pallas_call x1, Pallas kernels, pair_body(): pl.pallas_call(whole_kernel, out_shape=(out((rows, 384)), out((rows, 384)...  109 us
    pallas_call x1, Pallas kernels, pair_body(): pl.pallas_call(finish_kernel, out_shape=(out((rows, 384)), out((rows, 384...  7.32 us

profile of v3, /device:TPU:0, one launch (start us, length us, event | category | flops | bytes accessed | tf_op | source)
XLA Modules:
  0.0 117.3 jit_solution(14783103983972663819)
XLA Ops:
  0.7 109.1 %shard_map.468 = (bf16[512,384]{1,0:T(8,128)(2,1)}, bf16[512,384]{1,0:T(8,128)(2,1)}, bf16[3072,384]{1,0:T(8,128)(2,1)}, bf16[2,1536,384]{2,1,0:T(8,128)(2,1)}) custom-call(bf16[512,768]{1,0:T(8,128)(2,1)} %hidden_in.1, bf16[512,384]{1,0:T(8,128)(2,1)} %upstream.1, bf16[1024,1024]{1,0:T(8,128)(2,1)} %constant.8.clone.hbm_cos, ...), custom_call_target="tpu_custom_call" | custom-call | tf_op jit(solution)/shard_map/pallas_call | solution.py:1724
  109.8 7.3 %shard_map.469 = (bf16[512,384]{1,0:T(8,128)(2,1)}, bf16[512,384]{1,0:T(8,128)(2,1)}, f32[768]{0:T(1024)}, f32[768]{0:T(1024)}, f32[192,768]{1,0:T(8,128)}, /*in...) custom-call(bf16[512,384]{1,0:T(8,128)(2,1)} %get-tuple-element.54.h, ...), custom_call_target="tpu_custom_call" | custom-call | tf_op jit(solution)/shard_map/pallas_call | solution.py:1858

commit v4 on v3

--- a/solution.py
+++ b/solution.py
@@ -584,10 +584,15 @@
     liftleft,
     lowerright,
     lowerleft,
+    result_out,
+    result_grad,
+    result_channel,
+    result_mixer,
     hidden_out,
     hidden_grad,
     sums_channel,
     sums_mixer,
+    store_sem,
     inputs,
     table_cos,
     table_sin,
@@ -717,6 +722,12 @@
         load(("lift", k), liftleft.at[:, pl.ds(D * k, D)], w_lift.at[k, at])
     load("upstream", upstream, up_halves.at[narrow])
 
+    stores = []
+
+    def store(source, target):
+        stores.append(pltpu.make_async_copy(source, target, store_sem.at[len(stores)]))
+        stores[-1].start()
+
     barrier = pltpu.get_barrier_semaphore()
     others = [(wide + stride * (1 - 2 * bit), narrow) for stride, bit in zip(STRIDES, bits)]
     chip = wide // 2
@@ -732,8 +743,6 @@
     filter_vectors[0:5, :] = posweight[...]
     for i, source in enumerate((posbias, midbias, sinefreq)):
         filter_vectors[8 + i : 9 + i, :] = source[...].reshape(1, 128)
-
-    pl.semaphore_wait(barrier, 9)
 
     def send(source, target, device, index):
         return pltpu.make_async_remote_copy(
@@ -814,9 +823,6 @@
             device_id=device,
             device_id_type=MESH,
         )
-
-    up_copy = send(upstream, up_halves.at[narrow], partner, 0)
-    up_copy.start()
 
     row = lax.broadcasted_iota(jnp.int32, (D, 384), 0)
     lane = lax.broadcasted_iota(jnp.int32, (D, 384), 1)
@@ -879,8 +885,11 @@
         shaping[0, at, :] = shaped[:, :PAD]
         shaping[1, at, :] = shaped[:, PAD:]
 
+    pl.semaphore_wait(barrier, 9)
     sig_copy = send(sig_halves.at[1 - core], sig_rows.at[core], sibling, 1)
     sig_copy.start()
+    up_copy = send(upstream, up_halves.at[narrow], partner, 0)
+    up_copy.start()
     sig_rows[core] = sig_halves[core]
 
     row = lax.broadcasted_iota(jnp.int32, (D, PAD), 0)
@@ -997,15 +1006,22 @@
 
     per_half = rows // TILE
 
-    @pl.loop(0, spans)
+    def long_tile(part, index):
+        at = tile_rows(part * per_half + index)
+        result = mm(table_cos[at, :], prod_spec[0]) + mm(table_sin[at, :], prod_spec[1])
+        return result.astype(BF16)
+
+    @pl.loop(0, per_half)
     def _(index):
-        at = tile_rows(index)
-        result = mm(table_cos[at, :], prod_spec[0]) + mm(table_sin[at, :], prod_spec[1])
-        long_rows[index // per_half, tile_rows(lax.rem(index, per_half)), :] = result.astype(BF16)
+        long_rows[1 - core, tile_rows(index), :] = long_tile(1 - core, index)
 
     long_copy = send(long_rows.at[1 - core], long_halves.at[core], sibling, 2)
     long_copy.start()
-    long_halves[core] = long_rows[core]
+
+    @pl.loop(0, per_half)
+    def _(index):
+        long_halves[core, tile_rows(index), :] = long_tile(core, index)
+
     long_copy.wait_recv()
     sig_copy.wait_send()
     long_copy.wait_send()
@@ -1319,6 +1335,7 @@
     ds_copy.start()
     ds_halves[core] = long_rows[core]
 
+    advance(4, 1)
     advance(3, 2)
     advance(2, 3)
     retreat(1, 3)
@@ -1362,8 +1379,7 @@
         )
 
     pl.loop(0, spans // 2)(filter_back)
-    advance(4, 1)
-    retreat(1, 2)
+    advance(4, 2)
     pl.loop(spans // 2, spans)(filter_back)
     late[FILTER_OUT : FILTER_OUT + 128, :] = mm(d_lin[...].astype(BF16), place_core).astype(BF16)
     for i in range(3):
@@ -1372,8 +1388,9 @@
         ].astype(BF16)
 
 
-    advance(4, 2)
+    advance(4, 3)
     advance(3, 3)
+    retreat(1, 2)
     retreat(0, 2)
     retreat(2, 3)
 
@@ -1408,7 +1425,7 @@
         gain_sums[2:3, :] += jnp.sum(into * hat, axis=0, keepdims=True)
         gain_sums[3:4, :] += jnp.sum(into, axis=0, keepdims=True)
 
-    advance(4, 3)
+    retreat(4, 3)
     retreat(3, 3)
     late[VALUE_RIGHT : VALUE_RIGHT + 192, :] = first_gradient(0)
     late[VALUE_LEFT : VALUE_LEFT + 192, :] = second_gradient(0, ds_halves)
@@ -1420,7 +1437,7 @@
         late.at[pl.ds(pl.multiple_of((1 - core) * 384, 16), 384)], late_core, sibling, 0
     )
     to_core.start()
-    retreat(4, 3)
+    retreat(4, 2)
     to_core.wait()
 
     @pl.loop(0, 384 // CHUNK)
@@ -1460,9 +1477,14 @@
             d_middle[at, :] + stats[at, 1:2] * (into * first_half - plain - hat * along)
         ).astype(BF16)
 
-    retreat(4, 2)
+    retreat(4, 1)
+    early_rows = pl.ds(offsets[4][1], PART // 2)
+    across_early = late_copy(mixer_slab.at[early_rows], mixer_slab.at[early_rows], partner, 40)
+    across_early.start()
     retreat(1, 1)
     retreat(0, 1)
+    store(hidden_out, result_out)
+    store(hidden_grad, result_grad)
     total = late[pl.ds(share(0), CHUNK), :].astype(F32)
     for t in range(1, 8):
         direct[t - 1].wait()
@@ -1475,10 +1497,6 @@
     ]
     for copy in spread_out:
         copy.start()
-    retreat(4, 1)
-    early_rows = pl.ds(offsets[4][1], PART // 2)
-    across_early = late_copy(mixer_slab.at[early_rows], mixer_slab.at[early_rows], partner, 40)
-    across_early.start()
     retreat(2, 2)
     retreat(3, 2)
     across = []
@@ -1504,10 +1522,18 @@
         along_other.append(late_copy(other, other, sibling, 32 + t))
         along_other[t].start()
     retreat(3, 1)
-    for i in range(5):
+    for i in (1, 0, 2, 3):
         retreat(i, 0)
-    for copy in along_own + along_other + [along_early]:
+        at = pl.ds(PART * i, PART)
+        store(sums_channel.at[at], result_channel.at[at])
+    retreat(4, 0)
+    along_early.wait()
+    early = pl.ds(0, PART)
+    store(sums_mixer.at[:, early], result_mixer.at[:, early])
+    for copy in along_own + along_other:
         copy.wait()
+    rest = pl.ds(PART, PART)
+    store(sums_mixer.at[:, rest], result_mixer.at[:, rest])
 
     inner_copy(1 - narrow).wait_send()
     for copy in (up_copy, dl_copy, ds_copy, dn_copy, cross_copy, middle_copy):
@@ -1517,6 +1543,9 @@
     def _(index):
         for copy in (part_copy, shape_copy, value_copy):
             copy(index).wait_send()
+
+    for copy in stores:
+        copy.wait()
 
 
 def finish_kernel(
@@ -1551,6 +1580,14 @@
     grad_lowerleft,
     channel,
     mixer,
+    pass_out,
+    pass_grad,
+    valueright,
+    valueleft,
+    shaperight,
+    shapeleft,
+    outright,
+    outleft,
     gateright,
     gateleft,
     liftright,
@@ -1576,8 +1613,8 @@
         at = pl.ds(PART * i, PART)
         fetch(hbm_channel.at[at], channel.at[at])
     fetch(hbm_mixer, mixer)
-    hidden_out[...] = hidden_in[...]
-    hidden_grad[...] = hidden_grad_in[...]
+    fetch(hidden_in, pass_out)
+    fetch(hidden_grad_in, pass_grad)
 
     ins[0].wait()
     lowerright[...] = channel[LOWER_RIGHT : LOWER_RIGHT + D, :].astype(F32)
@@ -1607,23 +1644,29 @@
     row = lax.broadcasted_iota(jnp.int32, (384, D), 0)
     step = jnp.where(row >= 96, 96, 0) + jnp.where(row >= 192, 96, 0) + jnp.where(row >= 288, 96, 0)
     unselect = [mask(lane == row + step + 96 * h) for h in range(2)]
-    for first_row, target in ((PART + VALUE_RIGHT, grad_valueright), (SHAPE_RIGHT, grad_shaperight)):
+    for first_row, target, result in (
+        (PART + VALUE_RIGHT, valueright, grad_valueright),
+        (SHAPE_RIGHT, shaperight, grad_shaperight),
+    ):
         target[...] = mm(mixer[0, first_row : first_row + 192, :], unselect[0]) + mm(
             mixer[1, first_row : first_row + 192, :], unselect[1]
         )
+        store(target, result)
+    for first_row, target, result in (
+        (PART + OUT_RIGHT, outright, grad_outright),
+        (SHAPE_LEFT, shapeleft, grad_shapeleft),
+        (PART + VALUE_LEFT, valueleft, grad_valueleft),
+    ):
+        for h in range(2):
+            target[:, 384 * h : 384 * h + 384] = mixer[h, first_row : first_row + 192, :].astype(F32)
+        store(target, result)
     for h in range(2):
-        columns = slice(384 * h, 384 * h + 384)
-        for first_row, target in (
-            (PART + OUT_RIGHT, grad_outright),
-            (SHAPE_LEFT, grad_shapeleft),
-            (PART + VALUE_LEFT, grad_valueleft),
-        ):
-            target[:, columns] = mixer[h, first_row : first_row + 192, :].astype(F32)
         for side in range(2):
             at = slice(OUT_LEFT + 192 * h + 96 * side, OUT_LEFT + 192 * h + 96 * side + 96)
-            grad_outleft[96 * h : 96 * h + 96, 384 * side : 384 * side + 384] = mixer[
-                0, at, :
-            ].astype(F32) + mixer[1, at, :].astype(F32)
+            outleft[96 * h : 96 * h + 96, 384 * side : 384 * side + 384] = mixer[0, at, :].astype(
+                F32
+            ) + mixer[1, at, :].astype(F32)
+    store(outleft, grad_outleft)
     vectors = [mixer[h, PART + VECTORS : PART + VECTORS + 16, :].astype(F32) for h in range(2)]
     whole = jnp.concatenate(vectors, axis=1)
     both = vectors[0] + vectors[1]
@@ -1652,6 +1695,10 @@
             mixer[h, PART + FILTER_OUT : PART + FILTER_OUT + 128, :],
         )
     grad_filterout[...] = total
+    ins[5].wait()
+    store(pass_out, hidden_out)
+    ins[6].wait()
+    store(pass_grad, hidden_grad)
     for copy in outs:
         copy.wait()
 
@@ -1730,8 +1777,13 @@
             out((2, 2 * PART, 384)),
         ),
         in_specs=[hbm] * 4 + [vmem] * 12 + [hbm] * 13,
-        out_specs=[vmem] * 4,
+        out_specs=[hbm] * 4,
         scratch_shapes=[
+            buf(rows, 384),
+            buf(rows, 384),
+            buf(CHANNEL_ROWS, 384),
+            buf(2, 2 * PART, 384),
+            pltpu.SemaphoreType.DMA((8,)),
             buf(rows, D),
             buf(length, length),
             buf(length, length),
@@ -1884,11 +1936,14 @@
             out(lowerright.shape, F32),
             out(lowerleft.shape, F32),
         ),
-        in_specs=[vmem] * 2 + [hbm] * 2,
-        out_specs=[vmem] * 19 + [hbm] * 6,
+        in_specs=[hbm] * 4,
+        out_specs=[hbm] * 2 + [vmem] * 2 + [hbm] * 4 + [vmem] * 7 + [hbm] * 2 + [vmem] * 2 + [hbm] * 6,
         scratch_shapes=[
             buf(CHANNEL_ROWS, 384),
             buf(2, 2 * PART, 384),
+            buf(rows, 384),
+            buf(rows, 384),
+            *[buf(192, D, dtype=F32)] * 6,
             buf(*gateright.shape, dtype=F32),
             buf(*gateleft.shape, dtype=F32),
             buf(*liftright.shape, dtype=F32),
@@ -1896,8 +1951,8 @@
             buf(*lowerright.shape, dtype=F32),
             buf(*lowerleft.shape, dtype=F32),
             buf(144, 128, dtype=F32),
-            pltpu.SemaphoreType.DMA((5,)),
-            pltpu.SemaphoreType.DMA((6,)),
+            pltpu.SemaphoreType.DMA((7,)),
+            pltpu.SemaphoreType.DMA((14,)),
         ],
         compiler_params=pltpu.CompilerParams(vmem_limit_bytes=60 * 1024 * 1024),
     )(*results)

time: 117 us -> 112 us (0.957)
  Pallas kernels: 116 us -> 111 us
    pallas_call x1, Pallas kernels: 109 us -> 104 us  [pair_body(): pl.pallas_call(whole_kernel, out_shape=(out((rows, 384)), out((rows, 384)...]
where the time goes in v4:
time: 112 us
  Pallas kernels  111 us (99%)
    pallas_call x1, Pallas kernels, pair_body(): pl.pallas_call(whole_kernel, out_shape=(out((rows, 384)), out((rows, 384)...  104 us
    pallas_call x1, Pallas kernels, pair_body(): pl.pallas_call(finish_kernel, out_shape=(out((rows, 384)), out((rows, 384...  6.54 us

profile of v4, /device:TPU:0, one launch (start us, length us, event | category | flops | bytes accessed | tf_op | source)
XLA Modules:
  0.0 111.7 jit_solution(2666304340290402106)
XLA Ops:
  0.7 104.3 %shard_map.468 = (bf16[512,384]{1,0:T(8,128)(2,1)}, bf16[512,384]{1,0:T(8,128)(2,1)}, bf16[3072,384]{1,0:T(8,128)(2,1)}, bf16[2,1536,384]{2,1,0:T(8,128)(2,1)}) custom-call(bf16[512,768]{1,0:T(8,128)(2,1)} %hidden_in.1, bf16[512,384]{1,0:T(8,128)(2,1)} %upstream.1, bf16[1024,1024]{1,0:T(8,128)(2,1)} %constant.8.clone.hbm_cos, ...), custom_call_target="tpu_custom_call" | custom-call | tf_op jit(solution)/shard_map/pallas_call | solution.py:1771
  105.0 6.5 %shard_map.469 = (bf16[512,384]{1,0:T(8,128)(2,1)}, bf16[512,384]{1,0:T(8,128)(2,1)}, f32[768]{0:T(1024)}, f32[768]{0:T(1024)}, f32[192,768]{1,0:T(8,128)}, /*in...) custom-call(bf16[512,384]{1,0:T(8,128)(2,1)} %get-tuple-element.54.h, ...), custom_call_target="tpu_custom_call" | custom-call | tf_op jit(solution)/shard_map/pallas_call | solution.py:1910

commit v5 on v4

--- a/solution.py
+++ b/solution.py
@@ -1077,6 +1077,12 @@
     shift_second = vectors[3:4, :]
 
     @pl.loop(0, tiles)
+    def _(index):
+        at = tile_rows(index)
+        above = jnp.concatenate([up_halves[0, at, :], up_halves[1, at, :]], axis=1)
+        d_inner_lower[at, :] = mm_nt(above, w_lower_second[...]).astype(BF16)
+
+    @pl.loop(0, tiles)
     def _(order):
         index = first_other(order)
         at = tile_rows(index)
@@ -1113,9 +1119,7 @@
         out_own[at, :] = dn_own[:, own_half] + mm(inner_low, w_lower_second[:, own_half])
         part_send[at, :] = mm(inner_low, w_lower_second[:, other_half]).astype(BF16)
 
-        above = jnp.concatenate([up_halves[0, at, :], up_halves[1, at, :]], axis=1)
-        d_low = mm_nt(above, w_lower_second[...]).astype(BF16)
-        d_inner_lower[at, :] = d_low
+        d_low = d_inner_lower[at, :]
         gates = [None, None]
         lifts = [None, None]
         for k in range(2):

time: 112 us -> 112 us (level)
  no operation moved by 1% of the time
where the time goes in v5:
time: 112 us
  Pallas kernels  111 us (99%)
    pallas_call x1, Pallas kernels, pair_body(): pl.pallas_call(whole_kernel, out_shape=(out((rows, 384)), out((rows, 384)...  104 us
    pallas_call x1, Pallas kernels, pair_body(): pl.pallas_call(finish_kernel, out_shape=(out((rows, 384)), out((rows, 384...  6.54 us

profile of v5, /device:TPU:0, one launch (start us, length us, event | category | flops | bytes accessed | tf_op | source)
XLA Modules:
  0.0 111.5 jit_solution(1410287372859932010)
XLA Ops:
  0.7 104.1 %shard_map.468 = (bf16[512,384]{1,0:T(8,128)(2,1)}, bf16[512,384]{1,0:T(8,128)(2,1)}, bf16[3072,384]{1,0:T(8,128)(2,1)}, bf16[2,1536,384]{2,1,0:T(8,128)(2,1)}) custom-call(bf16[512,768]{1,0:T(8,128)(2,1)} %hidden_in.1, bf16[512,384]{1,0:T(8,128)(2,1)} %upstream.1, bf16[1024,1024]{1,0:T(8,128)(2,1)} %constant.8.clone.hbm_cos, ...), custom_call_target="tpu_custom_call" | custom-call | tf_op jit(solution)/shard_map/pallas_call | solution.py:1775
  104.8 6.5 %shard_map.469 = (bf16[512,384]{1,0:T(8,128)(2,1)}, bf16[512,384]{1,0:T(8,128)(2,1)}, f32[768]{0:T(1024)}, f32[768]{0:T(1024)}, f32[192,768]{1,0:T(8,128)}, /*in...) custom-call(bf16[512,384]{1,0:T(8,128)(2,1)} %get-tuple-element.54.h, ...), custom_call_target="tpu_custom_call" | custom-call | tf_op jit(solution)/shard_map/pallas_call | solution.py:1914

commit v6 on v4

--- a/solution.py
+++ b/solution.py
@@ -1286,9 +1286,6 @@
     late[OUT_RIGHT : OUT_RIGHT + 192, :] = jnp.where(
         lanes(384) < 192, parts[0][0:192, :], parts[1][0:192, :]
     ).astype(BF16)
-    advance(2, 1)
-    advance(1, 2)
-    advance(0, 2)
 
     dl_copy.wait_recv()
 
@@ -1311,11 +1308,11 @@
         sig_spec[0, at, :] = (both_re * turn_cos - both_im * turn_sin).astype(BF16)
         sig_spec[1, at, :] = (both_im * turn_cos + both_re * turn_sin).astype(BF16)
 
+    advance(2, 1)
+    advance(1, 2)
+    advance(0, 2)
     advance(4, 0)
     advance(3, 1)
-    advance(1, 3)
-    advance(2, 2)
-    advance(0, 3)
     ds_pad[length : length + 8, :] = jnp.zeros((8, PAD), F32)
 
     @pl.loop(0, spans)
@@ -1335,11 +1332,12 @@
     ds_copy.start()
     ds_halves[core] = long_rows[core]
 
+    advance(1, 3)
+    advance(2, 2)
+    advance(0, 3)
     advance(4, 1)
     advance(3, 2)
-    advance(2, 3)
     retreat(1, 3)
-    retreat(0, 3)
     grad_vectors[...] = jnp.zeros(grad_vectors.shape, F32)
     sums = [jnp.zeros((1, PAD), F32) for _ in range(3)]
     for index in range(spans):
@@ -1380,6 +1378,8 @@
 
     pl.loop(0, spans // 2)(filter_back)
     advance(4, 2)
+    advance(2, 3)
+    retreat(0, 3)
     pl.loop(spans // 2, spans)(filter_back)
     late[FILTER_OUT : FILTER_OUT + 128, :] = mm(d_lin[...].astype(BF16), place_core).astype(BF16)
     for i in range(3):
@@ -1393,7 +1393,6 @@
     retreat(1, 2)
     retreat(0, 2)
     retreat(2, 3)
-
     ds_copy.wait_recv()
     other_blocks = pl.ds(pl.multiple_of((1 - narrow) * 192, 192), 192)
 
@@ -1477,14 +1476,14 @@
             d_middle[at, :] + stats[at, 1:2] * (into * first_half - plain - hat * along)
         ).astype(BF16)
 
+    store(hidden_out, result_out)
+    store(hidden_grad, result_grad)
     retreat(4, 1)
     early_rows = pl.ds(offsets[4][1], PART // 2)
     across_early = late_copy(mixer_slab.at[early_rows], mixer_slab.at[early_rows], partner, 40)
     across_early.start()
     retreat(1, 1)
     retreat(0, 1)
-    store(hidden_out, result_out)
-    store(hidden_grad, result_grad)
     total = late[pl.ds(share(0), CHUNK), :].astype(F32)
     for t in range(1, 8):
         direct[t - 1].wait()

time: 112 us -> 112 us (level)
  no operation moved by 1% of the time
where the time goes in v6:
time: 112 us
  Pallas kernels  111 us (99%)
    pallas_call x1, Pallas kernels, pair_body(): pl.pallas_call(whole_kernel, out_shape=(out((rows, 384)), out((rows, 384)...  105 us
    pallas_call x1, Pallas kernels, pair_body(): pl.pallas_call(finish_kernel, out_shape=(out((rows, 384)), out((rows, 384...  6.54 us

profile of v6, /device:TPU:0, one launch (start us, length us, event | category | flops | bytes accessed | tf_op | source)
XLA Modules:
  0.0 112.0 jit_solution(16715616223886291015)
XLA Ops:
  0.7 104.6 %shard_map.468 = (bf16[512,384]{1,0:T(8,128)(2,1)}, bf16[512,384]{1,0:T(8,128)(2,1)}, bf16[3072,384]{1,0:T(8,128)(2,1)}, bf16[2,1536,384]{2,1,0:T(8,128)(2,1)}) custom-call(bf16[512,768]{1,0:T(8,128)(2,1)} %hidden_in.1, bf16[512,384]{1,0:T(8,128)(2,1)} %upstream.1, bf16[1024,1024]{1,0:T(8,128)(2,1)} %constant.8.clone.hbm_cos, ...), custom_call_target="tpu_custom_call" | custom-call | tf_op jit(solution)/shard_map/pallas_call | solution.py:1770
  105.3 6.5 %shard_map.469 = (bf16[512,384]{1,0:T(8,128)(2,1)}, bf16[512,384]{1,0:T(8,128)(2,1)}, f32[768]{0:T(1024)}, f32[768]{0:T(1024)}, f32[192,768]{1,0:T(8,128)}, /*in...) custom-call(bf16[512,384]{1,0:T(8,128)(2,1)} %get-tuple-element.54.h, ...), custom_call_target="tpu_custom_call" | custom-call | tf_op jit(solution)/shard_map/pallas_call | solution.py:1909
